TPU v7x, 32 devices: a whole 2x2x4 slice. The times are simulated.
32 devices in a mesh: dp: 4 (over y, x), tile: 8 (over z, core).
Axes of the slice: x: 2, y: 2, z: 4, core: 2. Of those that a mesh axis runs over, the one named last changes fastest.
Arguments:
- features: bfloat16 [4, 8, 8, 16, 1024], P('dp', 'tile'), may hold values from -6 to 6
- cotangent: bfloat16 [4, 8, 8, 16, 1024], P('dp', 'tile'), may hold values from -6 to 6
- in_weight: bfloat16 [3072, 1024], P(('dp', 'tile')), may hold values from -0.1875 to 0.1875
- out_weight: bfloat16 [3072, 1024], P(('dp', 'tile')), may hold values from -0.109375 to 0.109375
- hidden_bias: bfloat16 [3072], P(('dp', 'tile')), may hold values from -3 to 3
- kernel: float32 [49, 1024], P(None, 'dp'), may hold values from -0.875 to 0.875
- conv_bias: float32 [1024], P('dp'), may hold values from -3 to 3
- norm_gain: float32 [1024], P('dp'), may hold values from 0.5 to 1.5
- norm_bias: float32 [1024], P('dp'), may hold values from -3 to 3
- layer_scale: float32 [1024], P('dp'), may hold values from 0.5 to 1.5
- out_bias: float32 [1024], P('dp'), may hold values from -3 to 3
Outputs:
- block_out: bfloat16 [4, 8, 8, 16, 1024], P('dp', 'tile')
- grad_input: bfloat16 [4, 8, 8, 16, 1024], P('dp', 'tile')
- grad_kernel: float32 [49, 1024], P(None, 'dp')
- grad_conv_bias: float32 [1024], P('dp')
- grad_norm_gain: float32 [1024], P('dp')
- grad_norm_bias: float32 [1024], P('dp')
- grad_layer_scale: float32 [1024], P('dp')
All inputs are finite; a program needn't handle non-finite values.
Results may differ from a plain program's by a relative error of at most 0.0061.
Values may be sent and summed in bfloat16 or wider, within the bound.
No kernel may reach another device: no remote copies, remote signals or barrier semaphores. Data moves between devices by JAX's collectives and lax.ppermute only.
A program may use at most 128 MiB of HBM per device.

v0:
```python
import math

import jax
import jax.numpy as jnp
from jax import lax
from jax.sharding import PartitionSpec as P

KS = 7
GX = 4


def passed_along(block, axis, distance):
    devices = range(lax.axis_size(axis))
    route = [(i - distance, i) for i in devices if i - distance in devices]
    return lax.ppermute(block, axis, route)


def gelu_exact(values):
    return 0.5 * values * (1.0 + jax.scipy.special.erf(values * 0.7071067811865476))


def gelu_slope(values):
    return (
        0.5 * (1.0 + jax.scipy.special.erf(values * 0.7071067811865476))
        + values * jnp.exp(-0.5 * values * values) * 0.3989422804014327
    )


def edge_part(field, step, axis):
    length = field.shape[axis]
    margin = KS // 2
    if step < 0:
        return lax.slice_in_dim(field, length - margin, length, axis=axis)
    if step > 0:
        return lax.slice_in_dim(field, 0, margin, axis=axis)
    return field


def pad_field(field, row_place, col_place, grid_rows):
    bands = []
    for row_step in (-1, 0, 1):
        pieces = []
        for col_step in (-1, 0, 1):
            if row_step == 0 and col_step == 0:
                pieces.append(field)
            else:
                border = edge_part(edge_part(field, row_step, 1), col_step, 2)
                moved = passed_along(border, "tile", -(row_step * GX + col_step))
                row_new = row_place + row_step
                col_new = col_place + col_step
                pieces.append(
                    jnp.where(
                        (row_new >= 0) & (row_new < grid_rows) & (col_new >= 0) & (col_new < GX),
                        moved,
                        jnp.zeros_like(moved),
                    )
                )
        bands.append(jnp.concatenate(pieces, axis=2))
    return jnp.concatenate(bands, axis=1)


def per_device(
    features,
    cotangent,
    in_weight,
    out_weight,
    hidden_bias,
    kernel,
    conv_bias,
    norm_gain,
    norm_bias,
    layer_scale,
    out_bias,
):
    image_count, _, rows, cols, width = features.shape
    tile_count = lax.axis_size("tile")
    grid_rows = tile_count // GX
    place = lax.axis_index("tile")
    row_place = place // GX
    col_place = place % GX
    margin = KS // 2
    kernel_all, cbias, gain, nbias, lscale, obias = (
        lax.all_gather(kernel, "dp", axis=1, tiled=True),
        lax.all_gather(conv_bias, "dp", axis=0, tiled=True),
        lax.all_gather(norm_gain, "dp", axis=0, tiled=True),
        lax.all_gather(norm_bias, "dp", axis=0, tiled=True),
        lax.all_gather(layer_scale, "dp", axis=0, tiled=True),
        lax.all_gather(out_bias, "dp", axis=0, tiled=True),
    )
    picture = features.reshape(image_count, rows, cols, width)
    padded = pad_field(picture, row_place, col_place, grid_rows)
    convolved = jnp.zeros((image_count, rows, cols, width), jnp.float32) + cbias
    for tap_row in range(KS):
        for tap_col in range(KS):
            window = padded[:, tap_row : tap_row + rows, tap_col : tap_col + cols, :].astype(
                jnp.float32
            )
            convolved = convolved + kernel_all[tap_row * KS + tap_col] * window
    average = jnp.mean(convolved, axis=-1, keepdims=True)
    centered = convolved - average
    variance = jnp.mean(centered * centered, axis=-1, keepdims=True)
    inverse = lax.rsqrt(variance + 1e-06)
    pixel_rows = image_count * rows * cols
    standard = (centered * inverse).reshape(pixel_rows, width)
    inverse = inverse.reshape(pixel_rows, 1)
    normed = (standard * gain + nbias).astype(jnp.bfloat16)
    upstream = cotangent.reshape(pixel_rows, width).astype(jnp.float32)
    back_out = (upstream * lscale).astype(jnp.bfloat16)
    rows_in = lax.all_gather(in_weight, ("dp", "tile"), axis=0, tiled=True)
    rows_out = lax.all_gather(out_weight, ("dp", "tile"), axis=0, tiled=True)
    bias_part = lax.all_gather(hidden_bias, ("dp", "tile"), axis=0, tiled=True)
    pre = lax.dot_general(
        normed, rows_in, (((1,), (1,)), ((), ())), preferred_element_type=jnp.float32
    ) + bias_part.astype(jnp.float32)
    hidden = gelu_exact(pre).astype(jnp.bfloat16)
    mlp_sum = jnp.dot(hidden, rows_out, preferred_element_type=jnp.float32)
    back_hidden = lax.dot_general(
        back_out, rows_out, (((1,), (1,)), ((), ())), preferred_element_type=jnp.float32
    )
    back_pre = (back_hidden * gelu_slope(pre)).astype(jnp.bfloat16)
    normed_sum = jnp.dot(back_pre, rows_in, preferred_element_type=jnp.float32)
    mlp_sum, back_normed = (mlp_sum, normed_sum)
    projected = mlp_sum + obias
    source = picture.reshape(pixel_rows, width).astype(jnp.float32)
    block_out = (source + lscale * projected).astype(jnp.bfloat16).reshape(features.shape)
    scale_part = jnp.sum(upstream * projected, axis=0)
    gain_part = jnp.sum(back_normed * standard, axis=0)
    nbias_part = jnp.sum(back_normed, axis=0)
    scaled = back_normed * gain
    back_conv = inverse * (
        scaled
        - jnp.mean(scaled, axis=-1, keepdims=True)
        - standard * jnp.mean(scaled * standard, axis=-1, keepdims=True)
    )
    cbias_part = jnp.sum(back_conv, axis=0)
    back_grid = back_conv.reshape(image_count, rows, cols, width)
    back_padded = pad_field(back_grid.astype(jnp.bfloat16), row_place, col_place, grid_rows)
    grad_grid = upstream.reshape(image_count, rows, cols, width)
    kernel_rows = []
    for tap_row in range(KS):
        for tap_col in range(KS):
            tap_weight = kernel_all[tap_row * KS + tap_col]
            flipped = back_padded[
                :,
                2 * margin - tap_row : 2 * margin - tap_row + rows,
                2 * margin - tap_col : 2 * margin - tap_col + cols,
                :,
            ].astype(jnp.float32)
            grad_grid = grad_grid + tap_weight * flipped
            window = padded[:, tap_row : tap_row + rows, tap_col : tap_col + cols, :].astype(
                jnp.float32
            )
            kernel_rows.append(jnp.sum(back_grid * window, axis=(0, 1, 2)))
    grad_input = grad_grid.astype(jnp.bfloat16).reshape(features.shape)
    kernel_terms = jnp.stack(kernel_rows)
    shared = (
        lax.psum_scatter(kernel_terms, "dp", scatter_dimension=1, tiled=True),
        lax.psum_scatter(cbias_part, "dp", scatter_dimension=0, tiled=True),
        lax.psum_scatter(gain_part, "dp", scatter_dimension=0, tiled=True),
        lax.psum_scatter(nbias_part, "dp", scatter_dimension=0, tiled=True),
        lax.psum_scatter(scale_part, "dp", scatter_dimension=0, tiled=True),
    )
    kernel_sum, cbias_sum, gain_sum, nbias_sum, scale_sum = lax.psum(
        (shared[0], shared[1], shared[2], shared[3], shared[4]), "tile"
    )
    factor = 1.0 / math.sqrt(image_count * lax.axis_size("dp") * rows * cols * tile_count)
    return (
        block_out,
        grad_input,
        kernel_sum * factor,
        cbias_sum * factor,
        gain_sum * factor,
        nbias_sum * factor,
        scale_sum * factor,
    )


def solution(mesh):
    placed = (
        P("dp", "tile", None, None, None),
        P("dp", "tile", None, None, None),
        P(("dp", "tile"), None),
        P(("dp", "tile"), None),
        P(("dp", "tile")),
        P(None, "dp"),
        P("dp"),
        P("dp"),
        P("dp"),
        P("dp"),
        P("dp"),
    )
    return jax.shard_map(
        per_device,
        mesh=mesh,
        in_specs=placed,
        out_specs=(
            P("dp", "tile", None, None, None),
            P("dp", "tile", None, None, None),
            P(None, "dp"),
            P("dp"),
            P("dp"),
            P("dp"),
            P("dp"),
        ),
        check_vma=False,
    )
```

profile of v0, /device:TPU:0, one launch (start us, length us, event | category | flops | bytes accessed | tf_op | source)
XLA Modules:
  0.0 266.5 jit_solution(16052143262830818425)
XLA Ops:
  9.7 5.4 %collective-permute-start = (bf16[1,3,3,1024]{3,2,1,0:T(4,128)(2,1)S(1)}, bf16[1,3,3,1024]{3,2,1,0:T(4,128)(2,1)S(1)}, u32[]{:S(2)}, u32[]{:S(2)}) collective-permute-start(bf16[1,3,3,1024]{3,2,1,0:T(4,128)(2,1)S(1)} %get-tuple-element.100), channel_id=1, source_target_pairs={{0,5},{1,6},{2,7},{8,13},{9,14},{10,15},{16,21},{17,22},{18,23},{2... | collective-permute-start | bytes 55304 | tf_op jit(solution)/shard_map/ppermute | solution.py:15
  17.7 4.3 %collective-permute-start.2 = (bf16[1,3,3,1024]{3,2,1,0:T(4,128)(2,1)S(1)}, bf16[1,3,3,1024]{3,2,1,0:T(4,128)(2,1)S(1)}, u32[]{:S(2)}, u32[]{:S(2)}) collective-permute-start(bf16[1,3,3,1024]{3,2,1,0:T(4,128)(2,1)S(1)} %get-tuple-element.103), channel_id=1, source_target_pairs={{0,3},{1,4},{2,5},{3,6},{4,7},{8,11},{9,12},{10,13},{11,14},{12,15... | collective-permute-start | bytes 55304 | tf_op jit(solution)/shard_map/ppermute | solution.py:15
  23.0 4.5 %collective-permute-start.3 = (bf16[1,8,3,1024]{3,2,1,0:T(4,128)(2,1)S(1)}, bf16[1,8,3,1024]{3,2,1,0:T(4,128)(2,1)S(1)}, u32[]{:S(2)}, u32[]{:S(2)}) collective-permute-start(bf16[1,8,3,1024]{3,2,1,0:T(4,128)(2,1)S(1)} %get-tuple-element.106), channel_id=1, source_target_pairs={{0,1},{1,2},{2,3},{3,4},{4,5},{5,6},{6,7},{8,9},{9,10},{10,11},{11... | collective-permute-start | bytes 147464 | tf_op jit(solution)/shard_map/ppermute | solution.py:15
  27.5 9.1 %all_gather.29 = f32[49,1024]{1,0:T(8,128)S(1)} all-gather(f32[49,256]{1,0:T(8,128)} %param.16), channel_id=1, replica_groups=mesh['dp'=4,'tile'=8] {'dp'}, dimensions={1}, use_global_device_ids=true | all-gather | bytes 250880 | tf_op jit(solution)/shard_map/all_gather | solution.py:83
  38.1 40.3 %all-reduce = bf16[3072]{0:T(1024)(128)(2,1)S(1)} all-reduce(bf16[3072]{0:T(1024)(128)(2,1)S(1)} %dynamic-update-slice), channel_id=1, replica_groups=mesh['dp'=4,'tile'=8] {'dp','tile'}, use_global_device_ids=true, to_apply=%add | all-reduce | flops 3072 | bytes 12288
  79.7 8.8 %all-gather.1 = f32[4,1,256]{2,1,0:T(1,128)S(1)} all-gather(f32[1,1,256]{2,1,0:T(1,128)S(1)} %bitcast.410), channel_id=1, replica_groups=mesh['dp'=4,'tile'=8] {'dp'}, dimensions={0}, use_global_device_ids=true | all-gather | bytes 5120 | tf_op jit(solution)/shard_map/all_gather | solution.py:84
  88.5 8.2 %all-gather.2 = f32[4,1,256]{2,1,0:T(1,128)} all-gather(f32[1,1,256]{2,1,0:T(1,128)S(1)} %bitcast.411), channel_id=1, replica_groups=mesh['dp'=4,'tile'=8] {'dp'}, dimensions={0}, use_global_device_ids=true | all-gather | bytes 5120 | tf_op jit(solution)/shard_map/all_gather | solution.py:85
  96.7 7.4 %all-gather.3 = f32[4,1,256]{2,1,0:T(1,128)S(1)} all-gather(f32[1,1,256]{2,1,0:T(1,128)S(1)} %bitcast.412), channel_id=1, replica_groups=mesh['dp'=4,'tile'=8] {'dp'}, dimensions={0}, use_global_device_ids=true | all-gather | bytes 5120 | tf_op jit(solution)/shard_map/all_gather | solution.py:86
  104.1 8.3 %all-gather = f32[4,1,256]{2,1,0:T(1,128)} all-gather(f32[1,1,256]{2,1,0:T(1,128)S(1)} %bitcast.413), channel_id=1, replica_groups=mesh['dp'=4,'tile'=8] {'dp'}, dimensions={0}, use_global_device_ids=true | all-gather | bytes 5120 | tf_op jit(solution)/shard_map/all_gather | solution.py:87
  112.5 8.0 %all-gather.4 = f32[4,1,256]{2,1,0:T(1,128)} all-gather(f32[1,1,256]{2,1,0:T(1,128)S(1)} %bitcast.414), channel_id=1, replica_groups=mesh['dp'=4,'tile'=8] {'dp'}, dimensions={0}, use_global_device_ids=true | all-gather | bytes 5120 | tf_op jit(solution)/shard_map/all_gather | solution.py:88
  121.8 3.1 %collective-permute-start.1 = (bf16[1,3,16,1024]{3,2,1,0:T(8,128)(2,1)S(1)}, bf16[1,3,16,1024]{3,2,1,0:T(8,128)(2,1)S(1)}, u32[]{:S(2)}, u32[]{:S(2)}) collective-permute-start(bf16[1,3,16,1024]{3,2,1,0:T(8,128)(2,1)S(1)} %get-tuple-element.104), channel_id=1, source_target_pairs={{0,4},{1,5},{2,6},{3,7},{8,12},{9,13},{10,14},{11,15},{16,20},{17,... | collective-permute-start | bytes 294920 | tf_op jit(solution)/shard_map/ppermute | solution.py:15
  127.6 10.9 %collective-permute-done.6 = bf16[1,3,16,1024]{3,2,1,0:T(8,128)(2,1)S(1)} collective-permute-done((bf16[1,3,16,1024]{3,2,1,0:T(8,128)(2,1)S(1)}, bf16[1,3,16,1024]{3,2,1,0:T(8,128)(2,1)S(1)}, u32[]{:S(2)}, u32[]{:S(2)}) %collective-permute-start.6) | collective-permute-done | bytes 98336 | tf_op jit(solution)/shard_map/ppermute | solution.py:15
  139.2 6.7 %fusion.155 = (f32[8,16]{1,0:T(8,128)S(1)}, f32[1,8,16,1024]{3,2,1,0:T(8,128)S(1)}) fusion(bf16[1,11,22,1024]{3,2,1,0:T(8,128)(2,1)S(1)} %get-tuple-element.90, f32[1024]{0:T(1024)S(1)} %bitcast.303, f32[1024]{0:T(1024)S(1)} %bitcast.305, f32[1024]{0:T(1024)S(1)} %bitcast.307, f32[1024]{0:T(1024)S(1)} %bitcast.309, f32[1024]{0:T(1024)S(1)} %bitcast.311, ...), kind=kLoop, calls=%fused_computation.318 | loop fusion | flops 21757824 | bytes 12100096 | tf_op jit(solution)/shard_map/reduce_sum | solution.py:99
  148.3 5.1 %convolution_add_fusion = f32[128,3072]{1,0:T(8,128)S(1)} fusion(bf16[128,1024]{1,0:T(8,128)(2,1)} %fusion.135, bf16[3072,1024]{1,0:T(8,128)(2,1)} %all-gather.8.cloned.1.call-done, f32[3072]{0:T(1024)S(1)} %convert_element_type.473), kind=kOutput, calls=%fused_computation.1 | convolution fusion | flops 805699584 | bytes 8138752 | tf_op jit(solution)/shard_map/dot_general | solution.py:112
  155.0 4.8 %fusion.133 = (f32[1024]{0:T(1024)S(1)}, bf16[128,1024]{1,0:T(8,128)(2,1)}, bf16[128,1024]{1,0:T(8,128)(2,1)}) fusion(bf16[1,1,8,16,1024]{4,3,2,1,0:T(8,128)(2,1)} %param.12, f32[1024]{0:T(1024)} %bitcast.389, bf16[1,1,8,16,1024]{4,3,2,1,0:T(8,128)(2,1)S(1)} %copy-done, f32[1024]{0:T(1024)} %bitcast.390, ...), kind=kOutput, calls=%fused_computation.244 | convolution fusion | flops 808582144 | bytes 8925184 | tf_op jit(solution)/shard_map/dot_general | solution.py:116
  159.8 9.4 %fusion.139 = (f32[1024]{0:T(1024)}, f32[128]{0:T(128)}, f32[128]{0:T(128)}, f32[1024]{0:T(1024)}, f32[128,1024]{1,0:T(8,128)}) fusion(f32[1,8,16,1024]{3,2,1,0:T(8,128)S(1)} %subtract_multiply_fusion, f32[1024]{0:T(1024)} %bitcast.57, bf16[3072,1024]{1,0:T(8,128)(2,1)} %all-gather.8.cloned.1.call-done, bf16[128,1024]{1,0:T(8,128)(2,1)} %get-tuple-element.91, ...), kind=kOutput, calls=%fused_computation.254 | convolution fusion | flops 1615460096 | bytes 15479808 | tf_op jit(solution)/shard_map/dot_general | solution.py:121
  169.8 2.4 fusion.103
  176.0 15.0 %all-reduce.6 = (f32[1024]{0:T(1024)S(1)}, f32[1024]{0:T(1024)S(1)}, f32[1024]{0:T(1024)S(1)}, f32[1024]{0:T(1024)S(1)}) all-reduce(f32[1024]{0:T(1024)S(1)} %get-tuple-element.62, f32[1024]{0:T(1024)S(1)} %copy-done.80, f32[1024]{0:T(1024)S(1)} %copy-done.81, ...), channel_id=3, replica_groups=mesh['dp'=4,'tile'=8] {'dp'}, use_global_device_ids=true, to_apply=%region_56.57.clone | all-reduce | flops 4096 | bytes 32768
  191.7 4.5 %stack.199 = f32[49,1024]{1,0:T(8,128)} concatenate(f32[1,1024]{1,0:T(1,128)S(1)} %bitcast.379, f32[1,1024]{1,0:T(1,128)S(1)} %bitcast.380, f32[1,1024]{1,0:T(1,128)S(1)} %bitcast.381, f32[1,1024]{1,0:T(1,128)S(1)} %bitcast.409, f32[1,1024]{1,0:T(1,128)S(1)} %bitcast.408, f32[1,1024]{1,0:T(1,128)S(1)} %bitcast.407, f32[1,1024]{1,0:T(1,128)S(1)} %bitcast.406, ...), dimensions={0} | concatenate | bytes 401408 | tf_op jit(solution)/shard_map/stack | solution.py:155
  200.3 6.9 %collective-permute-start.8 = (bf16[1,8,3,1024]{3,2,1,0:T(4,128)(2,1)S(1)}, bf16[1,8,3,1024]{3,2,1,0:T(4,128)(2,1)S(1)}, u32[]{:S(2)}, u32[]{:S(2)}) collective-permute-start(bf16[1,8,3,1024]{3,2,1,0:T(4,128)(2,1)S(1)} %get-tuple-element.98), channel_id=1, source_target_pairs={{0,1},{1,2},{2,3},{3,4},{4,5},{5,6},{6,7},{8,9},{9,10},{10,11},{11... | collective-permute-start | bytes 147464 | tf_op jit(solution)/shard_map/ppermute | solution.py:15
  209.9 5.7 %collective-permute-start.14 = (bf16[1,3,16,1024]{3,2,1,0:T(8,128)(2,1)S(1)}, bf16[1,3,16,1024]{3,2,1,0:T(8,128)(2,1)S(1)}, u32[]{:S(2)}, u32[]{:S(2)}) collective-permute-start(bf16[1,3,16,1024]{3,2,1,0:T(8,128)(2,1)S(1)} %get-tuple-element.97), channel_id=1, source_target_pairs={{0,4},{1,5},{2,6},{3,7},{8,12},{9,13},{10,14},{11,15},{16,20},{17,... | collective-permute-start | bytes 294920 | tf_op jit(solution)/shard_map/ppermute | solution.py:15
  216.0 1.7 collective-permute-done.14
  218.4 5.5 %fusion.148 = bf16[1,1,8,16,1024]{4,3,2,1,0:T(8,128)(2,1)} fusion(bf16[1,11,22,1024]{3,2,1,0:T(8,128)(2,1)S(1)} %get-tuple-element.88, f32[1024]{0:T(1024)S(1)} %bitcast.304, f32[1024]{0:T(1024)S(1)} %bitcast.306, f32[1024]{0:T(1024)S(1)} %bitcast.308, f32[1024]{0:T(1024)S(1)} %bitcast.310, f32[1024]{0:T(1024)S(1)} %bitcast.312, f32[1024]{0:T(1024)S(1)} %bitcast.314, ...), kind=kLoop, calls=%fused_computation.287 | loop fusion | flops 21889024 | bytes 12095488 | tf_op jit(solution)/shard_map/reshape | solution.py:154
  224.0 33.1 %all-reduce.5 = (f32[49,256]{1,0:T(8,128)S(1)}, f32[256]{0:T(256)S(1)}, f32[256]{0:T(256)S(1)}, f32[256]{0:T(256)S(1)}, f32[256]{0:T(256)S(1)}) all-reduce(f32[49,256]{1,0:T(8,128)} %reduce-scatter.2.cloned.1.call-done, f32[256]{0:T(256)S(1)} %dynamic-slice.1, f32[256]{0:T(256)S(1)} %dynamic-slice.3, ...), channel_id=1, replica_groups=mesh['dp'=4,'tile'=8] {'tile'}, use_global_device_ids=true, to_apply=%region_54.55 | all-reduce | flops 13568 | bytes 108544 | tf_op jit(solution)/shard_map/psum | solution.py:163
  (264 shorter events, 31.1 us)
Async XLA Ops:
  7.3 141.1 %all-gather.8.cloned.1.call-start = ((), (), s32[]{:S(2)}) async-start(), calls=%async_computation.1 | async-start | bytes 6488064 | tf_op jit(solution)/shard_map/all_gather | solution.py:109
  8.0 147.0 %all-gather.10.cloned.1.call-start = ((), (), s32[]{:S(2)}) async-start(), calls=%async_computation.2 | async-start | bytes 6488064 | tf_op jit(solution)/shard_map/all_gather | solution.py:110
  8.7 215.2 %reduce-scatter.2.cloned.1.call-start = ((), (), s32[]{:S(2)}) async-start(), calls=%async_computation.3 | async-start | bytes 286720 | tf_op jit(solution)/shard_map/reduce_scatter | solution.py:157
  9.7 110.7 %collective-permute-start = (bf16[1,3,3,1024]{3,2,1,0:T(4,128)(2,1)S(1)}, bf16[1,3,3,1024]{3,2,1,0:T(4,128)(2,1)S(1)}, u32[]{:S(2)}, u32[]{:S(2)}) collective-permute-start(bf16[1,3,3,1024]{3,2,1,0:T(4,128)(2,1)S(1)} %get-tuple-element.100), channel_id=1, source_target_pairs={{0,5},{1,6},{2,7},{8,13},{9,14},{10,15},{16,21},{17,22},{18,23},{2... | collective-permute-start | bytes 55304 | tf_op jit(solution)/shard_map/ppermute | solution.py:15
  15.1 106.7 %collective-permute-start.7 = (bf16[1,3,3,1024]{3,2,1,0:T(4,128)(2,1)S(1)}, bf16[1,3,3,1024]{3,2,1,0:T(4,128)(2,1)S(1)}, u32[]{:S(2)}, u32[]{:S(2)}) collective-permute-start(bf16[1,3,3,1024]{3,2,1,0:T(4,128)(2,1)S(1)} %get-tuple-element.101), channel_id=1, source_target_pairs={{5,0},{6,1},{7,2},{13,8},{14,9},{15,10},{21,16},{22,17},{23,18},{2... | collective-permute-start | bytes 55304 | tf_op jit(solution)/shard_map/ppermute | solution.py:15
  16.4 108.5 %collective-permute-start.5 = (bf16[1,3,3,1024]{3,2,1,0:T(4,128)(2,1)S(1)}, bf16[1,3,3,1024]{3,2,1,0:T(4,128)(2,1)S(1)}, u32[]{:S(2)}, u32[]{:S(2)}) collective-permute-start(bf16[1,3,3,1024]{3,2,1,0:T(4,128)(2,1)S(1)} %get-tuple-element.102), channel_id=1, source_target_pairs={{3,0},{4,1},{5,2},{6,3},{7,4},{11,8},{12,9},{13,10},{14,11},{15,12... | collective-permute-start | bytes 55304 | tf_op jit(solution)/shard_map/ppermute | solution.py:15
  17.7 108.5 %collective-permute-start.2 = (bf16[1,3,3,1024]{3,2,1,0:T(4,128)(2,1)S(1)}, bf16[1,3,3,1024]{3,2,1,0:T(4,128)(2,1)S(1)}, u32[]{:S(2)}, u32[]{:S(2)}) collective-permute-start(bf16[1,3,3,1024]{3,2,1,0:T(4,128)(2,1)S(1)} %get-tuple-element.103), channel_id=1, source_target_pairs={{0,3},{1,4},{2,5},{3,6},{4,7},{8,11},{9,12},{10,13},{11,14},{12,15... | collective-permute-start | bytes 55304 | tf_op jit(solution)/shard_map/ppermute | solution.py:15
  23.0 103.3 %collective-permute-start.3 = (bf16[1,8,3,1024]{3,2,1,0:T(4,128)(2,1)S(1)}, bf16[1,8,3,1024]{3,2,1,0:T(4,128)(2,1)S(1)}, u32[]{:S(2)}, u32[]{:S(2)}) collective-permute-start(bf16[1,8,3,1024]{3,2,1,0:T(4,128)(2,1)S(1)} %get-tuple-element.106), channel_id=1, source_target_pairs={{0,1},{1,2},{2,3},{3,4},{4,5},{5,6},{6,7},{8,9},{9,10},{10,11},{11... | collective-permute-start | bytes 147464 | tf_op jit(solution)/shard_map/ppermute | solution.py:15
  37.7 108.2 %copy-start.70 = (f32[1,1024]{1,0:T(1,128)}, f32[1,1024]{1,0:T(1,128)S(1)}, u32[]{:S(2)}) copy-start(f32[1,1024]{1,0:T(1,128)S(1)} %get-tuple-element.150) | copy-start | bytes 12292
  37.7 108.2 %copy-start.72 = (f32[1,1024]{1,0:T(1,128)}, f32[1,1024]{1,0:T(1,128)S(1)}, u32[]{:S(2)}) copy-start(f32[1,1024]{1,0:T(1,128)S(1)} %get-tuple-element.151) | copy-start | bytes 12292
  37.7 108.2 %copy-start.74 = (f32[1,1024]{1,0:T(1,128)}, f32[1,1024]{1,0:T(1,128)S(1)}, u32[]{:S(2)}) copy-start(f32[1,1024]{1,0:T(1,128)S(1)} %get-tuple-element.152) | copy-start | bytes 12292
  37.7 108.2 %copy-start.76 = (f32[1,1024]{1,0:T(1,128)}, f32[1,1024]{1,0:T(1,128)S(1)}, u32[]{:S(2)}) copy-start(f32[1,1024]{1,0:T(1,128)S(1)} %get-tuple-element.153) | copy-start | bytes 12292
  37.8 108.2 %copy-start.78 = (f32[1,1024]{1,0:T(1,128)}, f32[1,1024]{1,0:T(1,128)S(1)}, u32[]{:S(2)}) copy-start(f32[1,1024]{1,0:T(1,128)S(1)} %get-tuple-element.154) | copy-start | bytes 12292
  120.4 5.9 %collective-permute-start.4 = (bf16[1,8,3,1024]{3,2,1,0:T(4,128)(2,1)S(1)}, bf16[1,8,3,1024]{3,2,1,0:T(4,128)(2,1)S(1)}, u32[]{:S(2)}, u32[]{:S(2)}) collective-permute-start(bf16[1,8,3,1024]{3,2,1,0:T(4,128)(2,1)S(1)} %get-tuple-element.107), channel_id=1, source_target_pairs={{1,0},{2,1},{3,2},{4,3},{5,4},{6,5},{7,6},{9,8},{10,9},{11,10},{12... | collective-permute-start | bytes 147464 | tf_op jit(solution)/shard_map/ppermute | solution.py:15
  121.8 5.9 %collective-permute-start.1 = (bf16[1,3,16,1024]{3,2,1,0:T(8,128)(2,1)S(1)}, bf16[1,3,16,1024]{3,2,1,0:T(8,128)(2,1)S(1)}, u32[]{:S(2)}, u32[]{:S(2)}) collective-permute-start(bf16[1,3,16,1024]{3,2,1,0:T(8,128)(2,1)S(1)} %get-tuple-element.104), channel_id=1, source_target_pairs={{0,4},{1,5},{2,6},{3,7},{8,12},{9,13},{10,14},{11,15},{16,20},{17,... | collective-permute-start | bytes 294920 | tf_op jit(solution)/shard_map/ppermute | solution.py:15
  124.9 13.6 %collective-permute-start.6 = (bf16[1,3,16,1024]{3,2,1,0:T(8,128)(2,1)S(1)}, bf16[1,3,16,1024]{3,2,1,0:T(8,128)(2,1)S(1)}, u32[]{:S(2)}, u32[]{:S(2)}) collective-permute-start(bf16[1,3,16,1024]{3,2,1,0:T(8,128)(2,1)S(1)} %get-tuple-element.105), channel_id=1, source_target_pairs={{4,0},{5,1},{6,2},{7,3},{12,8},{13,9},{14,10},{15,11},{20,16},{21,... | collective-permute-start | bytes 294920 | tf_op jit(solution)/shard_map/ppermute | solution.py:15
  174.6 32.6 %collective-permute-start.10 = (bf16[1,3,3,1024]{3,2,1,0:T(4,128)(2,1)S(1)}, bf16[1,3,3,1024]{3,2,1,0:T(4,128)(2,1)S(1)}, u32[]{:S(2)}, u32[]{:S(2)}) collective-permute-start(bf16[1,3,3,1024]{3,2,1,0:T(4,128)(2,1)S(1)} %get-tuple-element.92), channel_id=1, source_target_pairs={{3,0},{4,1},{5,2},{6,3},{7,4},{11,8},{12,9},{13,10},{14,11},{15,12... | collective-permute-start | bytes 55304 | tf_op jit(solution)/shard_map/ppermute | solution.py:15
  196.3 12.3 %collective-permute-start.13 = (bf16[1,3,3,1024]{3,2,1,0:T(4,128)(2,1)S(1)}, bf16[1,3,3,1024]{3,2,1,0:T(4,128)(2,1)S(1)}, u32[]{:S(2)}, u32[]{:S(2)}) collective-permute-start(bf16[1,3,3,1024]{3,2,1,0:T(4,128)(2,1)S(1)} %get-tuple-element.93), channel_id=1, source_target_pairs={{0,5},{1,6},{2,7},{8,13},{9,14},{10,15},{16,21},{17,22},{18,23},{2... | collective-permute-start | bytes 55304 | tf_op jit(solution)/shard_map/ppermute | solution.py:15
  197.7 12.2 %collective-permute-start.15 = (bf16[1,3,3,1024]{3,2,1,0:T(4,128)(2,1)S(1)}, bf16[1,3,3,1024]{3,2,1,0:T(4,128)(2,1)S(1)}, u32[]{:S(2)}, u32[]{:S(2)}) collective-permute-start(bf16[1,3,3,1024]{3,2,1,0:T(4,128)(2,1)S(1)} %get-tuple-element.94), channel_id=1, source_target_pairs={{0,3},{1,4},{2,5},{3,6},{4,7},{8,11},{9,12},{10,13},{11,14},{12,15... | collective-permute-start | bytes 55304 | tf_op jit(solution)/shard_map/ppermute | solution.py:15
  199.0 16.6 %collective-permute-start.12 = (bf16[1,3,3,1024]{3,2,1,0:T(4,128)(2,1)S(1)}, bf16[1,3,3,1024]{3,2,1,0:T(4,128)(2,1)S(1)}, u32[]{:S(2)}, u32[]{:S(2)}) collective-permute-start(bf16[1,3,3,1024]{3,2,1,0:T(4,128)(2,1)S(1)} %get-tuple-element.95), channel_id=1, source_target_pairs={{5,0},{6,1},{7,2},{13,8},{14,9},{15,10},{21,16},{22,17},{23,18},{2... | collective-permute-start | bytes 55304 | tf_op jit(solution)/shard_map/ppermute | solution.py:15
  200.3 15.3 %collective-permute-start.8 = (bf16[1,8,3,1024]{3,2,1,0:T(4,128)(2,1)S(1)}, bf16[1,8,3,1024]{3,2,1,0:T(4,128)(2,1)S(1)}, u32[]{:S(2)}, u32[]{:S(2)}) collective-permute-start(bf16[1,8,3,1024]{3,2,1,0:T(4,128)(2,1)S(1)} %get-tuple-element.98), channel_id=1, source_target_pairs={{0,1},{1,2},{2,3},{3,4},{4,5},{5,6},{6,7},{8,9},{9,10},{10,11},{11... | collective-permute-start | bytes 147464 | tf_op jit(solution)/shard_map/ppermute | solution.py:15
  207.2 8.5 %collective-permute-start.9 = (bf16[1,8,3,1024]{3,2,1,0:T(4,128)(2,1)S(1)}, bf16[1,8,3,1024]{3,2,1,0:T(4,128)(2,1)S(1)}, u32[]{:S(2)}, u32[]{:S(2)}) collective-permute-start(bf16[1,8,3,1024]{3,2,1,0:T(4,128)(2,1)S(1)} %get-tuple-element.99), channel_id=1, source_target_pairs={{1,0},{2,1},{3,2},{4,3},{5,4},{6,5},{7,6},{9,8},{10,9},{11,10},{12... | collective-permute-start | bytes 147464 | tf_op jit(solution)/shard_map/ppermute | solution.py:15
  208.5 7.4 %collective-permute-start.11 = (bf16[1,3,16,1024]{3,2,1,0:T(8,128)(2,1)S(1)}, bf16[1,3,16,1024]{3,2,1,0:T(8,128)(2,1)S(1)}, u32[]{:S(2)}, u32[]{:S(2)}) collective-permute-start(bf16[1,3,16,1024]{3,2,1,0:T(8,128)(2,1)S(1)} %get-tuple-element.96), channel_id=1, source_target_pairs={{4,0},{5,1},{6,2},{7,3},{12,8},{13,9},{14,10},{15,11},{20,16},{21,... | collective-permute-start | bytes 294920 | tf_op jit(solution)/shard_map/ppermute | solution.py:15
  209.9 7.8 %collective-permute-start.14 = (bf16[1,3,16,1024]{3,2,1,0:T(8,128)(2,1)S(1)}, bf16[1,3,16,1024]{3,2,1,0:T(8,128)(2,1)S(1)}, u32[]{:S(2)}, u32[]{:S(2)}) collective-permute-start(bf16[1,3,16,1024]{3,2,1,0:T(8,128)(2,1)S(1)} %get-tuple-element.97), channel_id=1, source_target_pairs={{0,4},{1,5},{2,6},{3,7},{8,12},{9,13},{10,14},{11,15},{16,20},{17,... | collective-permute-start | bytes 294920 | tf_op jit(solution)/shard_map/ppermute | solution.py:15
  (85 other events, 5050.1 us)
Sparse Core Ops, SparseCore 0:
  11.1 72.8 all-gather.7
  87.0 67.9 all-gather.9
  196.4 24.9 reduce-scatter.1
where the time goes:
time: 268 us; the launch traced here: 267 us
  blocking collectives  138 us (51%)
  starting transfers between devices  43 us (16%)
  other arithmetic  23.2 us (9%)
  matrix products  19.3 us (7%)
  waiting for transfers between devices  17.1 us (6%)
  between operations  16.3 us (6%)
  local copies, waits for them, and re-layouts  9.47 us (4%)
    unnamed x2, blocking collectives  55.3 us
    ppermute x16, starting transfers between devices, passed_along(): return lax.ppermute(block, axis, route)  42.8 us
    psum x1, blocking collectives, per_device(): lax.psum((shared[0], shared[1], shared[2], shared[3], shared[4]), 'tile')  33.1 us
    ppermute x16, waiting for transfers between devices, passed_along(): return lax.ppermute(block, axis, route)  14.1 us
    dot_general x1, matrix products, per_device(): normed_sum = jnp.dot(back_pre, rows_in, preferred_element_type=jnp.float32)  9.39 us
    all_gather x1, blocking collectives, per_device(): lax.all_gather(kernel, 'dp', axis=1, tiled=True)  9.12 us
    all_gather x1, blocking collectives, per_device(): lax.all_gather(conv_bias, 'dp', axis=0, tiled=True)  8.83 us
    all_gather x1, blocking collectives, per_device(): lax.all_gather(layer_scale, 'dp', axis=0, tiled=True)  8.31 us
  transfers between devices with their start and end apart: 19, of which 5 were waited for; matrix products, arithmetic and copies ran while one was open for 11% of the time, Pallas kernels for 0%

commit v1 on v0

v1 whole, which is shorter than its diff:
```python
import math

import jax
import jax.numpy as jnp
from jax import lax
from jax.experimental import pallas as pl
from jax.experimental.pallas import tpu as pltpu
from jax.sharding import PartitionSpec as P

KS = 7
GX = 4
MARGIN = KS // 2
LANES = 128
PITCH = 32
INSET = 8
TAP_ROWS = 56
BIAS_ROWS = 8
F32 = jnp.float32
BF16 = jnp.bfloat16

VMEM = pl.BlockSpec(memory_space=pltpu.VMEM)


def call(body, outs, scratch, args, flops=0, size=0, aliases=None, limit=32):
    return pl.pallas_call(
        body,
        out_shape=outs,
        in_specs=[VMEM] * len(args),
        out_specs=[VMEM] * len(outs),
        scratch_shapes=scratch,
        input_output_aliases=aliases or {},
        compiler_params=pltpu.CompilerParams(vmem_limit_bytes=limit * 1024 * 1024),
        cost_estimate=pl.CostEstimate(flops=flops, bytes_accessed=size, transcendentals=0),
    )(*args)


def shape(dims, kind):
    return jax.ShapeDtypeStruct(dims, kind)


def lane_tile(tile):
    return slice(tile * LANES, (tile + 1) * LANES)


def grid_place():
    place = lax.axis_index("tile")
    return place // GX, place % GX


def swap_rows(sends):
    count = lax.axis_size("tile")
    grid_rows = count // GX
    moved = []
    for first, block in enumerate(sends):
        route = []
        for place in range(count):
            row = place // GX
            if row % 2 == first and row + 1 < grid_rows:
                route += [(place, place + GX), (place + GX, place)]
        moved.append(lax.ppermute(block, "tile", route))
    return moved


def swap_cols(sends):
    count = lax.axis_size("tile")
    moved = []
    for first, block in enumerate(sends):
        route = []
        for place in range(count):
            col = place % GX
            if col % 2 == first and col + 1 < GX:
                route += [(place, place + 1), (place + 1, place)]
        moved.append(lax.ppermute(block, "tile", route))
    return moved


def row_pairings():
    return 1 if lax.axis_size("tile") // GX == 2 else 2


def above_below(bands, tile):
    row, _ = grid_place()
    even = row % 2 == 0
    first = bands[0][:, lane_tile(tile)].astype(F32)
    second = bands[1][:, lane_tile(tile)].astype(F32) if len(bands) > 1 else jnp.zeros_like(first)
    return jnp.where(even, second, first), jnp.where(even, first, second)


def border_columns(field, bands, rows, cols):
    width = field.shape[1]
    tall = rows + 2 * MARGIN
    packed = -(-tall * MARGIN // 16) * 16

    def body(field_ref, *refs):
        band_refs = refs[: len(bands)]
        outs, full, left, right = refs[len(bands) : -3], refs[-3], refs[-2], refs[-1]
        _, col = grid_place()
        even = col % 2 == 0
        left[...] = jnp.zeros_like(left)
        right[...] = jnp.zeros_like(right)
        for tile in range(width // LANES):
            above, below = above_below(band_refs, tile)
            full[: MARGIN * cols] = above
            full[MARGIN * cols : (MARGIN + rows) * cols] = field_ref[:, lane_tile(tile)].astype(F32)
            full[(MARGIN + rows) * cols :] = below
            for row in range(tall):
                here = pl.ds(row * MARGIN, MARGIN)
                left[here] = full[pl.ds(row * cols, MARGIN)]
                right[here] = full[pl.ds(row * cols + cols - MARGIN, MARGIN)]
            toward_left, toward_right = left[...], right[...]
            outs[0][:, lane_tile(tile)] = jnp.where(even, toward_right, toward_left).astype(BF16)
            outs[1][:, lane_tile(tile)] = jnp.where(even, toward_left, toward_right).astype(BF16)

    return call(
        body,
        [shape((packed, width), BF16)] * 2,
        [pltpu.VMEM((tall * cols, LANES), F32)] + [pltpu.VMEM((packed, LANES), F32)] * 2,
        [field, *bands],
        flops=200000,
        size=600000,
        limit=8,
    )


def fill_padded(padded, edge, field_ref, band_refs, side_refs, rows, cols):
    width = field_ref.shape[1]
    tall = rows + 2 * MARGIN
    _, col = grid_place()
    even = col % 2 == 0
    for tile in range(width // LANES):
        above, below = above_below(band_refs, tile)
        for row in range(MARGIN):
            source = slice(row * cols, (row + 1) * cols)
            padded[tile, pl.ds(row * PITCH + INSET, cols)] = above[source]
            padded[tile, pl.ds((MARGIN + rows + row) * PITCH + INSET, cols)] = below[source]
        for row in range(rows):
            padded[tile, pl.ds((MARGIN + row) * PITCH + INSET, cols)] = field_ref[
                row * cols : (row + 1) * cols, lane_tile(tile)
            ].astype(F32)
        first = side_refs[0][:, lane_tile(tile)].astype(F32)
        second = side_refs[1][:, lane_tile(tile)].astype(F32)
        edge[0] = jnp.where(even, second, first)
        edge[1] = jnp.where(even, first, second)
        for row in range(tall):
            padded[tile, pl.ds(row * PITCH + INSET - MARGIN, MARGIN)] = edge[0, pl.ds(row * MARGIN, MARGIN)]
            padded[tile, pl.ds(row * PITCH + INSET + cols, MARGIN)] = edge[1, pl.ds(row * MARGIN, MARGIN)]


def window(padded, tile, row, shift, cols):
    return padded[tile, pl.ds(row * PITCH + INSET - MARGIN + shift, cols), :]


def tap_sums(padded, tile, taps, sums, rows, cols, flipped):
    for b in range(KS):
        for r in range(rows + 2 * MARGIN):
            pixels = window(padded, tile, r, b, cols)
            for a in range(KS):
                if 0 <= r - a < rows:
                    index = (KS - 1 - a) * KS + KS - 1 - b if flipped else a * KS + b
                    sums[r - a] = sums[r - a] + taps[index] * pixels
    return sums


def forward(field, bands, sides, params, upstream, rows, cols):
    pixels, width = field.shape
    tiles = width // LANES
    span = (rows + 2 * MARGIN) * PITCH

    def body(*refs):
        field_ref = refs[0]
        band_refs = refs[1 : 1 + len(bands)]
        side_refs = refs[1 + len(bands) : 3 + len(bands)]
        params_ref, up_ref, acts, standard, inverse, padded, edge = refs[3 + len(bands) :]
        fill_padded(padded, edge, field_ref, band_refs, side_refs, rows, cols)

        @pl.loop(0, tiles)
        def _(tile):
            taps = [params_ref[tile, pl.ds(t, 1), :] for t in range(KS * KS)]
            start = jnp.broadcast_to(params_ref[tile, pl.ds(KS * KS, 1), :], (cols, LANES))
            sums = tap_sums(padded, tile, taps, [start] * rows, rows, cols, False)
            for row in range(rows):
                standard[tile, pl.ds(row * cols, cols), :] = sums[row]

        total = standard[0]
        for tile in range(1, tiles):
            total = total + standard[tile]
        average = jnp.sum(total, axis=1, keepdims=True) * (1.0 / width)
        total = jnp.zeros((pixels, LANES), F32)
        for tile in range(tiles):
            centered = standard[tile] - average
            total = total + centered * centered
        scale = lax.rsqrt(jnp.sum(total, axis=1, keepdims=True) * (1.0 / width) + 1e-06)
        inverse[...] = jnp.broadcast_to(scale, (pixels, LANES))
        for tile in range(tiles):
            value = (standard[tile] - average) * scale
            standard[tile] = value
            gain = params_ref[tile, KS * KS + 1 : KS * KS + 2, :]
            shift = params_ref[tile, KS * KS + 2 : KS * KS + 3, :]
            layer = params_ref[tile, KS * KS + 3 : KS * KS + 4, :]
            acts[:pixels, lane_tile(tile)] = (value * gain + shift).astype(BF16)
            acts[pixels:, lane_tile(tile)] = (up_ref[:, lane_tile(tile)].astype(F32) * layer).astype(BF16)

    return call(
        body,
        [
            shape((2 * pixels, width), BF16),
            shape((tiles, pixels, LANES), F32),
            shape((pixels, LANES), F32),
            shape((tiles, span, LANES), F32),
        ],
        [pltpu.VMEM((2, sides[0].shape[0], LANES), F32)],
        [field, *bands, *sides, params, upstream],
        flops=30000000,
        size=4000000,
        limit=16,
    )


def mlp_part(own, peer, in_parts, out_parts, biases, before, last):
    twice, width = own.shape
    pixels = twice // 2
    units = sum(part[2] for part in in_parts)
    arrays = []

    def slot(array):
        for index, known in enumerate(arrays):
            if known is array:
                return index
        arrays.append(array)
        return len(arrays) - 1

    in_slots = [(slot(a), first, count) for a, first, count in in_parts]
    out_slots = [(slot(a), first, count) for a, first, count in out_parts]
    bias_slots = [(slot(a), row, count) for a, row, count in biases]
    step = 32

    def body(*refs):
        own_ref, peer_ref = refs[:2]
        parts = refs[2 : 2 + len(arrays)]
        rest = refs[2 + len(arrays) :]
        if before is not None:
            sums_in, rest = rest[:2], rest[2:]
        outs, (norm, back, win, wout, pre, slope, hid, bpre) = rest[:-8], rest[-8:]
        norm[:pixels] = own_ref[:pixels]
        norm[pixels:] = peer_ref[:pixels]
        back[:pixels] = own_ref[pixels:]
        back[pixels:] = peer_ref[pixels:]
        for target, slots in ((win, in_slots), (wout, out_slots)):
            at = 0
            for index, first, count in slots:
                target[at : at + count] = parts[index][first : first + count]
                at += count
        row = jnp.concatenate(
            [parts[i][r : r + 1, :count].astype(F32) for i, r, count in bias_slots], axis=1
        )
        across = (((1,), (1,)), ((), ()))
        pre[...] = lax.dot_general(norm[...], win[...], across, preferred_element_type=F32) + row
        slope[...] = lax.dot_general(back[...], wout[...], across, preferred_element_type=F32)

        @pl.loop(0, twice // step)
        def _(part):
            here = pl.ds(pl.multiple_of(part * step, step), step)
            value = pre[here, :]
            half = 0.5 * (1.0 + lax.erf(value * 0.7071067811865476))
            hid[here, :] = (value * half).astype(BF16)
            bell = jnp.exp(-0.5 * value * value) * 0.3989422804014327
            bpre[here, :] = (slope[here, :] * (half + value * bell)).astype(BF16)

        projected = jnp.dot(hid[...], wout[...], preferred_element_type=F32)
        if before is not None:
            projected = projected + sums_in[0][...]
        if last:
            outs[0][:pixels] = projected[:pixels]
            outs[1][:pixels] = projected[pixels:].astype(BF16)
        else:
            outs[0][...] = projected
        normed = jnp.dot(bpre[...], win[...], preferred_element_type=F32)
        if before is not None:
            normed = normed + sums_in[1][...]
        if last:
            outs[0][pixels:] = normed[:pixels]
            outs[1][pixels:] = normed[pixels:].astype(BF16)
        else:
            outs[1][...] = normed

    args = [own, peer, *arrays] + (list(before) if before is not None else [])
    return call(
        body,
        [shape((twice, width), F32), shape((twice, width), BF16 if last else F32)],
        [
            pltpu.VMEM((twice, width), BF16),
            pltpu.VMEM((twice, width), BF16),
            pltpu.VMEM((units, width), BF16),
            pltpu.VMEM((units, width), BF16),
            pltpu.VMEM((twice, units), F32),
            pltpu.VMEM((twice, units), F32),
            pltpu.VMEM((twice, units), BF16),
            pltpu.VMEM((twice, units), BF16),
        ],
        args,
        flops=8 * twice * units * width,
        size=4 * units * width + 16 * twice * width,
        limit=24,
    )


def norm_backward(own, peer, standard, inverse, params, field, upstream, rows, cols):
    pixels, width = field.shape
    tiles = width // LANES
    strip = MARGIN * cols

    def body(own_ref, peer_ref, std, inv, params_ref, field_ref, up_ref, conv, wire, block, vectors, *sends):
        zero = jnp.zeros((pixels, LANES), F32)
        plain, mixed = zero, zero
        for tile in range(tiles):
            lanes = lane_tile(tile)
            normed = own_ref[pixels:, lanes] + peer_ref[pixels:, lanes].astype(F32)
            gain = params_ref[tile, KS * KS + 1 : KS * KS + 2, :]
            scaled = normed * gain
            product = normed * std[tile]
            conv[tile] = scaled
            plain = plain + scaled
            mixed = mixed + product * gain
            vectors[tile] = jnp.zeros((8, LANES), F32)
            vectors[tile, 1:2, :] = jnp.sum(product, axis=0, keepdims=True)
            vectors[tile, 2:3, :] = jnp.sum(normed, axis=0, keepdims=True)
        plain = jnp.sum(plain, axis=1, keepdims=True) * (1.0 / width)
        mixed = jnp.sum(mixed, axis=1, keepdims=True) * (1.0 / width)
        for tile in range(tiles):
            value = inv[...] * (conv[tile] - plain - std[tile] * mixed)
            conv[tile] = value
            wire[:, lane_tile(tile)] = value.astype(BF16)
            vectors[tile, 0:1, :] = jnp.sum(value, axis=0, keepdims=True)
        row, _ = grid_place()
        even = row % 2 == 0
        top, bottom = wire[:strip, :], wire[pixels - strip :, :]
        sends[0][...] = jnp.where(even, bottom, top)
        if len(sends) > 1:
            sends[1][...] = jnp.where(even, top, bottom)
        for tile in range(tiles):
            lanes = lane_tile(tile)
            out_bias = params_ref[tile, KS * KS + 4 : KS * KS + 5, :]
            layer = params_ref[tile, KS * KS + 3 : KS * KS + 4, :]
            projected = own_ref[:pixels, lanes] + peer_ref[:pixels, lanes].astype(F32) + out_bias
            block[:, lanes] = (field_ref[:, lanes].astype(F32) + layer * projected).astype(BF16)
            vectors[tile, 3:4, :] = jnp.sum(up_ref[:, lanes].astype(F32) * projected, axis=0, keepdims=True)

    return call(
        body,
        [
            shape((tiles, pixels, LANES), F32),
            shape((pixels, width), BF16),
            shape((pixels, width), BF16),
            shape((tiles, 8, LANES), F32),
        ]
        + [shape((strip, width), BF16)] * row_pairings(),
        [],
        [own, peer, standard, inverse, params, field, upstream],
        flops=3000000,
        size=5000000,
        limit=16,
    )


def kernel_gradient(padded, back_conv, vectors, rows, cols):
    tiles = back_conv.shape[0]

    def body(padded_ref, conv, vectors_ref, out):
        @pl.loop(0, tiles)
        def _(tile):
            grads = [conv[tile, pl.ds(row * cols, cols), :] for row in range(rows)]
            for b in range(KS):
                sums = [None] * KS
                for r in range(rows + 2 * MARGIN):
                    pixels = window(padded_ref, tile, r, b, cols)
                    for a in range(KS):
                        if 0 <= r - a < rows:
                            term = pixels * grads[r - a]
                            sums[a] = term if sums[a] is None else sums[a] + term
                for a in range(KS):
                    out[tile, pl.ds(a * KS + b, 1), :] = jnp.sum(sums[a], axis=0, keepdims=True)
            out[tile, pl.ds(KS * KS, TAP_ROWS - KS * KS), :] = vectors_ref[tile, : TAP_ROWS - KS * KS, :]

    return call(
        body,
        [shape((tiles, TAP_ROWS, LANES), F32)],
        [],
        [padded, back_conv, vectors],
        flops=15000000,
        size=3000000,
        limit=8,
    )[0]


def input_gradient(wire, bands, sides, params, upstream, rows, cols):
    pixels, width = wire.shape
    tiles = width // LANES
    span = (rows + 2 * MARGIN) * PITCH

    def body(*refs):
        wire_ref = refs[0]
        band_refs = refs[1 : 1 + len(bands)]
        side_refs = refs[1 + len(bands) : 3 + len(bands)]
        params_ref, up_ref, out, padded, edge = refs[3 + len(bands) :]
        fill_padded(padded, edge, wire_ref, band_refs, side_refs, rows, cols)

        @pl.loop(0, tiles)
        def _(tile):
            lanes = pl.ds(pl.multiple_of(tile * LANES, LANES), LANES)
            taps = [params_ref[tile, pl.ds(t, 1), :] for t in range(KS * KS)]
            start = [up_ref[pl.ds(row * cols, cols), lanes].astype(F32) for row in range(rows)]
            sums = tap_sums(padded, tile, taps, start, rows, cols, True)
            for row in range(rows):
                out[pl.ds(row * cols, cols), lanes] = sums[row].astype(BF16)

    return call(
        body,
        [shape((pixels, width), BF16)],
        [pltpu.VMEM((tiles, span, LANES), F32), pltpu.VMEM((2, sides[0].shape[0], LANES), F32)],
        [wire, *bands, *sides, params, upstream],
        flops=15000000,
        size=1500000,
        limit=16,
    )[0]


def across(block, bits):
    groups = lax.axis_size("dp")
    return lax.ppermute(block, "dp", [(i, i ^ bits) for i in range(groups)])


def ring(block):
    count = lax.axis_size("tile")
    chips = count // 2
    return lax.ppermute(
        block, "tile", [(i, (i // 2 + 1) % chips * 2 + i % 2) for i in range(count)]
    )


def tile_swap(block, bits):
    return lax.ppermute(block, "tile", [(i, i ^ bits) for i in range(lax.axis_size("tile"))])


def gather_params(pack):
    groups = lax.axis_size("dp")
    rows, own = pack.shape
    if own % LANES or groups & (groups - 1):
        whole = lax.all_gather(pack, "dp", axis=1, tiled=True)
        return whole.reshape(rows, -1, LANES).transpose(1, 0, 2)
    here = pack.reshape(rows, own // LANES, LANES).transpose(1, 0, 2)
    me = lax.axis_index("dp")
    pieces = jnp.stack([here] + [across(here, bits) for bits in range(1, groups)])
    return jnp.concatenate(
        [lax.dynamic_index_in_dim(pieces, me ^ source, 0, keepdims=False) for source in range(groups)]
    )


def sum_params(parts, own):
    groups = lax.axis_size("dp")
    tiles, rows, _ = parts.shape
    if own % LANES or groups & (groups - 1):
        flat = parts.transpose(1, 0, 2).reshape(rows, -1)
        return lax.psum(lax.psum_scatter(flat, "dp", scatter_dimension=1, tiled=True), "tile")
    me = lax.axis_index("dp")
    count = own // LANES
    total = lax.dynamic_slice_in_dim(parts, me * count, count, 0)
    moved = [
        across(lax.dynamic_slice_in_dim(parts, (me ^ bits) * count, count, 0), bits)
        for bits in range(1, groups)
    ]
    for block in moved:
        total = total + block
    bits = 1
    while bits < lax.axis_size("tile"):
        total = total + tile_swap(total, bits)
        bits *= 2
    return total.transpose(1, 0, 2).reshape(rows, own)


def weight_shares(in_weight, out_weight, hidden_bias):
    units, width = in_weight.shape
    groups, count = lax.axis_size("dp"), lax.axis_size("tile")
    if units % 16 or groups != 4 or units > width:
        core = lax.axis_index("tile") % 2

        def mine(array):
            whole = lax.all_gather(array, ("dp", "tile"), axis=0, tiled=True)
            whole = whole.reshape((groups * count // 2, 2, units) + array.shape[1:])
            return lax.dynamic_index_in_dim(whole, core, 1, keepdims=False).reshape(
                (-1,) + array.shape[1:]
            )

        rows_in, rows_out, bias = mine(in_weight), mine(out_weight), mine(hidden_bias)
        part = rows_in.shape[0] // 4
        shares = []
        for at in range(0, 4 * part, part):
            shares.append(
                (
                    [(rows_in[at : at + part], 0, part)],
                    [(rows_out[at : at + part], 0, part)],
                    [(bias[at : at + part].reshape(1, part), 0, part)],
                )
            )
        return shares
    row = jnp.pad(hidden_bias.reshape(1, units), ((0, BIAS_ROWS - 1), (0, width - units)))
    held = jnp.concatenate([in_weight, out_weight, row])
    shares = []
    for step in range(count // 2):
        onward = ring(held) if step + 1 < count // 2 else None
        first, second = across(held, 1), across(held, 2)
        far_in = across(first[:units], 2)
        far_out = across(second[units:], 1)
        shares.append(
            (
                [(held, 0, units), (first, 0, units), (second, 0, units), (far_in, 0, units)],
                [(held, units, units), (first, units, units), (second, units, units), (far_out, 0, units)],
                [(held, 2 * units, units), (first, 2 * units, units), (second, 2 * units, units), (far_out, units, units)],
            )
        )
        held = onward
    return shares


def per_device(
    features,
    cotangent,
    in_weight,
    out_weight,
    hidden_bias,
    kernel,
    conv_bias,
    norm_gain,
    norm_bias,
    layer_scale,
    out_bias,
):
    image_count, _, rows, cols, width = features.shape
    groups, count = lax.axis_size("dp"), lax.axis_size("tile")
    pixels = rows * cols
    own = kernel.shape[1]
    strip = MARGIN * cols
    shares = weight_shares(in_weight, out_weight, hidden_bias)

    vectors = [v.reshape(1, own) for v in (conv_bias, norm_gain, norm_bias, layer_scale, out_bias)]
    pack = jnp.concatenate([kernel, *vectors, jnp.zeros((TAP_ROWS - KS * KS - 5, own), F32)])
    params = gather_params(pack)

    field = features.reshape(pixels, width)
    upstream = cotangent.reshape(pixels, width)
    row, _ = grid_place()
    sends = [
        lax.dynamic_slice_in_dim(field, (1 - (row + first) % 2) * (pixels - strip), strip, 0)
        for first in range(row_pairings())
    ]
    bands = swap_rows(sends)
    sides = swap_cols(border_columns(field, bands, rows, cols))
    acts, standard, inverse, padded = forward(field, bands, sides, params, upstream, rows, cols)
    peer_acts = tile_swap(acts, 1)

    sums = None
    for index, share in enumerate(shares):
        sums = mlp_part(acts, peer_acts, *share, sums, index + 1 == len(shares))
    mine, theirs = sums
    back_conv, wire, block, vector_parts, *back_sends = norm_backward(
        mine, tile_swap(theirs, 1), standard, inverse, params, field, upstream, rows, cols
    )
    back_bands = swap_rows(back_sends)
    parts = kernel_gradient(padded, back_conv, vector_parts, rows, cols)
    back_sides = swap_cols(border_columns(wire, back_bands, rows, cols))
    grad = input_gradient(wire, back_bands, back_sides, params, upstream, rows, cols)
    factor = 1.0 / math.sqrt(image_count * groups * count * pixels)
    sums = sum_params(parts, own) * factor
    taps = KS * KS
    return (
        block.reshape(features.shape),
        grad.reshape(features.shape),
        sums[:taps],
        sums[taps],
        sums[taps + 1],
        sums[taps + 2],
        sums[taps + 3],
    )


def solution(mesh):
    placed = (
        P("dp", "tile", None, None, None),
        P("dp", "tile", None, None, None),
        P(("dp", "tile"), None),
        P(("dp", "tile"), None),
        P(("dp", "tile")),
        P(None, "dp"),
        P("dp"),
        P("dp"),
        P("dp"),
        P("dp"),
        P("dp"),
    )
    return jax.shard_map(
        per_device,
        mesh=mesh,
        in_specs=placed,
        out_specs=(
            P("dp", "tile", None, None, None),
            P("dp", "tile", None, None, None),
            P(None, "dp"),
            P("dp"),
            P("dp"),
            P("dp"),
            P("dp"),
        ),
        check_vma=False,
    )
```

time: 268 us -> 124 us (0.46)
  the two profiles are of different devices: /device:TPU:0 before, /device:TPU:1 now
where the time goes in v1:
time: 124 us; the launch traced here: 123 us
  waiting for transfers between devices  52.5 us (42%)
  starting transfers between devices  37.8 us (30%)
  Pallas kernels  20.8 us (17%)
  local copies, waits for them, and re-layouts  9.88 us (8%)
    ppermute x22, waiting for transfers between devices, across(): return lax.ppermute(block, 'dp', [(i, i ^ bits) for i in range(groups)])  25.7 us
    pallas_call x10, Pallas kernels, call(): pl.pallas_call(body, out_shape=outs, in_specs=[VMEM] * len(args), out_spe...  20.8 us
    ppermute x22, starting transfers between devices, across(): return lax.ppermute(block, 'dp', [(i, i ^ bits) for i in range(groups)])  20.4 us
    ppermute x2, waiting for transfers between devices, swap_rows(): moved.append(lax.ppermute(block, 'tile', route))  11.6 us
    ppermute x3, waiting for transfers between devices, ring(): lax.ppermute(block, 'tile', [(i, (i // 2 + 1) % chips * 2 + i % 2) for i...  8.88 us
    unnamed x42, local copies, waits for them, and re-layouts  6.57 us
    ppermute x5, starting transfers between devices, tile_swap(): lax.ppermute(block, 'tile', [(i, i ^ bits) for i in range(lax.axis_size('...  6.46 us
    ppermute x4, starting transfers between devices, swap_cols(): moved.append(lax.ppermute(block, 'tile', route))  6.44 us
  transfers between devices with their start and end apart: 36, of which 15 were waited for; matrix products, arithmetic and copies ran while one was open for 2% of the time, Pallas kernels for 11%

profile of v1, /device:TPU:1, one launch (start us, length us, event | category | flops | bytes accessed | tf_op | source)
XLA Modules:
  0.0 123.3 jit_solution(16605954398230551532)
XLA Ops:
  1.8 2.2 %collective-permute-start.7 = (bf16[200,1024]{1,0:T(8,128)(2,1)S(1)}, bf16[200,1024]{1,0:T(8,128)(2,1)}, u32[]{:S(2)}, u32[]{:S(2)}) collective-permute-start(bf16[200,1024]{1,0:T(8,128)(2,1)S(1)} %fusion.1.refs_2_), channel_id=1, source_target_pairs={{0,2},{1,3},{2,4},{3,5},{4,6},{5,7},{6,0},{7,1},{8,10},{9,11},{10,... | collective-permute-start | bytes 1228808 | tf_op jit(solution)/shard_map/ppermute | solution.py:435
  6.4 8.9 %collective-permute-done.7.refs_2_ = bf16[200,1024]{1,0:T(8,128)(2,1)} collective-permute-done((bf16[200,1024]{1,0:T(8,128)(2,1)S(1)}, bf16[200,1024]{1,0:T(8,128)(2,1)}, u32[]{:S(2)}, u32[]{:S(2)}) %collective-permute-start.7) | collective-permute-done | bytes 409632 | tf_op jit(solution)/shard_map/ppermute | solution.py:435
  19.3 2.2 %collective-permute-start.5 = (f32[2,56,128]{2,1,0:T(8,128)S(1)}, f32[2,56,128]{2,1,0:T(8,128)S(1)}, u32[]{:S(2)}, u32[]{:S(2)}) collective-permute-start(f32[2,56,128]{2,1,0:T(8,128)S(1)} %bitcast.43), channel_id=1, source_target_pairs={{0,24},{8,16},{16,8},{24,0},{1,25},{9,17},{17,9},{25,1},{2,26},{10... | collective-permute-start | bytes 172040 | tf_op jit(solution)/shard_map/ppermute | solution.py:429
  21.5 11.0 %collective-permute-done.refs_0_.refs_1_ = bf16[48,1024]{1,0:T(8,128)(2,1)S(1)} collective-permute-done((bf16[48,1024]{1,0:T(8,128)(2,1)S(1)}, bf16[48,1024]{1,0:T(8,128)(2,1)S(1)}, u32[]{:S(2)}, u32[]{:S(2)}) %collective-permute-start) | collective-permute-done | bytes 98336 | tf_op jit(solution)/shard_map/ppermute | solution.py:60
  35.7 2.0 %collective-permute-start.2 = (bf16[48,1024]{1,0:T(8,128)(2,1)S(1)}, bf16[48,1024]{1,0:T(8,128)(2,1)S(1)}, u32[]{:S(2)}, u32[]{:S(2)}) collective-permute-start(bf16[48,1024]{1,0:T(8,128)(2,1)S(1)} %get-tuple-element.29), channel_id=1, source_target_pairs={{1,2},{2,1},{5,6},{6,5},{9,10},{10,9},{13,14},{14,13},{17,18},{18,... | collective-permute-start | bytes 294920 | tf_op jit(solution)/shard_map/ppermute | solution.py:73
  39.2 1.5 %collective-permute-done.4 = f32[2,56,128]{2,1,0:T(8,128)S(1)} collective-permute-done((f32[2,56,128]{2,1,0:T(8,128)S(1)}, f32[2,56,128]{2,1,0:T(8,128)S(1)}, u32[]{:S(2)}, u32[]{:S(2)}) %collective-permute-start.4) | collective-permute-done | bytes 57376 | tf_op jit(solution)/shard_map/ppermute | solution.py:429
  43.5 10.6 %collective-permute-done.24.refs_5_ = bf16[96,1024]{1,0:T(8,128)(2,1)S(1)} collective-permute-done((bf16[96,1024]{1,0:T(8,128)(2,1)S(1)}, bf16[96,1024]{1,0:T(8,128)(2,1)S(1)}, u32[]{:S(2)}, u32[]{:S(2)}) %collective-permute-start.24) | collective-permute-done | bytes 196640 | tf_op jit(solution)/shard_map/ppermute | solution.py:429
  58.8 3.0 %shard_map.163 = (bf16[256,1024]{1,0:T(8,128)(2,1)S(1)}, f32[8,128,128]{2,1,0:T(8,128)S(1)}, f32[128,128]{1,0:T(8,128)S(1)}, f32[8,448,128]{2,1,0:T(8,128)S(1)}) custom-call(bf16[128,1024]{1,0:T(8,128)(2,1)S(1)} %bitcast.36, bf16[48,1024]{1,0:T(8,128)(2,1)S(1)} %copy-done.8, bf16[48,1024]{1,0:T(8,128)(2,1)S(1)} %copy-done.12, ...), custom_call_target="tpu_custom_call" | custom-call | flops 30000000 | bytes 4000000 | tf_op jit(solution)/shard_map/pallas_call | solution.py:25
  61.8 1.8 %collective-permute-start.6 = (bf16[256,1024]{1,0:T(8,128)(2,1)S(1)}, bf16[256,1024]{1,0:T(8,128)(2,1)S(1)}, u32[]{:S(2)}, u32[]{:S(2)}) collective-permute-start(bf16[256,1024]{1,0:T(8,128)(2,1)S(1)} %get-tuple-element.30.refs_0_), channel_id=1, source_target_pairs={{0,1},{1,0},{2,3},{3,2},{4,5},{5,4},{6,7},{7,6},{8,9},{9,8},{10,11... | collective-permute-start | bytes 1572872 | tf_op jit(solution)/shard_map/ppermute | solution.py:441
  66.8 7.9 %collective-permute-done.11.refs_4_ = bf16[200,1024]{1,0:T(8,128)(2,1)S(1)} collective-permute-done((bf16[200,1024]{1,0:T(8,128)(2,1)S(1)}, bf16[200,1024]{1,0:T(8,128)(2,1)S(1)}, u32[]{:S(2)}, u32[]{:S(2)}) %collective-permute-start.11) | collective-permute-done | bytes 409632 | tf_op jit(solution)/shard_map/ppermute | solution.py:429
  77.0 1.9 %collective-permute-done.20.refs_5_ = bf16[96,1024]{1,0:T(8,128)(2,1)S(1)} collective-permute-done((bf16[96,1024]{1,0:T(8,128)(2,1)S(1)}, bf16[96,1024]{1,0:T(8,128)(2,1)S(1)}, u32[]{:S(2)}, u32[]{:S(2)}) %collective-permute-start.20) | collective-permute-done | bytes 196640 | tf_op jit(solution)/shard_map/ppermute | solution.py:429
  79.5 1.7 %shard_map.164 = (f32[256,1024]{1,0:T(8,128)S(1)}, f32[256,1024]{1,0:T(8,128)S(1)}) custom-call(bf16[256,1024]{1,0:T(8,128)(2,1)S(1)} %get-tuple-element.30.refs_0_, bf16[256,1024]{1,0:T(8,128)(2,1)S(1)} %collective-permute-done.6.refs_1_, bf16[200,1024]{1,0:T(8,128)(2,1)S(1)} %copy-done.6, bf16[200,1024]{1,0:T(8,128)(2,1)S(1)} %copy-done.16, ...), custom_call_target="tpu_custom_call" | custom-call | flops 805306368 | bytes 5767168 | tf_op jit(solution)/shard_map/pallas_call | solution.py:25
  81.3 2.7 %shard_map.165 = (f32[256,1024]{1,0:T(8,128)S(1)}, f32[256,1024]{1,0:T(8,128)S(1)}) custom-call(bf16[256,1024]{1,0:T(8,128)(2,1)S(1)} %get-tuple-element.30.refs_0_, bf16[256,1024]{1,0:T(8,128)(2,1)S(1)} %collective-permute-done.6.refs_1_, bf16[200,1024]{1,0:T(8,128)(2,1)} %collective-permute-done.7.refs_2_, ...), custom_call_target="tpu_custom_call" | custom-call | flops 805306368 | bytes 5767168 | tf_op jit(solution)/shard_map/pallas_call | solution.py:25
  84.1 2.7 %shard_map.166 = (f32[256,1024]{1,0:T(8,128)S(1)}, f32[256,1024]{1,0:T(8,128)S(1)}) custom-call(bf16[256,1024]{1,0:T(8,128)(2,1)S(1)} %get-tuple-element.30.refs_0_, bf16[256,1024]{1,0:T(8,128)(2,1)S(1)} %collective-permute-done.6.refs_1_, bf16[200,1024]{1,0:T(8,128)(2,1)} %collective-permute-done.8.refs_2_, ...), custom_call_target="tpu_custom_call" | custom-call | flops 805306368 | bytes 5767168 | tf_op jit(solution)/shard_map/pallas_call | solution.py:25
  87.1 1.6 %collective-permute-done.13.refs_6_ = bf16[104,1024]{1,0:T(8,128)(2,1)S(1)} collective-permute-done((bf16[104,1024]{1,0:T(8,128)(2,1)S(1)}, bf16[104,1024]{1,0:T(8,128)(2,1)S(1)}, u32[]{:S(2)}, u32[]{:S(2)}) %collective-permute-start.13) | collective-permute-done | bytes 213024 | tf_op jit(solution)/shard_map/ppermute | solution.py:429
  88.7 2.5 %shard_map.167 = (f32[256,1024]{1,0:T(8,128)S(1)}, bf16[256,1024]{1,0:T(8,128)(2,1)}) custom-call(bf16[256,1024]{1,0:T(8,128)(2,1)S(1)} %get-tuple-element.30.refs_0_, bf16[256,1024]{1,0:T(8,128)(2,1)S(1)} %collective-permute-done.6.refs_1_, bf16[200,1024]{1,0:T(8,128)(2,1)S(1)} %collective-permute-done.9.refs_2_, ...), custom_call_target="tpu_custom_call" | custom-call | flops 805306368 | bytes 5767168 | tf_op jit(solution)/shard_map/pallas_call | solution.py:25
  93.3 1.9 %collective-permute-done.26.peer_ref = bf16[256,1024]{1,0:T(8,128)(2,1)} collective-permute-done((bf16[256,1024]{1,0:T(8,128)(2,1)}, bf16[256,1024]{1,0:T(8,128)(2,1)}, u32[]{:S(2)}, u32[]{:S(2)}) %collective-permute-start.26) | collective-permute-done | bytes 524320 | tf_op jit(solution)/shard_map/ppermute | solution.py:441
  96.4 2.4 %shard_map.168 = (f32[8,128,128]{2,1,0:T(8,128)S(1)}, bf16[128,1024]{1,0:T(8,128)(2,1)S(1)}, bf16[128,1024]{1,0:T(8,128)(2,1)}, f32[8,8,128]{2,1,0:T(8,128)S(1)}, bf16[48,1024]{1,0:T(8,128)(2,1)S(1)}) custom-call(f32[256,1024]{1,0:T(8,128)S(1)} %copy-done.4, bf16[256,1024]{1,0:T(8,128)(2,1)} %collective-permute-done.26.peer_ref, ...), custom_call_target="tpu_custom_call" | custom-call | flops 3000000 | bytes 5000000 | tf_op jit(solution)/shard_map/pallas_call | solution.py:25
  98.8 2.0 %shard_map.171 = f32[8,56,128]{2,1,0:T(8,128)S(1)} custom-call(f32[8,448,128]{2,1,0:T(8,128)S(1)} %get-tuple-element.46.padded_ref, f32[8,128,128]{2,1,0:T(8,128)S(1)} %get-tuple-element.47.conv, f32[8,8,128]{2,1,0:T(8,128)S(1)} %get-tuple-element.48.vectors_ref), custom_call_target="tpu_custom_call" | custom-call | flops 15000000 | bytes 3000000 | tf_op jit(solution)/shard_map/pallas_call | solution.py:25
  106.3 2.0 %collective-permute-start.33 = (f32[2,56,128]{2,1,0:T(8,128)S(1)}, f32[2,56,128]{2,1,0:T(8,128)S(1)}, u32[]{:S(2)}, u32[]{:S(2)}) collective-permute-start(f32[2,56,128]{2,1,0:T(8,128)S(1)} %add_add_fusion), channel_id=1, source_target_pairs={{0,1},{1,0},{2,3},{3,2},{4,5},{5,4},{6,7},{7,6},{8,9},{9,8},{10,11... | collective-permute-start | bytes 172040 | tf_op jit(solution)/shard_map/ppermute | solution.py:441
  111.3 2.2 %collective-permute-start.29 = (bf16[48,1024]{1,0:T(8,128)(2,1)S(1)}, bf16[48,1024]{1,0:T(8,128)(2,1)S(1)}, u32[]{:S(2)}, u32[]{:S(2)}) collective-permute-start(bf16[48,1024]{1,0:T(8,128)(2,1)S(1)} %get-tuple-element.45), channel_id=1, source_target_pairs={{1,2},{2,1},{5,6},{6,5},{9,10},{10,9},{13,14},{14,13},{17,18},{18,... | collective-permute-start | bytes 294920 | tf_op jit(solution)/shard_map/ppermute | solution.py:73
  113.6 1.4 %collective-permute-start.35 = (f32[2,56,128]{2,1,0:T(8,128)S(1)}, f32[2,56,128]{2,1,0:T(8,128)S(1)}, u32[]{:S(2)}, u32[]{:S(2)}) collective-permute-start(f32[2,56,128]{2,1,0:T(8,128)S(1)} %add.67), channel_id=1, source_target_pairs={{0,4},{1,5},{2,6},{3,7},{4,0},{5,1},{6,2},{7,3},{8,12},{9,13},{10,... | collective-permute-start | bytes 172040 | tf_op jit(solution)/shard_map/ppermute | solution.py:441
  115.0 3.6 %collective-permute-done.29.refs_3_ = bf16[48,1024]{1,0:T(8,128)(2,1)S(1)} collective-permute-done((bf16[48,1024]{1,0:T(8,128)(2,1)S(1)}, bf16[48,1024]{1,0:T(8,128)(2,1)S(1)}, u32[]{:S(2)}, u32[]{:S(2)}) %collective-permute-start.29) | collective-permute-done | bytes 98336 | tf_op jit(solution)/shard_map/ppermute | solution.py:73
  118.6 3.4 %shard_map.170 = bf16[128,1024]{1,0:T(8,128)(2,1)} custom-call(bf16[128,1024]{1,0:T(8,128)(2,1)S(1)} %get-tuple-element.42.field_ref.refs_0_, bf16[48,1024]{1,0:T(8,128)(2,1)S(1)} %collective-permute-done.27.refs_0_.refs_1_, bf16[48,1024]{1,0:T(8,128)(2,1)S(1)} %collective-permute-done.28.refs_2_, bf16[48,1024]{1,0:T(8,128)(2,1)S(1)} %collective-permute-done.29.refs_3_, ...), custom_call_target="tpu_custom_call" | custom-call | flops 15000000 | bytes 1500000 | tf_op jit(solution)/shard_map/pallas_call | solution.py:25
  (124 shorter events, 39.1 us)
Async XLA Ops:
  1.8 13.5 %collective-permute-start.7 = (bf16[200,1024]{1,0:T(8,128)(2,1)S(1)}, bf16[200,1024]{1,0:T(8,128)(2,1)}, u32[]{:S(2)}, u32[]{:S(2)}) collective-permute-start(bf16[200,1024]{1,0:T(8,128)(2,1)S(1)} %fusion.1.refs_2_), channel_id=1, source_target_pairs={{0,2},{1,3},{2,4},{3,5},{4,6},{5,7},{6,0},{7,1},{8,10},{9,11},{10,... | collective-permute-start | bytes 1228808 | tf_op jit(solution)/shard_map/ppermute | solution.py:435
  4.0 33.7 %collective-permute-start.23 = (bf16[200,1024]{1,0:T(8,128)(2,1)S(1)}, bf16[200,1024]{1,0:T(8,128)(2,1)S(1)}, u32[]{:S(2)}, u32[]{:S(2)}) collective-permute-start(bf16[200,1024]{1,0:T(8,128)(2,1)S(1)} %fusion.1.refs_2_), channel_id=1, source_target_pairs={{0,16},{8,24},{16,0},{24,8},{1,17},{9,25},{17,1},{25,9},{2,18},{10... | collective-permute-start | bytes 1228808 | tf_op jit(solution)/shard_map/ppermute | solution.py:429
  5.2 33.7 %collective-permute-start.22 = (bf16[200,1024]{1,0:T(8,128)(2,1)S(1)}, bf16[200,1024]{1,0:T(8,128)(2,1)S(1)}, u32[]{:S(2)}, u32[]{:S(2)}) collective-permute-start(bf16[200,1024]{1,0:T(8,128)(2,1)S(1)} %fusion.1.refs_2_), channel_id=1, source_target_pairs={{0,8},{8,0},{16,24},{24,16},{1,9},{9,1},{17,25},{25,17},{2,10},{10... | collective-permute-start | bytes 1228808 | tf_op jit(solution)/shard_map/ppermute | solution.py:429
  15.3 28.1 %collective-permute-start.8 = (bf16[200,1024]{1,0:T(8,128)(2,1)}, bf16[200,1024]{1,0:T(8,128)(2,1)}, u32[]{:S(2)}, u32[]{:S(2)}) collective-permute-start(bf16[200,1024]{1,0:T(8,128)(2,1)} %collective-permute-done.7.refs_2_), channel_id=1, source_target_pairs={{0,2},{1,3},{2,4},{3,5},{4,6},{5,7},{6,0},{7,1},{8,10},{9,11},{10,... | collective-permute-start | bytes 1228808 | tf_op jit(solution)/shard_map/ppermute | solution.py:435
  16.2 16.3 %collective-permute-start = (bf16[48,1024]{1,0:T(8,128)(2,1)S(1)}, bf16[48,1024]{1,0:T(8,128)(2,1)S(1)}, u32[]{:S(2)}, u32[]{:S(2)}) collective-permute-start(bf16[48,1024]{1,0:T(8,128)(2,1)S(1)} %constant_dynamic-slice_fusion.3), channel_id=1, source_target_pairs={{0,4},{4,0},{1,5},{5,1},{2,6},{6,2},{3,7},{7,3},{8,12},{12,8},{9,1... | collective-permute-start | bytes 294920 | tf_op jit(solution)/shard_map/ppermute | solution.py:60
  19.3 15.3 %collective-permute-start.5 = (f32[2,56,128]{2,1,0:T(8,128)S(1)}, f32[2,56,128]{2,1,0:T(8,128)S(1)}, u32[]{:S(2)}, u32[]{:S(2)}) collective-permute-start(f32[2,56,128]{2,1,0:T(8,128)S(1)} %bitcast.43), channel_id=1, source_target_pairs={{0,24},{8,16},{16,8},{24,0},{1,25},{9,17},{17,9},{25,1},{2,26},{10... | collective-permute-start | bytes 172040 | tf_op jit(solution)/shard_map/ppermute | solution.py:429
  35.7 7.3 %collective-permute-start.2 = (bf16[48,1024]{1,0:T(8,128)(2,1)S(1)}, bf16[48,1024]{1,0:T(8,128)(2,1)S(1)}, u32[]{:S(2)}, u32[]{:S(2)}) collective-permute-start(bf16[48,1024]{1,0:T(8,128)(2,1)S(1)} %get-tuple-element.29), channel_id=1, source_target_pairs={{1,2},{2,1},{5,6},{6,5},{9,10},{10,9},{13,14},{14,13},{17,18},{18,... | collective-permute-start | bytes 294920 | tf_op jit(solution)/shard_map/ppermute | solution.py:73
  38.9 22.9 %collective-permute-start.19 = (bf16[200,1024]{1,0:T(8,128)(2,1)}, bf16[200,1024]{1,0:T(8,128)(2,1)S(1)}, u32[]{:S(2)}, u32[]{:S(2)}) collective-permute-start(bf16[200,1024]{1,0:T(8,128)(2,1)} %collective-permute-done.7.refs_2_), channel_id=1, source_target_pairs={{0,16},{8,24},{16,0},{24,8},{1,17},{9,25},{17,1},{25,9},{2,18},{10... | collective-permute-start | bytes 1228808 | tf_op jit(solution)/shard_map/ppermute | solution.py:429
  40.8 14.5 %collective-permute-start.25 = (bf16[104,1024]{1,0:T(8,128)(2,1)S(1)}, bf16[104,1024]{1,0:T(8,128)(2,1)S(1)}, u32[]{:S(2)}, u32[]{:S(2)}) collective-permute-start(bf16[104,1024]{1,0:T(8,128)(2,1)S(1)} %slice.67), channel_id=1, source_target_pairs={{0,8},{8,0},{16,24},{24,16},{1,9},{9,1},{17,25},{25,17},{2,10},{10... | collective-permute-start | bytes 638984 | tf_op jit(solution)/shard_map/ppermute | solution.py:429
  41.7 12.3 %collective-permute-start.24 = (bf16[96,1024]{1,0:T(8,128)(2,1)S(1)}, bf16[96,1024]{1,0:T(8,128)(2,1)S(1)}, u32[]{:S(2)}, u32[]{:S(2)}) collective-permute-start(bf16[96,1024]{1,0:T(8,128)(2,1)S(1)} %slice.66), channel_id=1, source_target_pairs={{0,16},{8,24},{16,0},{24,8},{1,17},{9,25},{17,1},{25,9},{2,18},{10... | collective-permute-start | bytes 589832 | tf_op jit(solution)/shard_map/ppermute | solution.py:429
  43.0 21.2 %collective-permute-start.18 = (bf16[200,1024]{1,0:T(8,128)(2,1)}, bf16[200,1024]{1,0:T(8,128)(2,1)S(1)}, u32[]{:S(2)}, u32[]{:S(2)}) collective-permute-start(bf16[200,1024]{1,0:T(8,128)(2,1)} %collective-permute-done.7.refs_2_), channel_id=1, source_target_pairs={{0,8},{8,0},{16,24},{24,16},{1,9},{9,1},{17,25},{25,17},{2,10},{10... | collective-permute-start | bytes 1228808 | tf_op jit(solution)/shard_map/ppermute | solution.py:429
  43.4 20.2 %collective-permute-start.9 = (bf16[200,1024]{1,0:T(8,128)(2,1)}, bf16[200,1024]{1,0:T(8,128)(2,1)S(1)}, u32[]{:S(2)}, u32[]{:S(2)}) collective-permute-start(bf16[200,1024]{1,0:T(8,128)(2,1)} %collective-permute-done.8.refs_2_), channel_id=1, source_target_pairs={{0,2},{1,3},{2,4},{3,5},{4,6},{5,7},{6,0},{7,1},{8,10},{9,11},{10,... | collective-permute-start | bytes 1228808 | tf_op jit(solution)/shard_map/ppermute | solution.py:435
  54.0 10.6 %collective-permute-start.15 = (bf16[200,1024]{1,0:T(8,128)(2,1)}, bf16[200,1024]{1,0:T(8,128)(2,1)S(1)}, u32[]{:S(2)}, u32[]{:S(2)}) collective-permute-start(bf16[200,1024]{1,0:T(8,128)(2,1)} %collective-permute-done.8.refs_2_), channel_id=1, source_target_pairs={{0,16},{8,24},{16,0},{24,8},{1,17},{9,25},{17,1},{25,9},{2,18},{10... | collective-permute-start | bytes 1228808 | tf_op jit(solution)/shard_map/ppermute | solution.py:429
  55.2 10.5 %collective-permute-start.14 = (bf16[200,1024]{1,0:T(8,128)(2,1)}, bf16[200,1024]{1,0:T(8,128)(2,1)S(1)}, u32[]{:S(2)}, u32[]{:S(2)}) collective-permute-start(bf16[200,1024]{1,0:T(8,128)(2,1)} %collective-permute-done.8.refs_2_), channel_id=1, source_target_pairs={{0,8},{8,0},{16,24},{24,16},{1,9},{9,1},{17,25},{25,17},{2,10},{10... | collective-permute-start | bytes 1228808 | tf_op jit(solution)/shard_map/ppermute | solution.py:429
  61.8 14.5 %collective-permute-start.6 = (bf16[256,1024]{1,0:T(8,128)(2,1)S(1)}, bf16[256,1024]{1,0:T(8,128)(2,1)S(1)}, u32[]{:S(2)}, u32[]{:S(2)}) collective-permute-start(bf16[256,1024]{1,0:T(8,128)(2,1)S(1)} %get-tuple-element.30.refs_0_), channel_id=1, source_target_pairs={{0,1},{1,0},{2,3},{3,2},{4,5},{5,4},{6,7},{7,6},{8,9},{9,8},{10,11... | collective-permute-start | bytes 1572872 | tf_op jit(solution)/shard_map/ppermute | solution.py:441
  63.7 11.0 %collective-permute-start.11 = (bf16[200,1024]{1,0:T(8,128)(2,1)S(1)}, bf16[200,1024]{1,0:T(8,128)(2,1)S(1)}, u32[]{:S(2)}, u32[]{:S(2)}) collective-permute-start(bf16[200,1024]{1,0:T(8,128)(2,1)S(1)} %collective-permute-done.9.refs_2_), channel_id=1, source_target_pairs={{0,16},{8,24},{16,0},{24,8},{1,17},{9,25},{17,1},{25,9},{2,18},{10... | collective-permute-start | bytes 1228808 | tf_op jit(solution)/shard_map/ppermute | solution.py:429
  64.1 11.0 %collective-permute-start.10 = (bf16[200,1024]{1,0:T(8,128)(2,1)S(1)}, bf16[200,1024]{1,0:T(8,128)(2,1)S(1)}, u32[]{:S(2)}, u32[]{:S(2)}) collective-permute-start(bf16[200,1024]{1,0:T(8,128)(2,1)S(1)} %collective-permute-done.9.refs_2_), channel_id=1, source_target_pairs={{0,8},{8,0},{16,24},{24,16},{1,9},{9,1},{17,25},{25,17},{2,10},{10... | collective-permute-start | bytes 1228808 | tf_op jit(solution)/shard_map/ppermute | solution.py:429
  64.7 14.2 %collective-permute-start.20 = (bf16[96,1024]{1,0:T(8,128)(2,1)S(1)}, bf16[96,1024]{1,0:T(8,128)(2,1)S(1)}, u32[]{:S(2)}, u32[]{:S(2)}) collective-permute-start(bf16[96,1024]{1,0:T(8,128)(2,1)S(1)} %slice.64), channel_id=1, source_target_pairs={{0,16},{8,24},{16,0},{24,8},{1,17},{9,25},{17,1},{25,9},{2,18},{10... | collective-permute-start | bytes 589832 | tf_op jit(solution)/shard_map/ppermute | solution.py:429
  65.7 15.6 %collective-permute-start.21 = (bf16[104,1024]{1,0:T(8,128)(2,1)S(1)}, bf16[104,1024]{1,0:T(8,128)(2,1)S(1)}, u32[]{:S(2)}, u32[]{:S(2)}) collective-permute-start(bf16[104,1024]{1,0:T(8,128)(2,1)S(1)} %slice.65), channel_id=1, source_target_pairs={{0,8},{8,0},{16,24},{24,16},{1,9},{9,1},{17,25},{25,17},{2,10},{10... | collective-permute-start | bytes 638984 | tf_op jit(solution)/shard_map/ppermute | solution.py:429
  74.7 9.4 %collective-permute-start.17 = (bf16[104,1024]{1,0:T(8,128)(2,1)S(1)}, bf16[104,1024]{1,0:T(8,128)(2,1)S(1)}, u32[]{:S(2)}, u32[]{:S(2)}) collective-permute-start(bf16[104,1024]{1,0:T(8,128)(2,1)S(1)} %slice.63), channel_id=1, source_target_pairs={{0,8},{8,0},{16,24},{24,16},{1,9},{9,1},{17,25},{25,17},{2,10},{10... | collective-permute-start | bytes 638984 | tf_op jit(solution)/shard_map/ppermute | solution.py:429
  75.2 8.9 %collective-permute-start.16 = (bf16[96,1024]{1,0:T(8,128)(2,1)S(1)}, bf16[96,1024]{1,0:T(8,128)(2,1)S(1)}, u32[]{:S(2)}, u32[]{:S(2)}) collective-permute-start(bf16[96,1024]{1,0:T(8,128)(2,1)S(1)} %slice.62), channel_id=1, source_target_pairs={{0,16},{8,24},{16,0},{24,8},{1,17},{9,25},{17,1},{25,9},{2,18},{10... | collective-permute-start | bytes 589832 | tf_op jit(solution)/shard_map/ppermute | solution.py:429
  76.3 12.3 %collective-permute-start.13 = (bf16[104,1024]{1,0:T(8,128)(2,1)S(1)}, bf16[104,1024]{1,0:T(8,128)(2,1)S(1)}, u32[]{:S(2)}, u32[]{:S(2)}) collective-permute-start(bf16[104,1024]{1,0:T(8,128)(2,1)S(1)} %slice.61), channel_id=1, source_target_pairs={{0,8},{8,0},{16,24},{24,16},{1,9},{9,1},{17,25},{25,17},{2,10},{10... | collective-permute-start | bytes 638984 | tf_op jit(solution)/shard_map/ppermute | solution.py:429
  78.9 8.2 %collective-permute-start.12 = (bf16[96,1024]{1,0:T(8,128)(2,1)S(1)}, bf16[96,1024]{1,0:T(8,128)(2,1)S(1)}, u32[]{:S(2)}, u32[]{:S(2)}) collective-permute-start(bf16[96,1024]{1,0:T(8,128)(2,1)S(1)} %slice.60), channel_id=1, source_target_pairs={{0,16},{8,24},{16,0},{24,8},{1,17},{9,25},{17,1},{25,9},{2,18},{10... | collective-permute-start | bytes 589832 | tf_op jit(solution)/shard_map/ppermute | solution.py:429
  113.6 8.5 %collective-permute-start.35 = (f32[2,56,128]{2,1,0:T(8,128)S(1)}, f32[2,56,128]{2,1,0:T(8,128)S(1)}, u32[]{:S(2)}, u32[]{:S(2)}) collective-permute-start(f32[2,56,128]{2,1,0:T(8,128)S(1)} %add.67), channel_id=1, source_target_pairs={{0,4},{1,5},{2,6},{3,7},{4,0},{5,1},{6,2},{7,3},{8,12},{9,13},{10,... | collective-permute-start | bytes 172040 | tf_op jit(solution)/shard_map/ppermute | solution.py:441
  (32 other events, 400.9 us)

commit v2 on v1

v2 whole, which is shorter than its diff:
```python
import math

import jax
import jax.numpy as jnp
from jax import lax
from jax.experimental import pallas as pl
from jax.experimental.pallas import tpu as pltpu
from jax.sharding import PartitionSpec as P

KS = 7
GX = 4
MARGIN = KS // 2
LANES = 128
PITCH = 32
INSET = 8
TAP_ROWS = 56
BIAS_ROWS = 8
PARAM_ROWS = 32
F32 = jnp.float32
BF16 = jnp.bfloat16

VMEM = pl.BlockSpec(memory_space=pltpu.VMEM)


def call(body, outs, scratch, args, flops=0, size=0, aliases=None, limit=32):
    return pl.pallas_call(
        body,
        out_shape=outs,
        in_specs=[VMEM] * len(args),
        out_specs=[VMEM] * len(outs),
        scratch_shapes=scratch,
        input_output_aliases=aliases or {},
        compiler_params=pltpu.CompilerParams(vmem_limit_bytes=limit * 1024 * 1024),
        cost_estimate=pl.CostEstimate(flops=flops, bytes_accessed=size, transcendentals=0),
    )(*args)


def shape(dims, kind):
    return jax.ShapeDtypeStruct(dims, kind)


def lane_tile(tile):
    return slice(tile * LANES, (tile + 1) * LANES)


def grid_place():
    place = lax.axis_index("tile")
    return place // GX, place % GX


def swap_rows(sends):
    count = lax.axis_size("tile")
    grid_rows = count // GX
    moved = []
    for first, block in enumerate(sends):
        route = []
        for place in range(count):
            row = place // GX
            if row % 2 == first and row + 1 < grid_rows:
                route += [(place, place + GX), (place + GX, place)]
        moved.append(lax.ppermute(block, "tile", route))
    return moved


def swap_cols(sends):
    count = lax.axis_size("tile")
    moved = []
    for first, block in enumerate(sends):
        route = []
        for place in range(count):
            col = place % GX
            if col % 2 == first and col + 1 < GX:
                route += [(place, place + 1), (place + 1, place)]
        moved.append(lax.ppermute(block, "tile", route))
    return moved


def row_pairings():
    return 1 if lax.axis_size("tile") // GX == 2 else 2


def above_below(bands, tile):
    row, _ = grid_place()
    even = row % 2 == 0
    first = bands[0][:, lane_tile(tile)].astype(F32)
    second = bands[1][:, lane_tile(tile)].astype(F32) if len(bands) > 1 else jnp.zeros_like(first)
    return jnp.where(even, second, first), jnp.where(even, first, second)


def border_columns(field, bands, rows, cols):
    width = field.shape[1]
    tall = rows + 2 * MARGIN
    packed = -(-tall * MARGIN // 16) * 16

    def body(field_ref, *refs):
        band_refs = refs[: len(bands)]
        outs, full, left, right = refs[len(bands) : -3], refs[-3], refs[-2], refs[-1]
        _, col = grid_place()
        even = col % 2 == 0
        left[...] = jnp.zeros_like(left)
        right[...] = jnp.zeros_like(right)
        for tile in range(width // LANES):
            above, below = above_below(band_refs, tile)
            full[: MARGIN * cols] = above
            full[MARGIN * cols : (MARGIN + rows) * cols] = field_ref[:, lane_tile(tile)].astype(F32)
            full[(MARGIN + rows) * cols :] = below
            for row in range(tall):
                here = pl.ds(row * MARGIN, MARGIN)
                left[here] = full[pl.ds(row * cols, MARGIN)]
                right[here] = full[pl.ds(row * cols + cols - MARGIN, MARGIN)]
            toward_left, toward_right = left[...], right[...]
            outs[0][:, lane_tile(tile)] = jnp.where(even, toward_right, toward_left).astype(BF16)
            outs[1][:, lane_tile(tile)] = jnp.where(even, toward_left, toward_right).astype(BF16)

    return call(
        body,
        [shape((packed, width), BF16)] * 2,
        [pltpu.VMEM((tall * cols, LANES), F32)] + [pltpu.VMEM((packed, LANES), F32)] * 2,
        [field, *bands],
        size=1107000,
        limit=8,
    )


def fill_padded(padded, edge, field_ref, band_refs, side_refs, rows, cols):
    width = field_ref.shape[1]
    tall = rows + 2 * MARGIN
    _, col = grid_place()
    even = col % 2 == 0
    for tile in range(width // LANES):
        above, below = above_below(band_refs, tile)
        for row in range(MARGIN):
            source = slice(row * cols, (row + 1) * cols)
            padded[tile, pl.ds(row * PITCH + INSET, cols)] = above[source]
            padded[tile, pl.ds((MARGIN + rows + row) * PITCH + INSET, cols)] = below[source]
        for row in range(rows):
            padded[tile, pl.ds((MARGIN + row) * PITCH + INSET, cols)] = field_ref[
                row * cols : (row + 1) * cols, lane_tile(tile)
            ].astype(F32)
        first = side_refs[0][:, lane_tile(tile)].astype(F32)
        second = side_refs[1][:, lane_tile(tile)].astype(F32)
        edge[0] = jnp.where(even, second, first)
        edge[1] = jnp.where(even, first, second)
        for row in range(tall):
            padded[tile, pl.ds(row * PITCH + INSET - MARGIN, MARGIN)] = edge[0, pl.ds(row * MARGIN, MARGIN)]
            padded[tile, pl.ds(row * PITCH + INSET + cols, MARGIN)] = edge[1, pl.ds(row * MARGIN, MARGIN)]


def window(padded, tile, row, shift, cols):
    return padded[tile, pl.ds(row * PITCH + INSET - MARGIN + shift, cols), :]


def tap_sums(padded, tile, taps, sums, rows, cols, flipped):
    for b in range(KS):
        for r in range(rows + 2 * MARGIN):
            pixels = window(padded, tile, r, b, cols)
            for a in range(KS):
                if 0 <= r - a < rows:
                    index = (KS - 1 - a) * KS + KS - 1 - b if flipped else a * KS + b
                    sums[r - a] = sums[r - a] + taps[index] * pixels
    return sums


def forward(field, bands, sides, params, rows, cols):
    pixels, width = field.shape
    tiles = width // LANES
    span = (rows + 2 * MARGIN) * PITCH

    def body(*refs):
        field_ref = refs[0]
        band_refs = refs[1 : 1 + len(bands)]
        side_refs = refs[1 + len(bands) : 3 + len(bands)]
        params_ref, acts, standard, inverse, padded, edge = refs[3 + len(bands) :]
        fill_padded(padded, edge, field_ref, band_refs, side_refs, rows, cols)

        @pl.loop(0, tiles)
        def _(tile):
            taps = [params_ref[tile, pl.ds(t, 1), :] for t in range(KS * KS)]
            start = jnp.broadcast_to(params_ref[tile, pl.ds(KS * KS, 1), :], (cols, LANES))
            sums = tap_sums(padded, tile, taps, [start] * rows, rows, cols, False)
            for row in range(rows):
                standard[tile, pl.ds(row * cols, cols), :] = sums[row]

        total = standard[0]
        for tile in range(1, tiles):
            total = total + standard[tile]
        average = jnp.sum(total, axis=1, keepdims=True) * (1.0 / width)
        total = jnp.zeros((pixels, LANES), F32)
        for tile in range(tiles):
            centered = standard[tile] - average
            total = total + centered * centered
        scale = lax.rsqrt(jnp.sum(total, axis=1, keepdims=True) * (1.0 / width) + 1e-06)
        inverse[...] = jnp.broadcast_to(scale, (pixels, LANES))
        for tile in range(tiles):
            value = (standard[tile] - average) * scale
            standard[tile] = value
            gain = params_ref[tile, KS * KS + 1 : KS * KS + 2, :]
            shift = params_ref[tile, KS * KS + 2 : KS * KS + 3, :]
            acts[:, lane_tile(tile)] = (value * gain + shift).astype(BF16)

    return call(
        body,
        [
            shape((pixels, width), BF16),
            shape((tiles, pixels, LANES), F32),
            shape((pixels, LANES), F32),
            shape((tiles, span, LANES), F32),
        ],
        [pltpu.VMEM((2, sides[0].shape[0], LANES), F32)],
        [field, *bands, *sides, params],
        size=10701000,
        limit=16,
    )


def hidden_values(normed, upstream, params, shards, units):
    pixels, width = normed[0].shape
    members, count = len(normed), len(shards)
    total, kept = members * pixels, members * pixels // 2
    tiles = width // LANES
    every = count * units
    step = 32

    def body(*refs):
        normed_refs, up_refs, params_ref = refs[:members], refs[members : 2 * members], refs[2 * members]
        shard_refs, rest = refs[2 * members + 1 : 2 * members + 1 + count], refs[2 * members + 1 + count :]
        hid, stay, send, norm, back, win, wout, pre, slope, bpre = rest
        for index in range(members):
            here = slice(index * pixels, (index + 1) * pixels)
            norm[here] = normed_refs[index][...]
            for tile in range(tiles):
                lanes = lane_tile(tile)
                layer = params_ref[tile, KS * KS + 3 : KS * KS + 4, :]
                back[here, lanes] = (up_refs[index][:, lanes].astype(F32) * layer).astype(BF16)
        for index, shard in enumerate(shard_refs):
            here = slice(index * units, (index + 1) * units)
            win[here] = shard[:units]
            wout[here] = shard[units : 2 * units]
        row = jnp.concatenate(
            [shard[2 * units : 2 * units + 1, :units].astype(F32) for shard in shard_refs], axis=1
        )
        across = (((1,), (1,)), ((), ()))
        pre[...] = lax.dot_general(norm[...], win[...], across, preferred_element_type=F32) + row
        slope[...] = lax.dot_general(back[...], wout[...], across, preferred_element_type=F32)

        @pl.loop(0, total // step)
        def _(part):
            here = pl.ds(pl.multiple_of(part * step, step), step)
            value = pre[here, :]
            half = 0.5 * (1.0 + lax.erf(value * 0.7071067811865476))
            hid[here, :] = (value * half).astype(BF16)
            bell = jnp.exp(-0.5 * value * value) * 0.3989422804014327
            bpre[here, :] = (slope[here, :] * (half + value * bell)).astype(BF16)

        back_normed = jnp.dot(bpre[...], win[...], preferred_element_type=F32)
        stay[...] = back_normed[:kept]
        send[...] = back_normed[kept:].astype(BF16)

    return call(
        body,
        [shape((total, every), BF16), shape((kept, width), F32), shape((kept, width), BF16)],
        [
            pltpu.VMEM((total, width), BF16),
            pltpu.VMEM((total, width), BF16),
            pltpu.VMEM((every, width), BF16),
            pltpu.VMEM((every, width), BF16),
            pltpu.VMEM((total, every), F32),
            pltpu.VMEM((total, every), F32),
            pltpu.VMEM((total, every), BF16),
        ],
        [*normed, *upstream, params, *shards],
        size=13653000,
        limit=28,
    )


def project(hidden, upstream, shards, units):
    pixels, width = upstream[0].shape
    members, count = len(upstream), len(shards)
    total, kept = members * pixels, members * pixels // 2
    tiles = width // LANES

    def body(*refs):
        hidden_ref, up_refs, shard_refs = refs[0], refs[1 : 1 + members], refs[1 + members : 1 + members + count]
        stay, send, scale, wout = refs[1 + members + count :]
        for index, shard in enumerate(shard_refs):
            wout[index * units : (index + 1) * units] = shard[units : 2 * units]
        projected = jnp.dot(hidden_ref[...], wout[...], preferred_element_type=F32)
        stay[...] = projected[:kept]
        send[...] = projected[kept:].astype(BF16)
        for tile in range(tiles):
            lanes = lane_tile(tile)
            sums = jnp.zeros((pixels, LANES), F32)
            for index in range(members):
                rows = projected[index * pixels : (index + 1) * pixels, lanes]
                sums = sums + up_refs[index][:, lanes].astype(F32) * rows
            scale[tile] = jnp.broadcast_to(jnp.sum(sums, axis=0, keepdims=True), (8, LANES))

    return call(
        body,
        [shape((kept, width), F32), shape((kept, width), BF16), shape((tiles, 8, LANES), F32)],
        [pltpu.VMEM((count * units, width), BF16)],
        [hidden, *upstream, *shards],
        size=3911400,
        limit=20,
    )


def pair_sum(mine, peer):
    rows, width = mine.shape
    half = rows // 2

    def body(mine_ref, peer_ref, out):
        out[...] = (mine_ref[half:, :] + peer_ref[half:, :].astype(F32)).astype(BF16)

    return call(body, [shape((half, width), BF16)], [], [mine, peer], size=738000, limit=4)[0]


def norm_backward(own, peer, far, standard, inverse, params, upstream, rows, cols):
    pixels, width = upstream.shape
    tiles = width // LANES
    strip = MARGIN * cols

    def body(own_ref, peer_ref, far_ref, std, inv, params_ref, up_ref, conv, wire, vectors, *sends):
        zero = jnp.zeros((pixels, LANES), F32)
        plain, mixed = zero, zero
        for tile in range(tiles):
            lanes = lane_tile(tile)
            normed = own_ref[:pixels, lanes] + peer_ref[:pixels, lanes].astype(F32) + far_ref[:, lanes].astype(F32)
            gain = params_ref[tile, KS * KS + 1 : KS * KS + 2, :]
            scaled = normed * gain
            product = normed * std[tile]
            conv[tile] = scaled
            plain = plain + scaled
            mixed = mixed + product * gain
            vectors[tile] = jnp.zeros((8, LANES), F32)
            vectors[tile, 1:2, :] = jnp.sum(product, axis=0, keepdims=True)
            vectors[tile, 2:3, :] = jnp.sum(normed, axis=0, keepdims=True)
            out_bias = params_ref[tile, KS * KS + 4 : KS * KS + 5, :]
            vectors[tile, 3:4, :] = jnp.sum(up_ref[:, lanes].astype(F32), axis=0, keepdims=True) * out_bias
        plain = jnp.sum(plain, axis=1, keepdims=True) * (1.0 / width)
        mixed = jnp.sum(mixed, axis=1, keepdims=True) * (1.0 / width)
        for tile in range(tiles):
            value = inv[...] * (conv[tile] - plain - std[tile] * mixed)
            conv[tile] = value
            wire[:, lane_tile(tile)] = value.astype(BF16)
            vectors[tile, 0:1, :] = jnp.sum(value, axis=0, keepdims=True)
        row, _ = grid_place()
        even = row % 2 == 0
        top, bottom = wire[:strip, :], wire[pixels - strip :, :]
        sends[0][...] = jnp.where(even, bottom, top)
        if len(sends) > 1:
            sends[1][...] = jnp.where(even, top, bottom)

    return call(
        body,
        [
            shape((tiles, pixels, LANES), F32),
            shape((pixels, width), BF16),
            shape((tiles, 8, LANES), F32),
        ]
        + [shape((strip, width), BF16)] * row_pairings(),
        [],
        [own, peer, far, standard, inverse, params, upstream],
        size=1845000,
        limit=16,
    )


def block_output(own, peer, far, params, field):
    pixels, width = field.shape

    def body(own_ref, peer_ref, far_ref, params_ref, field_ref, block):
        for tile in range(width // LANES):
            lanes = lane_tile(tile)
            out_bias = params_ref[tile, KS * KS + 4 : KS * KS + 5, :]
            layer = params_ref[tile, KS * KS + 3 : KS * KS + 4, :]
            projected = own_ref[:pixels, lanes] + peer_ref[:pixels, lanes].astype(F32) + far_ref[:, lanes].astype(F32)
            block[:, lanes] = (field_ref[:, lanes].astype(F32) + layer * (projected + out_bias)).astype(BF16)

    return call(
        body,
        [shape((pixels, width), BF16)],
        [],
        [own, peer, far, params, field],
        size=3210300,
        limit=8,
    )[0]


def kernel_gradient(padded, back_conv, vectors, scale_part, rows, cols, groups):
    tiles = back_conv.shape[0]
    share = tiles // groups

    def body(padded_ref, conv, vectors_ref, scale_ref, *refs):
        outs, out = refs[:-1], refs[-1]

        @pl.loop(0, tiles)
        def _(tile):
            grads = [conv[tile, pl.ds(row * cols, cols), :] for row in range(rows)]
            for b in range(KS):
                sums = [None] * KS
                for r in range(rows + 2 * MARGIN):
                    pixels = window(padded_ref, tile, r, b, cols)
                    for a in range(KS):
                        if 0 <= r - a < rows:
                            term = pixels * grads[r - a]
                            sums[a] = term if sums[a] is None else sums[a] + term
                for a in range(KS):
                    out[tile, pl.ds(a * KS + b, 1), :] = jnp.sum(sums[a], axis=0, keepdims=True)
            out[tile, pl.ds(KS * KS, TAP_ROWS - KS * KS), :] = vectors_ref[tile, : TAP_ROWS - KS * KS, :]
            out[tile, pl.ds(KS * KS + 3, 1), :] += scale_ref[tile, :1, :]

        if groups == 1:
            outs[0][...] = out[...]
        else:
            me = lax.axis_index("dp")
            for bits in range(groups):
                for part in range(share):
                    outs[bits][part] = out[(me ^ bits) * share + part]

    return call(
        body,
        [shape((share, TAP_ROWS, LANES), F32)] * groups,
        [pltpu.VMEM((tiles, TAP_ROWS, LANES), F32)],
        [padded, back_conv, vectors, scale_part],
        size=7380000,
        limit=8,
    )


def input_gradient(wire, bands, sides, params, upstream, rows, cols):
    pixels, width = wire.shape
    tiles = width // LANES
    span = (rows + 2 * MARGIN) * PITCH

    def body(*refs):
        wire_ref = refs[0]
        band_refs = refs[1 : 1 + len(bands)]
        side_refs = refs[1 + len(bands) : 3 + len(bands)]
        params_ref, up_ref, out, padded, edge = refs[3 + len(bands) :]
        fill_padded(padded, edge, wire_ref, band_refs, side_refs, rows, cols)

        @pl.loop(0, tiles)
        def _(tile):
            lanes = pl.ds(pl.multiple_of(tile * LANES, LANES), LANES)
            taps = [params_ref[tile, pl.ds(t, 1), :] for t in range(KS * KS)]
            start = [up_ref[pl.ds(row * cols, cols), lanes].astype(F32) for row in range(rows)]
            sums = tap_sums(padded, tile, taps, start, rows, cols, True)
            for row in range(rows):
                out[pl.ds(row * cols, cols), lanes] = sums[row].astype(BF16)

    return call(
        body,
        [shape((pixels, width), BF16)],
        [pltpu.VMEM((tiles, span, LANES), F32), pltpu.VMEM((2, sides[0].shape[0], LANES), F32)],
        [wire, *bands, *sides, params, upstream],
        size=12177000,
        limit=16,
    )[0]


def across(block, bits):
    groups = lax.axis_size("dp")
    return lax.ppermute(block, "dp", [(i, i ^ bits) for i in range(groups)])


def tile_swap(block, bits):
    return lax.ppermute(block, "tile", [(i, i ^ bits) for i in range(lax.axis_size("tile"))])


def place_params(own, joints, last):
    share, rows, _ = own.shape
    half = rows // 2

    def body(own_ref, one_ref, two_ref, last_ref, out):
        me = lax.axis_index("dp")
        for part in range(share):
            out[me * share + part] = own_ref[part]
            out[(me ^ 3) * share + part] = last_ref[part]
        for bits, ref in ((1, one_ref), (2, two_ref)):
            start = ref.shape[0] - PARAM_ROWS
            for part in range(2 * share):
                high = ref[start:, lane_tile(2 * part)].astype(F32)
                value = high + ref[start:, lane_tile(2 * part + 1)].astype(F32)
                out[(me ^ bits) * share + part // 2, pl.ds(part % 2 * half, half), :] = value[:half]

    return call(
        body,
        [shape((4 * share, rows, LANES), F32)],
        [],
        [own, *joints, last],
        size=738000,
        limit=4,
    )[0]


def gather_params(kernel, vectors):
    own = kernel.shape[1]
    pack = jnp.concatenate([kernel, *vectors, jnp.zeros((TAP_ROWS - KS * KS - len(vectors), own), F32)])
    whole = lax.all_gather(pack, "dp", axis=1, tiled=True)
    return whole.reshape(TAP_ROWS, -1, LANES).transpose(1, 0, 2)


def sum_params(parts, factor):
    flat = parts.transpose(1, 0, 2).reshape(TAP_ROWS, -1)
    sums = lax.psum(lax.psum_scatter(flat, "dp", scatter_dimension=1, tiled=True), "tile") * factor
    taps = KS * KS
    return [sums[:taps]] + [sums[taps + index] for index in range(4)]


def add_blocks(blocks):
    def body(*refs):
        value = refs[0][...]
        for ref in refs[1:-1]:
            value = value + ref[...]
        refs[-1][...] = value

    return call(body, [shape(blocks[0].shape, F32)], [], blocks, size=738000, limit=4)[0]


def finish(total, moved, factor):
    tiles, rows, _ = total.shape
    taps = KS * KS

    def body(*refs):
        outs = refs[1 + len(moved) :]
        for tile in range(tiles):
            value = refs[0][tile]
            for other in refs[1 : 1 + len(moved)]:
                value = value + other[tile]
            value = value * factor
            outs[0][:, lane_tile(tile)] = value[:taps]
            for index in range(4):
                outs[1 + index][:, lane_tile(tile)] = value[taps + index : taps + index + 1]

    taps_sum, *vectors = call(
        body,
        [shape((taps, tiles * LANES), F32)] + [shape((1, tiles * LANES), F32)] * 4,
        [],
        [total, *moved],
        size=2214000,
        limit=4,
    )
    return [taps_sum] + [v.reshape(-1) for v in vectors]


def after(block, *others):
    return lax.optimization_barrier((block, *others))[0]


def pack_shard(rows_in, rows_out, bias):
    units, width = rows_in.shape
    row = jnp.pad(bias.reshape(1, units), ((0, BIAS_ROWS - 1), (0, width - units)))
    return jnp.concatenate([rows_in, rows_out, row])


def first_sends(field, rows_in, rows_out, bias, kernel, vectors, strip):
    pixels, width = field.shape
    units = rows_in.shape[0]
    taps, own = kernel.shape
    pairings = row_pairings()
    shard_rows = 2 * units + BIAS_ROWS
    half = TAP_ROWS // 2

    def body(bias_ref, field_ref, in_ref, out_ref, kernel_ref, *refs):
        vector_refs, refs = refs[: len(vectors)], refs[len(vectors) :]
        shard, joint, pack, sends = refs[0], refs[1], refs[2], refs[3 : 3 + pairings]
        tap_stage, vector_stage, sems = refs[3 + pairings :]
        row, _ = grid_place()
        copies = [
            pltpu.make_async_copy(in_ref, shard.at[pl.ds(0, units)], sems.at[0]),
            pltpu.make_async_copy(out_ref, shard.at[pl.ds(units, units)], sems.at[1]),
            pltpu.make_async_copy(kernel_ref, tap_stage, sems.at[2]),
        ]
        for index in range(pairings):
            start = pl.multiple_of((1 - (row + index) % 2) * (pixels - strip), 16)
            copies.append(
                pltpu.make_async_copy(field_ref.at[pl.ds(start, strip)], sends[index], sems.at[3 + index])
            )
        for index, ref in enumerate(vector_refs):
            copies.append(
                pltpu.make_async_copy(ref, vector_stage.at[index], sems.at[3 + pairings + index])
            )
        for copy in copies:
            copy.start()
        line = jnp.concatenate([bias_ref[...].astype(F32), jnp.zeros((1, width - units), F32)], axis=1)
        first = lax.broadcasted_iota(jnp.int32, (BIAS_ROWS, width), 0) == 0
        shard[2 * units :] = jnp.where(first, jnp.broadcast_to(line, (BIAS_ROWS, width)), 0.0).astype(BF16)
        for copy in copies:
            copy.wait()
        for tile in range(own // LANES):
            pack[tile, TAP_ROWS - 8 :, :] = jnp.zeros((8, LANES), F32)
            pack[tile, :taps, :] = tap_stage[:, lane_tile(tile)]
            for index in range(len(vectors)):
                pack[tile, taps + index : taps + index + 1, :] = vector_stage[index, :, lane_tile(tile)]
        joint[:shard_rows] = shard[...]
        for part in range(2 * own // LANES):
            value = pack[part // 2, part % 2 * half : (part % 2 + 1) * half, :]
            value = jnp.concatenate([value, jnp.zeros((PARAM_ROWS - half, LANES), F32)])
            high = value.astype(BF16)
            joint[shard_rows:, lane_tile(2 * part)] = high
            joint[shard_rows:, lane_tile(2 * part + 1)] = (value - high.astype(F32)).astype(BF16)

    outs = [
        shape((shard_rows, width), BF16),
        shape((shard_rows + PARAM_ROWS, width), BF16),
        shape((own // LANES, TAP_ROWS, LANES), F32),
    ]
    outs += [shape((strip, width), BF16)] * pairings
    args = [bias.reshape(1, units), field, rows_in, rows_out, kernel, *vectors]
    return pl.pallas_call(
        body,
        out_shape=outs,
        in_specs=[VMEM] + [pl.BlockSpec(memory_space=pltpu.HBM)] * (len(args) - 1),
        out_specs=[VMEM] * len(outs),
        scratch_shapes=[
            pltpu.VMEM((taps, own), F32),
            pltpu.VMEM((len(vectors), 1, own), F32),
            pltpu.SemaphoreType.DMA((3 + pairings + len(vectors),)),
        ],
        compiler_params=pltpu.CompilerParams(vmem_limit_bytes=62 * 1024 * 1024),
        cost_estimate=pl.CostEstimate(flops=10000, bytes_accessed=1000000, transcendentals=0),
    )(*args)


def row_sends(field, strip):
    row, _ = grid_place()
    starts = [(1 - (row + first) % 2) * (field.shape[0] - strip) for first in range(row_pairings())]
    return [lax.dynamic_slice_in_dim(field, start, strip, 0) for start in starts]


def gathered_shard(in_weight, out_weight, hidden_bias):
    units = in_weight.shape[0]
    groups, count = lax.axis_size("dp"), lax.axis_size("tile")
    place = lax.axis_index("tile")
    member = place // 4 % 2 * 2 + place % 2

    def mine(array):
        whole = lax.all_gather(array, ("dp", "tile"), axis=0, tiled=True)
        whole = whole.reshape((4, groups * count // 4 * units) + array.shape[1:])
        return lax.dynamic_index_in_dim(whole, member, 0, keepdims=False)

    rows_in, rows_out, bias = mine(in_weight), mine(out_weight), mine(hidden_bias)
    return pack_shard(rows_in, rows_out, bias)


def per_device(
    features,
    cotangent,
    in_weight,
    out_weight,
    hidden_bias,
    kernel,
    conv_bias,
    norm_gain,
    norm_bias,
    layer_scale,
    out_bias,
):
    image_count, _, rows, cols, width = features.shape
    groups, count = lax.axis_size("dp"), lax.axis_size("tile")
    units = in_weight.shape[0]
    pixels = rows * cols
    own = kernel.shape[1]
    strip = MARGIN * cols
    field = features.reshape(pixels, width)
    upstream = cotangent.reshape(pixels, width)

    by_permutes = units % 16 == 0 and groups == 4 and count == 8 and units < width and 4 * own == width
    vectors = [v.reshape(1, own) for v in (conv_bias, norm_gain, norm_bias, layer_scale, out_bias)]
    if by_permutes:
        held, joint, piece, *sends = first_sends(
            field, in_weight, out_weight, hidden_bias, kernel, vectors, strip
        )
        first, second, other = across(joint, 1), across(joint, 2), tile_swap(held, 2)
        last = across(piece, 3)
        bands = swap_rows(sends)
        first, second, other, last, bands = lax.optimization_barrier((first, second, other, last, bands))
        params = place_params(piece, [first, second], last)
        other_first = across(after(other, first, second), 1)
        other_second = across(after(other, first, second), 2)
        far = across(after(first, other_first, other_second), 2)
        other_far = across(after(other_second, other_first), 1)
        shards = [held, first, second, far, other, other_first, other_second, other_far]
    else:
        bands = swap_rows(row_sends(field, strip))
        params = gather_params(kernel, vectors)
        shards = [gathered_shard(in_weight, out_weight, hidden_bias)]
        units = shards[0].shape[0] // 2 - BIAS_ROWS // 2
    far_upstream = tile_swap(after(upstream, *bands), 4)
    sides = swap_cols(border_columns(field, bands, rows, cols))
    acts, standard, inverse, padded = forward(field, bands, sides, params, rows, cols)
    far_acts = tile_swap(after(acts, far_upstream), 4)
    normed = [acts, far_acts, tile_swap(acts, 1), tile_swap(far_acts, 1)]
    upstreams = [upstream, far_upstream, tile_swap(upstream, 1), tile_swap(far_upstream, 1)]
    hidden, back_own, back_send = hidden_values(normed, upstreams, params, shards, units)

    def group_sum(mine, theirs, *others):
        peer = tile_swap(theirs, 1)
        return mine, peer, tile_swap(after(pair_sum(mine, peer), *others), 4)

    back_sums = group_sum(back_own, back_send)
    out_own, out_send, scale_part = project(hidden, upstreams, shards, units)
    back_conv, wire, vector_parts, *back_sends = norm_backward(
        *back_sums, standard, inverse, params, upstream, rows, cols
    )
    parts = kernel_gradient(
        padded, back_conv, vector_parts, scale_part, rows, cols, groups if by_permutes else 1
    )
    back_bands = swap_rows(back_sends)
    block = block_output(*group_sum(out_own, out_send, *back_bands), params, field)
    back_sides = swap_cols(border_columns(wire, back_bands, rows, cols))
    grad = input_gradient(wire, back_bands, back_sides, params, upstream, rows, cols)
    factor = 1.0 / math.sqrt(image_count * groups * count * pixels)
    if by_permutes:
        total = add_blocks([parts[0]] + [across(parts[bits], bits) for bits in range(1, groups)])
        total = add_blocks([total, tile_swap(total, 1)])
        moved = [tile_swap(total, bits) for bits in range(2, count, 2)]
        sums = finish(after(total, grad), moved, factor)
    else:
        sums = sum_params(parts[0], factor)
    return (block.reshape(features.shape), grad.reshape(features.shape), *sums)


def solution(mesh):
    placed = (
        P("dp", "tile", None, None, None),
        P("dp", "tile", None, None, None),
        P(("dp", "tile"), None),
        P(("dp", "tile"), None),
        P(("dp", "tile")),
        P(None, "dp"),
        P("dp"),
        P("dp"),
        P("dp"),
        P("dp"),
        P("dp"),
    )
    return jax.shard_map(
        per_device,
        mesh=mesh,
        in_specs=placed,
        out_specs=(
            P("dp", "tile", None, None, None),
            P("dp", "tile", None, None, None),
            P(None, "dp"),
            P("dp"),
            P("dp"),
            P("dp"),
            P("dp"),
        ),
        check_vma=False,
    )
```

time: 124 us -> 104 us (0.84)
  the two profiles are of different devices: /device:TPU:1 before, /device:TPU:0 now
where the time goes in v2:
time: 104 us
  waiting for transfers between devices  47.5 us (46%)
  starting transfers between devices  35 us (34%)
  Pallas kernels  18.4 us (18%)
  local copies, waits for them, and re-layouts  1.78 us (2%)
    ppermute x15, waiting for transfers between devices, tile_swap(): lax.ppermute(block, 'tile', [(i, i ^ bits) for i in range(lax.axis_size('...  30.5 us
    ppermute x15, starting transfers between devices, tile_swap(): lax.ppermute(block, 'tile', [(i, i ^ bits) for i in range(lax.axis_size('...  18.6 us
    pallas_call x15, Pallas kernels, call(): pl.pallas_call(body, out_shape=outs, in_specs=[VMEM] * len(args), out_spe...  15.6 us
    ppermute x10, starting transfers between devices, across(): return lax.ppermute(block, 'dp', [(i, i ^ bits) for i in range(groups)])  12.3 us
    ppermute x10, waiting for transfers between devices, across(): return lax.ppermute(block, 'dp', [(i, i ^ bits) for i in range(groups)])  10.4 us
    ppermute x2, waiting for transfers between devices, swap_rows(): moved.append(lax.ppermute(block, 'tile', route))  6.56 us
    pallas_call x1, Pallas kernels, first_sends(): pl.pallas_call(body, out_shape=outs, in_specs=[VMEM] + [pl.BlockSpec(memo...  2.86 us
    ppermute x2, starting transfers between devices, swap_rows(): moved.append(lax.ppermute(block, 'tile', route))  2.66 us
  transfers between devices with their start and end apart: 31, of which 14 were waited for; matrix products, arithmetic and copies ran while one was open for 0% of the time, Pallas kernels for 11%

profile of v2, /device:TPU:0, one launch (start us, length us, event | category | flops | bytes accessed | tf_op | source)
XLA Modules:
  0.0 103.5 jit_solution(14034424016263953881)
XLA Ops:
  0.7 2.9 %shard_map.162 = (bf16[200,1024]{1,0:T(8,128)(2,1)}, bf16[232,1024]{1,0:T(8,128)(2,1)}, f32[2,56,128]{2,1,0:T(8,128)}, bf16[48,1024]{1,0:T(8,128)(2,1)}) custom-call(bf16[1,96]{1,0:T(2,128)(2,1)} %bitcast.31, bf16[128,1024]{1,0:T(8,128)(2,1)} %bitcast.14, bf16[96,1024]{1,0:T(8,128)(2,1)} %in_ref.1, bf16[96,1024]{1,0:T(8,128)(2,1)} %out_ref.1, ...), custom_call_target="tpu_custom_call" | custom-call | flops 10000 | bytes 1000000 | tf_op jit(solution)/shard_map/pallas_call | solution.py:612
  3.5 3.0 %collective-permute-start = (bf16[232,1024]{1,0:T(8,128)(2,1)}, bf16[232,1024]{1,0:T(8,128)(2,1)S(1)}, u32[]{:S(2)}, u32[]{:S(2)}) collective-permute-start(bf16[232,1024]{1,0:T(8,128)(2,1)} %get-tuple-element.50), channel_id=1, source_target_pairs={{0,8},{8,0},{16,24},{24,16},{1,9},{9,1},{17,25},{25,17},{2,10},{10... | collective-permute-start | bytes 1425416 | tf_op jit(solution)/shard_map/ppermute | solution.py:465
  6.5 1.5 %collective-permute-start.1 = (bf16[232,1024]{1,0:T(8,128)(2,1)}, bf16[232,1024]{1,0:T(8,128)(2,1)S(1)}, u32[]{:S(2)}, u32[]{:S(2)}) collective-permute-start(bf16[232,1024]{1,0:T(8,128)(2,1)} %get-tuple-element.50), channel_id=1, source_target_pairs={{0,16},{8,24},{16,0},{24,8},{1,17},{9,25},{17,1},{25,9},{2,18},{10... | collective-permute-start | bytes 1425416 | tf_op jit(solution)/shard_map/ppermute | solution.py:465
  8.1 1.6 %collective-permute-start.2 = (bf16[200,1024]{1,0:T(8,128)(2,1)}, bf16[200,1024]{1,0:T(8,128)(2,1)S(1)}, u32[]{:S(2)}, u32[]{:S(2)}) collective-permute-start(bf16[200,1024]{1,0:T(8,128)(2,1)} %get-tuple-element.51.refs_9_.refs_5_), channel_id=1, source_target_pairs={{0,2},{1,3},{2,0},{3,1},{4,6},{5,7},{6,4},{7,5},{8,10},{9,11},{10,... | collective-permute-start | bytes 1228808 | tf_op jit(solution)/shard_map/ppermute | solution.py:469
  9.6 2.6 %collective-permute-start.4 = (bf16[48,1024]{1,0:T(8,128)(2,1)}, bf16[48,1024]{1,0:T(8,128)(2,1)S(1)}, u32[]{:S(2)}, u32[]{:S(2)}) collective-permute-start(bf16[48,1024]{1,0:T(8,128)(2,1)} %get-tuple-element.53), channel_id=1, source_target_pairs={{0,4},{4,0},{1,5},{5,1},{2,6},{6,2},{3,7},{7,3},{8,12},{12,8},{9,1... | collective-permute-start | bytes 294920 | tf_op jit(solution)/shard_map/ppermute | solution.py:61
  12.7 7.5 %collective-permute-done.3.last_ref = f32[2,56,128]{2,1,0:T(8,128)S(1)} collective-permute-done((f32[2,56,128]{2,1,0:T(8,128)}, f32[2,56,128]{2,1,0:T(8,128)S(1)}, u32[]{:S(2)}, u32[]{:S(2)}) %collective-permute-start.3) | collective-permute-done | bytes 57376 | tf_op jit(solution)/shard_map/ppermute | solution.py:465
  22.4 2.6 %collective-permute-start.7 = (bf16[128,1024]{1,0:T(8,128)(2,1)}, bf16[128,1024]{1,0:T(8,128)(2,1)S(1)}, u32[]{:S(2)}, u32[]{:S(2)}) collective-permute-start(bf16[128,1024]{1,0:T(8,128)(2,1)} %bitcast.18), channel_id=1, source_target_pairs={{0,4},{1,5},{2,6},{3,7},{4,0},{5,1},{6,2},{7,3},{8,12},{9,13},{10,... | collective-permute-start | bytes 786440 | tf_op jit(solution)/shard_map/ppermute | solution.py:469
  27.7 3.0 %collective-permute-start.11 = (bf16[128,1024]{1,0:T(8,128)(2,1)S(1)}, bf16[128,1024]{1,0:T(8,128)(2,1)S(1)}, u32[]{:S(2)}, u32[]{:S(2)}) collective-permute-start(bf16[128,1024]{1,0:T(8,128)(2,1)S(1)} %bitcast.19), channel_id=1, source_target_pairs={{0,1},{1,0},{2,3},{3,2},{4,5},{5,4},{6,7},{7,6},{8,9},{9,8},{10,11... | collective-permute-start | bytes 786440 | tf_op jit(solution)/shard_map/ppermute | solution.py:469
  30.7 2.9 %shard_map.165 = (bf16[128,1024]{1,0:T(8,128)(2,1)S(1)}, f32[8,128,128]{2,1,0:T(8,128)S(1)}, f32[128,128]{1,0:T(8,128)S(1)}, f32[8,448,128]{2,1,0:T(8,128)S(1)}) custom-call(bf16[128,1024]{1,0:T(8,128)(2,1)S(1)} %bitcast.16, bf16[48,1024]{1,0:T(8,128)(2,1)S(1)} %collective-permute-done.4.refs_0_.refs_1_, ...), custom_call_target="tpu_custom_call" | custom-call | bytes 10701000 | tf_op jit(solution)/shard_map/pallas_call | solution.py:26
  33.6 1.9 %collective-permute-done.7.refs_5_.refs_2_ = bf16[128,1024]{1,0:T(8,128)(2,1)S(1)} collective-permute-done((bf16[128,1024]{1,0:T(8,128)(2,1)}, bf16[128,1024]{1,0:T(8,128)(2,1)S(1)}, u32[]{:S(2)}, u32[]{:S(2)}) %collective-permute-start.7) | collective-permute-done | bytes 262176 | tf_op jit(solution)/shard_map/ppermute | solution.py:469
  35.5 1.6 %collective-permute-start.15 = (bf16[232,1024]{1,0:T(8,128)(2,1)S(1)}, bf16[232,1024]{1,0:T(8,128)(2,1)S(1)}, u32[]{:S(2)}, u32[]{:S(2)}) collective-permute-start(bf16[232,1024]{1,0:T(8,128)(2,1)S(1)} %collective-permute-done.one_ref.refs_10_.refs_6_), channel_id=1, source_target_pairs={{0,16},{8,24},{16,0},{24,8},{1,17},{9,25},{17,1},{25,9},{2,18},{10... | collective-permute-start | bytes 1425416 | tf_op jit(solution)/shard_map/ppermute | solution.py:465
  38.0 4.4 %collective-permute-start.9 = (bf16[128,1024]{1,0:T(8,128)(2,1)S(1)}, bf16[128,1024]{1,0:T(8,128)(2,1)S(1)}, u32[]{:S(2)}, u32[]{:S(2)}) collective-permute-start(bf16[128,1024]{1,0:T(8,128)(2,1)S(1)} %get-tuple-element.62.refs_0_), channel_id=1, source_target_pairs={{0,1},{1,0},{2,3},{3,2},{4,5},{5,4},{6,7},{7,6},{8,9},{9,8},{10,11... | collective-permute-start | bytes 786440 | tf_op jit(solution)/shard_map/ppermute | solution.py:469
  42.4 8.5 %collective-permute-done.8.refs_1_ = bf16[128,1024]{1,0:T(8,128)(2,1)S(1)} collective-permute-done((bf16[128,1024]{1,0:T(8,128)(2,1)S(1)}, bf16[128,1024]{1,0:T(8,128)(2,1)S(1)}, u32[]{:S(2)}, u32[]{:S(2)}) %collective-permute-start.8) | collective-permute-done | bytes 262176 | tf_op jit(solution)/shard_map/ppermute | solution.py:469
  52.5 3.7 %shard_map.166 = (bf16[512,768]{1,0:T(8,128)(2,1)S(1)}, f32[256,1024]{1,0:T(8,128)S(1)}, bf16[256,1024]{1,0:T(8,128)(2,1)S(1)}) custom-call(bf16[128,1024]{1,0:T(8,128)(2,1)S(1)} %get-tuple-element.62.refs_0_, bf16[128,1024]{1,0:T(8,128)(2,1)S(1)} %collective-permute-done.8.refs_1_, bf16[128,1024]{1,0:T(8,128)(2,1)S(1)} %collective-permute-done.9.refs_2_, ...), custom_call_target="tpu_custom_call" | custom-call | bytes 13653000 | tf_op jit(solution)/shard_map/pallas_call | solution.py:26
  58.3 14.6 %collective-permute-done.19.far_ref = bf16[128,1024]{1,0:T(8,128)(2,1)S(1)} collective-permute-done((bf16[128,1024]{1,0:T(8,128)(2,1)S(1)}, bf16[128,1024]{1,0:T(8,128)(2,1)S(1)}, u32[]{:S(2)}, u32[]{:S(2)}) %collective-permute-start.19) | collective-permute-done | bytes 262176 | tf_op jit(solution)/shard_map/ppermute | solution.py:469
  73.5 6.5 %collective-permute-done.20.refs_0_.refs_1_ = bf16[48,1024]{1,0:T(8,128)(2,1)S(1)} collective-permute-done((bf16[48,1024]{1,0:T(8,128)(2,1)S(1)}, bf16[48,1024]{1,0:T(8,128)(2,1)S(1)}, u32[]{:S(2)}, u32[]{:S(2)}) %collective-permute-start.20) | collective-permute-done | bytes 98336 | tf_op jit(solution)/shard_map/ppermute | solution.py:61
  80.0 2.0 %shard_map.174 = (f32[2,56,128]{2,1,0:T(8,128)S(1)}, f32[2,56,128]{2,1,0:T(8,128)S(1)}, f32[2,56,128]{2,1,0:T(8,128)S(1)}, f32[2,56,128]{2,1,0:T(8,128)S(1)}) custom-call(f32[8,448,128]{2,1,0:T(8,128)S(1)} %get-tuple-element.79.padded_ref, f32[8,128,128]{2,1,0:T(8,128)S(1)} %get-tuple-element.80.conv, f32[8,8,128]{2,1,0:T(8,128)S(1)} %get-tuple-element.81.vectors_ref, ...), custom_call_target="tpu_custom_call" | custom-call | bytes 7380000 | tf_op jit(solution)/shard_map/pallas_call | solution.py:26
  82.2 1.5 %collective-permute-start.25 = (f32[2,56,128]{2,1,0:T(8,128)S(1)}, f32[2,56,128]{2,1,0:T(8,128)S(1)}, u32[]{:S(2)}, u32[]{:S(2)}) collective-permute-start(f32[2,56,128]{2,1,0:T(8,128)S(1)} %get-tuple-element.85), channel_id=1, source_target_pairs={{0,16},{8,24},{16,0},{24,8},{1,17},{9,25},{17,1},{25,9},{2,18},{10... | collective-permute-start | bytes 172040 | tf_op jit(solution)/shard_map/ppermute | solution.py:465
  83.7 1.9 %collective-permute-start.26 = (f32[2,56,128]{2,1,0:T(8,128)S(1)}, f32[2,56,128]{2,1,0:T(8,128)S(1)}, u32[]{:S(2)}, u32[]{:S(2)}) collective-permute-start(f32[2,56,128]{2,1,0:T(8,128)S(1)} %get-tuple-element.86), channel_id=1, source_target_pairs={{0,24},{8,16},{16,8},{24,0},{1,25},{9,17},{17,9},{25,1},{2,26},{10... | collective-permute-start | bytes 172040 | tf_op jit(solution)/shard_map/ppermute | solution.py:465
  86.5 2.2 %collective-permute-done.26.refs_3_ = f32[2,56,128]{2,1,0:T(8,128)S(1)} collective-permute-done((f32[2,56,128]{2,1,0:T(8,128)S(1)}, f32[2,56,128]{2,1,0:T(8,128)S(1)}, u32[]{:S(2)}, u32[]{:S(2)}) %collective-permute-start.26) | collective-permute-done | bytes 57376 | tf_op jit(solution)/shard_map/ppermute | solution.py:465
  90.1 3.6 %collective-permute-start.28 = (f32[2,56,128]{2,1,0:T(8,128)S(1)}, f32[2,56,128]{2,1,0:T(8,128)S(1)}, u32[]{:S(2)}, u32[]{:S(2)}) collective-permute-start(f32[2,56,128]{2,1,0:T(8,128)S(1)} %shard_map.176.refs_0_), channel_id=1, source_target_pairs={{0,2},{1,3},{2,0},{3,1},{4,6},{5,7},{6,4},{7,5},{8,10},{9,11},{10,... | collective-permute-start | bytes 172040 | tf_op jit(solution)/shard_map/ppermute | solution.py:469
  93.7 2.2 %collective-permute-start.29 = (f32[2,56,128]{2,1,0:T(8,128)S(1)}, f32[2,56,128]{2,1,0:T(8,128)S(1)}, u32[]{:S(2)}, u32[]{:S(2)}) collective-permute-start(f32[2,56,128]{2,1,0:T(8,128)S(1)} %shard_map.176.refs_0_), channel_id=1, source_target_pairs={{0,4},{1,5},{2,6},{3,7},{4,0},{5,1},{6,2},{7,3},{8,12},{9,13},{10,... | collective-permute-start | bytes 172040 | tf_op jit(solution)/shard_map/ppermute | solution.py:469
  96.2 3.4 %shard_map.173 = bf16[128,1024]{1,0:T(8,128)(2,1)} custom-call(bf16[128,1024]{1,0:T(8,128)(2,1)S(1)} %get-tuple-element.76.field_ref.refs_0_, bf16[48,1024]{1,0:T(8,128)(2,1)S(1)} %collective-permute-done.20.refs_0_.refs_1_, bf16[48,1024]{1,0:T(8,128)(2,1)S(1)} %collective-permute-done.22.refs_2_, bf16[48,1024]{1,0:T(8,128)(2,1)S(1)} %collective-permute-done.23.refs_3_, ...), custom_call_target="tpu_custom_call" | custom-call | bytes 12177000 | tf_op jit(solution)/shard_map/pallas_call | solution.py:26
  99.6 1.5 %collective-permute-done.29.refs_2_ = f32[2,56,128]{2,1,0:T(8,128)S(1)} collective-permute-done((f32[2,56,128]{2,1,0:T(8,128)S(1)}, f32[2,56,128]{2,1,0:T(8,128)S(1)}, u32[]{:S(2)}, u32[]{:S(2)}) %collective-permute-start.29) | collective-permute-done | bytes 57376 | tf_op jit(solution)/shard_map/ppermute | solution.py:469
  (64 shorter events, 15.7 us)
Async XLA Ops:
  3.5 17.5 %collective-permute-start = (bf16[232,1024]{1,0:T(8,128)(2,1)}, bf16[232,1024]{1,0:T(8,128)(2,1)S(1)}, u32[]{:S(2)}, u32[]{:S(2)}) collective-permute-start(bf16[232,1024]{1,0:T(8,128)(2,1)} %get-tuple-element.50), channel_id=1, source_target_pairs={{0,8},{8,0},{16,24},{24,16},{1,9},{9,1},{17,25},{25,17},{2,10},{10... | collective-permute-start | bytes 1425416 | tf_op jit(solution)/shard_map/ppermute | solution.py:465
  6.5 14.5 %collective-permute-start.1 = (bf16[232,1024]{1,0:T(8,128)(2,1)}, bf16[232,1024]{1,0:T(8,128)(2,1)S(1)}, u32[]{:S(2)}, u32[]{:S(2)}) collective-permute-start(bf16[232,1024]{1,0:T(8,128)(2,1)} %get-tuple-element.50), channel_id=1, source_target_pairs={{0,16},{8,24},{16,0},{24,8},{1,17},{9,25},{17,1},{25,9},{2,18},{10... | collective-permute-start | bytes 1425416 | tf_op jit(solution)/shard_map/ppermute | solution.py:465
  8.1 13.0 %collective-permute-start.2 = (bf16[200,1024]{1,0:T(8,128)(2,1)}, bf16[200,1024]{1,0:T(8,128)(2,1)S(1)}, u32[]{:S(2)}, u32[]{:S(2)}) collective-permute-start(bf16[200,1024]{1,0:T(8,128)(2,1)} %get-tuple-element.51.refs_9_.refs_5_), channel_id=1, source_target_pairs={{0,2},{1,3},{2,0},{3,1},{4,6},{5,7},{6,4},{7,5},{8,10},{9,11},{10,... | collective-permute-start | bytes 1228808 | tf_op jit(solution)/shard_map/ppermute | solution.py:469
  9.6 10.6 %collective-permute-start.4 = (bf16[48,1024]{1,0:T(8,128)(2,1)}, bf16[48,1024]{1,0:T(8,128)(2,1)S(1)}, u32[]{:S(2)}, u32[]{:S(2)}) collective-permute-start(bf16[48,1024]{1,0:T(8,128)(2,1)} %get-tuple-element.53), channel_id=1, source_target_pairs={{0,4},{4,0},{1,5},{5,1},{2,6},{6,2},{3,7},{7,3},{8,12},{12,8},{9,1... | collective-permute-start | bytes 294920 | tf_op jit(solution)/shard_map/ppermute | solution.py:61
  12.2 7.9 %collective-permute-start.3 = (f32[2,56,128]{2,1,0:T(8,128)}, f32[2,56,128]{2,1,0:T(8,128)S(1)}, u32[]{:S(2)}, u32[]{:S(2)}) collective-permute-start(f32[2,56,128]{2,1,0:T(8,128)} %get-tuple-element.52.own_ref), channel_id=1, source_target_pairs={{0,24},{8,16},{16,8},{24,0},{1,25},{9,17},{17,9},{25,1},{2,26},{10... | collective-permute-start | bytes 172040 | tf_op jit(solution)/shard_map/ppermute | solution.py:465
  21.0 14.5 %collective-permute-start.13 = (bf16[200,1024]{1,0:T(8,128)(2,1)S(1)}, bf16[200,1024]{1,0:T(8,128)(2,1)S(1)}, u32[]{:S(2)}, u32[]{:S(2)}) collective-permute-start(bf16[200,1024]{1,0:T(8,128)(2,1)S(1)} %collective-permute-done.2.refs_13_.refs_9_), channel_id=1, source_target_pairs={{0,8},{8,0},{16,24},{24,16},{1,9},{9,1},{17,25},{25,17},{2,10},{10... | collective-permute-start | bytes 1228808 | tf_op jit(solution)/shard_map/ppermute | solution.py:465
  21.6 13.9 %collective-permute-start.14 = (bf16[200,1024]{1,0:T(8,128)(2,1)S(1)}, bf16[200,1024]{1,0:T(8,128)(2,1)S(1)}, u32[]{:S(2)}, u32[]{:S(2)}) collective-permute-start(bf16[200,1024]{1,0:T(8,128)(2,1)S(1)} %collective-permute-done.2.refs_13_.refs_9_), channel_id=1, source_target_pairs={{0,16},{8,24},{16,0},{24,8},{1,17},{9,25},{17,1},{25,9},{2,18},{10... | collective-permute-start | bytes 1228808 | tf_op jit(solution)/shard_map/ppermute | solution.py:465
  22.4 13.2 %collective-permute-start.7 = (bf16[128,1024]{1,0:T(8,128)(2,1)}, bf16[128,1024]{1,0:T(8,128)(2,1)S(1)}, u32[]{:S(2)}, u32[]{:S(2)}) collective-permute-start(bf16[128,1024]{1,0:T(8,128)(2,1)} %bitcast.18), channel_id=1, source_target_pairs={{0,4},{1,5},{2,6},{3,7},{4,0},{5,1},{6,2},{7,3},{8,12},{9,13},{10,... | collective-permute-start | bytes 786440 | tf_op jit(solution)/shard_map/ppermute | solution.py:469
  27.7 14.7 %collective-permute-start.11 = (bf16[128,1024]{1,0:T(8,128)(2,1)S(1)}, bf16[128,1024]{1,0:T(8,128)(2,1)S(1)}, u32[]{:S(2)}, u32[]{:S(2)}) collective-permute-start(bf16[128,1024]{1,0:T(8,128)(2,1)S(1)} %bitcast.19), channel_id=1, source_target_pairs={{0,1},{1,0},{2,3},{3,2},{4,5},{5,4},{6,7},{7,6},{8,9},{9,8},{10,11... | collective-permute-start | bytes 786440 | tf_op jit(solution)/shard_map/ppermute | solution.py:469
  35.5 15.4 %collective-permute-start.8 = (bf16[128,1024]{1,0:T(8,128)(2,1)S(1)}, bf16[128,1024]{1,0:T(8,128)(2,1)S(1)}, u32[]{:S(2)}, u32[]{:S(2)}) collective-permute-start(bf16[128,1024]{1,0:T(8,128)(2,1)S(1)} %get-tuple-element.62.refs_0_), channel_id=1, source_target_pairs={{0,4},{1,5},{2,6},{3,7},{4,0},{5,1},{6,2},{7,3},{8,12},{9,13},{10,... | collective-permute-start | bytes 786440 | tf_op jit(solution)/shard_map/ppermute | solution.py:469
  35.5 16.9 %collective-permute-start.15 = (bf16[232,1024]{1,0:T(8,128)(2,1)S(1)}, bf16[232,1024]{1,0:T(8,128)(2,1)S(1)}, u32[]{:S(2)}, u32[]{:S(2)}) collective-permute-start(bf16[232,1024]{1,0:T(8,128)(2,1)S(1)} %collective-permute-done.one_ref.refs_10_.refs_6_), channel_id=1, source_target_pairs={{0,16},{8,24},{16,0},{24,8},{1,17},{9,25},{17,1},{25,9},{2,18},{10... | collective-permute-start | bytes 1425416 | tf_op jit(solution)/shard_map/ppermute | solution.py:465
  37.1 15.3 %collective-permute-start.16 = (bf16[200,1024]{1,0:T(8,128)(2,1)S(1)}, bf16[200,1024]{1,0:T(8,128)(2,1)S(1)}, u32[]{:S(2)}, u32[]{:S(2)}) collective-permute-start(bf16[200,1024]{1,0:T(8,128)(2,1)S(1)} %collective-permute-done.14.refs_15_.refs_11_), channel_id=1, source_target_pairs={{0,8},{8,0},{16,24},{24,16},{1,9},{9,1},{17,25},{25,17},{2,10},{10... | collective-permute-start | bytes 1228808 | tf_op jit(solution)/shard_map/ppermute | solution.py:465
  38.0 13.1 %collective-permute-start.9 = (bf16[128,1024]{1,0:T(8,128)(2,1)S(1)}, bf16[128,1024]{1,0:T(8,128)(2,1)S(1)}, u32[]{:S(2)}, u32[]{:S(2)}) collective-permute-start(bf16[128,1024]{1,0:T(8,128)(2,1)S(1)} %get-tuple-element.62.refs_0_), channel_id=1, source_target_pairs={{0,1},{1,0},{2,3},{3,2},{4,5},{5,4},{6,7},{7,6},{8,9},{9,8},{10,11... | collective-permute-start | bytes 786440 | tf_op jit(solution)/shard_map/ppermute | solution.py:469
  42.4 8.6 %collective-permute-start.12 = (bf16[128,1024]{1,0:T(8,128)(2,1)S(1)}, bf16[128,1024]{1,0:T(8,128)(2,1)S(1)}, u32[]{:S(2)}, u32[]{:S(2)}) collective-permute-start(bf16[128,1024]{1,0:T(8,128)(2,1)S(1)} %collective-permute-done.7.refs_5_.refs_2_), channel_id=1, source_target_pairs={{0,1},{1,0},{2,3},{3,2},{4,5},{5,4},{6,7},{7,6},{8,9},{9,8},{10,11... | collective-permute-start | bytes 786440 | tf_op jit(solution)/shard_map/ppermute | solution.py:469
  57.4 16.0 %collective-permute-start.17 = (bf16[256,1024]{1,0:T(8,128)(2,1)S(1)}, bf16[256,1024]{1,0:T(8,128)(2,1)S(1)}, u32[]{:S(2)}, u32[]{:S(2)}) collective-permute-start(bf16[256,1024]{1,0:T(8,128)(2,1)S(1)} %get-tuple-element.69), channel_id=1, source_target_pairs={{0,1},{1,0},{2,3},{3,2},{4,5},{5,4},{6,7},{7,6},{8,9},{9,8},{10,11... | collective-permute-start | bytes 1572872 | tf_op jit(solution)/shard_map/ppermute | solution.py:469
  58.2 14.6 %collective-permute-start.19 = (bf16[128,1024]{1,0:T(8,128)(2,1)S(1)}, bf16[128,1024]{1,0:T(8,128)(2,1)S(1)}, u32[]{:S(2)}, u32[]{:S(2)}) collective-permute-start(bf16[128,1024]{1,0:T(8,128)(2,1)S(1)} %shard_map.169), channel_id=1, source_target_pairs={{0,4},{1,5},{2,6},{3,7},{4,0},{5,1},{6,2},{7,3},{8,12},{9,13},{10,... | collective-permute-start | bytes 786440 | tf_op jit(solution)/shard_map/ppermute | solution.py:469
  73.3 6.6 %collective-permute-start.20 = (bf16[48,1024]{1,0:T(8,128)(2,1)S(1)}, bf16[48,1024]{1,0:T(8,128)(2,1)S(1)}, u32[]{:S(2)}, u32[]{:S(2)}) collective-permute-start(bf16[48,1024]{1,0:T(8,128)(2,1)S(1)} %get-tuple-element.74), channel_id=1, source_target_pairs={{0,4},{4,0},{1,5},{5,1},{2,6},{6,2},{3,7},{7,3},{8,12},{12,8},{9,1... | collective-permute-start | bytes 294920 | tf_op jit(solution)/shard_map/ppermute | solution.py:61
  80.0 22.6 %collective-permute-start.21 = (bf16[128,1024]{1,0:T(8,128)(2,1)S(1)}, bf16[128,1024]{1,0:T(8,128)(2,1)S(1)}, u32[]{:S(2)}, u32[]{:S(2)}) collective-permute-start(bf16[128,1024]{1,0:T(8,128)(2,1)S(1)} %shard_map.168), channel_id=1, source_target_pairs={{0,4},{1,5},{2,6},{3,7},{4,0},{5,1},{6,2},{7,3},{8,12},{9,13},{10,... | collective-permute-start | bytes 786440 | tf_op jit(solution)/shard_map/ppermute | solution.py:469
  83.7 5.1 %collective-permute-start.26 = (f32[2,56,128]{2,1,0:T(8,128)S(1)}, f32[2,56,128]{2,1,0:T(8,128)S(1)}, u32[]{:S(2)}, u32[]{:S(2)}) collective-permute-start(f32[2,56,128]{2,1,0:T(8,128)S(1)} %get-tuple-element.86), channel_id=1, source_target_pairs={{0,24},{8,16},{16,8},{24,0},{1,25},{9,17},{17,9},{25,1},{2,26},{10... | collective-permute-start | bytes 172040 | tf_op jit(solution)/shard_map/ppermute | solution.py:465
  85.7 10.2 %collective-permute-start.22 = (bf16[48,1024]{1,0:T(8,128)(2,1)S(1)}, bf16[48,1024]{1,0:T(8,128)(2,1)S(1)}, u32[]{:S(2)}, u32[]{:S(2)}) collective-permute-start(bf16[48,1024]{1,0:T(8,128)(2,1)S(1)} %get-tuple-element.77), channel_id=1, source_target_pairs={{0,1},{1,0},{2,3},{3,2},{4,5},{5,4},{6,7},{7,6},{8,9},{9,8},{10,11... | collective-permute-start | bytes 294920 | tf_op jit(solution)/shard_map/ppermute | solution.py:74
  88.8 7.3 %collective-permute-start.23 = (bf16[48,1024]{1,0:T(8,128)(2,1)S(1)}, bf16[48,1024]{1,0:T(8,128)(2,1)S(1)}, u32[]{:S(2)}, u32[]{:S(2)}) collective-permute-start(bf16[48,1024]{1,0:T(8,128)(2,1)S(1)} %get-tuple-element.78), channel_id=1, source_target_pairs={{1,2},{2,1},{5,6},{6,5},{9,10},{10,9},{13,14},{14,13},{17,18},{18,... | collective-permute-start | bytes 294920 | tf_op jit(solution)/shard_map/ppermute | solution.py:74
  90.1 9.5 %collective-permute-start.28 = (f32[2,56,128]{2,1,0:T(8,128)S(1)}, f32[2,56,128]{2,1,0:T(8,128)S(1)}, u32[]{:S(2)}, u32[]{:S(2)}) collective-permute-start(f32[2,56,128]{2,1,0:T(8,128)S(1)} %shard_map.176.refs_0_), channel_id=1, source_target_pairs={{0,2},{1,3},{2,0},{3,1},{4,6},{5,7},{6,4},{7,5},{8,10},{9,11},{10,... | collective-permute-start | bytes 172040 | tf_op jit(solution)/shard_map/ppermute | solution.py:469
  93.7 7.4 %collective-permute-start.29 = (f32[2,56,128]{2,1,0:T(8,128)S(1)}, f32[2,56,128]{2,1,0:T(8,128)S(1)}, u32[]{:S(2)}, u32[]{:S(2)}) collective-permute-start(f32[2,56,128]{2,1,0:T(8,128)S(1)} %shard_map.176.refs_0_), channel_id=1, source_target_pairs={{0,4},{1,5},{2,6},{3,7},{4,0},{5,1},{6,2},{7,3},{8,12},{9,13},{10,... | collective-permute-start | bytes 172040 | tf_op jit(solution)/shard_map/ppermute | solution.py:469
  95.9 6.1 %collective-permute-start.30 = (f32[2,56,128]{2,1,0:T(8,128)S(1)}, f32[2,56,128]{2,1,0:T(8,128)S(1)}, u32[]{:S(2)}, u32[]{:S(2)}) collective-permute-start(f32[2,56,128]{2,1,0:T(8,128)S(1)} %shard_map.176.refs_0_), channel_id=1, source_target_pairs={{0,6},{1,7},{2,4},{3,5},{4,2},{5,3},{6,0},{7,1},{8,14},{9,15},{10,... | collective-permute-start | bytes 172040 | tf_op jit(solution)/shard_map/ppermute | solution.py:469
  (12 other events, 105.4 us)

commit v3 on v2

--- a/solution.py
+++ b/solution.py
@@ -14,7 +14,7 @@
 PITCH = 32
 INSET = 8
 TAP_ROWS = 56
-BIAS_ROWS = 8
+BIAS_ROWS = 16
 PARAM_ROWS = 32
 F32 = jnp.float32
 BF16 = jnp.bfloat16
@@ -69,8 +69,9 @@
         route = []
         for place in range(count):
             col = place % GX
-            if col % 2 == first and col + 1 < GX:
-                route += [(place, place + 1), (place + 1, place)]
+            if col % 2 == first:
+                other = place - col + (col + 1) % GX
+                route += [(place, other), (other, place)]
         moved.append(lax.ppermute(block, "tile", route))
     return moved
 
@@ -127,6 +128,7 @@
     tall = rows + 2 * MARGIN
     _, col = grid_place()
     even = col % 2 == 0
+    inner = (col > 0) & (col < GX - 1)
     for tile in range(width // LANES):
         above, below = above_below(band_refs, tile)
         for row in range(MARGIN):
@@ -138,7 +140,7 @@
                 row * cols : (row + 1) * cols, lane_tile(tile)
             ].astype(F32)
         first = side_refs[0][:, lane_tile(tile)].astype(F32)
-        second = side_refs[1][:, lane_tile(tile)].astype(F32)
+        second = jnp.where(inner, side_refs[1][:, lane_tile(tile)].astype(F32), 0.0)
         edge[0] = jnp.where(even, second, first)
         edge[1] = jnp.where(even, first, second)
         for row in range(tall):
@@ -213,12 +215,26 @@
     )
 
 
+def arrays_of(shards):
+    arrays, slots = [], []
+    for shard in shards:
+        places = []
+        for array, start, _ in shard:
+            known = [index for index, other in enumerate(arrays) if other is array]
+            if not known:
+                arrays.append(array)
+            places.append((known[0] if known else len(arrays) - 1, start))
+        slots.append(places)
+    return arrays, slots
+
+
 def hidden_values(normed, upstream, params, shards, units):
     pixels, width = normed[0].shape
-    members, count = len(normed), len(shards)
+    arrays, slots = arrays_of(shards)
+    members, count = len(normed), len(arrays)
     total, kept = members * pixels, members * pixels // 2
     tiles = width // LANES
-    every = count * units
+    every = len(shards) * units
     step = 32
 
     def body(*refs):
@@ -232,12 +248,12 @@
                 lanes = lane_tile(tile)
                 layer = params_ref[tile, KS * KS + 3 : KS * KS + 4, :]
                 back[here, lanes] = (up_refs[index][:, lanes].astype(F32) * layer).astype(BF16)
-        for index, shard in enumerate(shard_refs):
+        for index, (rows_in, rows_out, _) in enumerate(slots):
             here = slice(index * units, (index + 1) * units)
-            win[here] = shard[:units]
-            wout[here] = shard[units : 2 * units]
+            win[here] = shard_refs[rows_in[0]][rows_in[1] : rows_in[1] + units]
+            wout[here] = shard_refs[rows_out[0]][rows_out[1] : rows_out[1] + units]
         row = jnp.concatenate(
-            [shard[2 * units : 2 * units + 1, :units].astype(F32) for shard in shard_refs], axis=1
+            [shard_refs[bias[0]][bias[1] : bias[1] + 1, :units].astype(F32) for *_, bias in slots], axis=1
         )
         across = (((1,), (1,)), ((), ()))
         pre[...] = lax.dot_general(norm[...], win[...], across, preferred_element_type=F32) + row
@@ -268,7 +284,7 @@
             pltpu.VMEM((total, every), F32),
             pltpu.VMEM((total, every), BF16),
         ],
-        [*normed, *upstream, params, *shards],
+        [*normed, *upstream, params, *arrays],
         size=13653000,
         limit=28,
     )
@@ -276,15 +292,16 @@
 
 def project(hidden, upstream, shards, units):
     pixels, width = upstream[0].shape
-    members, count = len(upstream), len(shards)
+    arrays, slots = arrays_of([[rows_out] for _, rows_out, _ in shards])
+    members, count = len(upstream), len(arrays)
     total, kept = members * pixels, members * pixels // 2
     tiles = width // LANES
 
     def body(*refs):
         hidden_ref, up_refs, shard_refs = refs[0], refs[1 : 1 + members], refs[1 + members : 1 + members + count]
         stay, send, scale, wout = refs[1 + members + count :]
-        for index, shard in enumerate(shard_refs):
-            wout[index * units : (index + 1) * units] = shard[units : 2 * units]
+        for index, ((slot, start),) in enumerate(slots):
+            wout[index * units : (index + 1) * units] = shard_refs[slot][start : start + units]
         projected = jnp.dot(hidden_ref[...], wout[...], preferred_element_type=F32)
         stay[...] = projected[:kept]
         send[...] = projected[kept:].astype(BF16)
@@ -299,8 +316,8 @@
     return call(
         body,
         [shape((kept, width), F32), shape((kept, width), BF16), shape((tiles, 8, LANES), F32)],
-        [pltpu.VMEM((count * units, width), BF16)],
-        [hidden, *upstream, *shards],
+        [pltpu.VMEM((len(shards) * units, width), BF16)],
+        [hidden, *upstream, *arrays],
         size=3911400,
         limit=20,
     )
@@ -469,16 +486,16 @@
     return lax.ppermute(block, "tile", [(i, i ^ bits) for i in range(lax.axis_size("tile"))])
 
 
-def place_params(own, joints, last):
+def place_params(own, joints):
     share, rows, _ = own.shape
     half = rows // 2
 
-    def body(own_ref, one_ref, two_ref, last_ref, out):
+    def body(own_ref, *refs):
+        joint_refs, out = refs[:-1], refs[-1]
         me = lax.axis_index("dp")
         for part in range(share):
             out[me * share + part] = own_ref[part]
-            out[(me ^ 3) * share + part] = last_ref[part]
-        for bits, ref in ((1, one_ref), (2, two_ref)):
+        for bits, ref in enumerate(joint_refs, 1):
             start = ref.shape[0] - PARAM_ROWS
             for part in range(2 * share):
                 high = ref[start:, lane_tile(2 * part)].astype(F32)
@@ -489,7 +506,7 @@
         body,
         [shape((4 * share, rows, LANES), F32)],
         [],
-        [own, *joints, last],
+        [own, *joints],
         size=738000,
         limit=4,
     )[0]
@@ -559,71 +576,79 @@
     pixels, width = field.shape
     units = rows_in.shape[0]
     taps, own = kernel.shape
-    pairings = row_pairings()
-    shard_rows = 2 * units + BIAS_ROWS
     half = TAP_ROWS // 2
 
     def body(bias_ref, field_ref, in_ref, out_ref, kernel_ref, *refs):
         vector_refs, refs = refs[: len(vectors)], refs[len(vectors) :]
-        shard, joint, pack, sends = refs[0], refs[1], refs[2], refs[3 : 3 + pairings]
-        tap_stage, vector_stage, sems = refs[3 + pairings :]
+        joint, cross, pack, tap_stage, vector_stage, sems = refs
         row, _ = grid_place()
-        copies = [
-            pltpu.make_async_copy(in_ref, shard.at[pl.ds(0, units)], sems.at[0]),
-            pltpu.make_async_copy(out_ref, shard.at[pl.ds(units, units)], sems.at[1]),
-            pltpu.make_async_copy(kernel_ref, tap_stage, sems.at[2]),
+        start = pl.multiple_of((1 - row % 2) * (pixels - strip), 16)
+        small = [pltpu.make_async_copy(kernel_ref, tap_stage, sems.at[0])]
+        for index, ref in enumerate(vector_refs):
+            small.append(pltpu.make_async_copy(ref, vector_stage.at[index], sems.at[1 + index]))
+        at = 1 + len(vectors)
+        large = [
+            pltpu.make_async_copy(field_ref.at[pl.ds(start, strip)], cross.at[pl.ds(0, strip)], sems.at[at]),
+            pltpu.make_async_copy(in_ref, joint.at[pl.ds(0, units)], sems.at[at + 1]),
+            pltpu.make_async_copy(out_ref, joint.at[pl.ds(units, units)], sems.at[at + 2]),
         ]
-        for index in range(pairings):
-            start = pl.multiple_of((1 - (row + index) % 2) * (pixels - strip), 16)
-            copies.append(
-                pltpu.make_async_copy(field_ref.at[pl.ds(start, strip)], sends[index], sems.at[3 + index])
-            )
-        for index, ref in enumerate(vector_refs):
-            copies.append(
-                pltpu.make_async_copy(ref, vector_stage.at[index], sems.at[3 + pairings + index])
-            )
-        for copy in copies:
+        for copy in small + large:
             copy.start()
         line = jnp.concatenate([bias_ref[...].astype(F32), jnp.zeros((1, width - units), F32)], axis=1)
-        first = lax.broadcasted_iota(jnp.int32, (BIAS_ROWS, width), 0) == 0
-        shard[2 * units :] = jnp.where(first, jnp.broadcast_to(line, (BIAS_ROWS, width)), 0.0).astype(BF16)
-        for copy in copies:
+        line = jnp.broadcast_to(line, (BIAS_ROWS, width))
+        places = lax.broadcasted_iota(jnp.int32, (BIAS_ROWS, width), 0)
+        cross[strip + 2 * units :] = jnp.where(places == 0, line, 0.0).astype(BF16)
+        for copy in small:
             copy.wait()
         for tile in range(own // LANES):
             pack[tile, TAP_ROWS - 8 :, :] = jnp.zeros((8, LANES), F32)
             pack[tile, :taps, :] = tap_stage[:, lane_tile(tile)]
             for index in range(len(vectors)):
                 pack[tile, taps + index : taps + index + 1, :] = vector_stage[index, :, lane_tile(tile)]
-        joint[:shard_rows] = shard[...]
         for part in range(2 * own // LANES):
             value = pack[part // 2, part % 2 * half : (part % 2 + 1) * half, :]
             value = jnp.concatenate([value, jnp.zeros((PARAM_ROWS - half, LANES), F32)])
-            high = value.astype(BF16)
-            joint[shard_rows:, lane_tile(2 * part)] = high
-            joint[shard_rows:, lane_tile(2 * part + 1)] = (value - high.astype(F32)).astype(BF16)
+            high = value.astype(BF16).astype(F32)
+            for side, rest in enumerate((high, value - high)):
+                lanes = lane_tile(2 * part + side)
+                spread = jnp.broadcast_to(line[:1, lanes], (PARAM_ROWS, LANES))
+                places = lax.broadcasted_iota(jnp.int32, (PARAM_ROWS, LANES), 0)
+                joint[2 * units :, lanes] = jnp.where(places == half, spread, rest).astype(BF16)
+        for copy in large:
+            copy.wait()
+        cross[strip : strip + 2 * units] = joint[: 2 * units]
 
     outs = [
-        shape((shard_rows, width), BF16),
-        shape((shard_rows + PARAM_ROWS, width), BF16),
+        shape((2 * units + PARAM_ROWS, width), BF16),
+        shape((strip + 2 * units + BIAS_ROWS, width), BF16),
         shape((own // LANES, TAP_ROWS, LANES), F32),
     ]
-    outs += [shape((strip, width), BF16)] * pairings
     args = [bias.reshape(1, units), field, rows_in, rows_out, kernel, *vectors]
+    far = pl.BlockSpec(memory_space=pltpu.HBM)
     return pl.pallas_call(
         body,
         out_shape=outs,
-        in_specs=[VMEM] + [pl.BlockSpec(memory_space=pltpu.HBM)] * (len(args) - 1),
+        in_specs=[VMEM] + [far] * (len(args) - 1),
         out_specs=[VMEM] * len(outs),
         scratch_shapes=[
             pltpu.VMEM((taps, own), F32),
             pltpu.VMEM((len(vectors), 1, own), F32),
-            pltpu.SemaphoreType.DMA((3 + pairings + len(vectors),)),
+            pltpu.SemaphoreType.DMA((4 + len(vectors),)),
         ],
         compiler_params=pltpu.CompilerParams(vmem_limit_bytes=62 * 1024 * 1024),
         cost_estimate=pl.CostEstimate(flops=10000, bytes_accessed=1000000, transcendentals=0),
     )(*args)
 
 
+def cut_rows(block, cuts):
+    def body(ref, *outs):
+        for (start, count), out in zip(cuts, outs):
+            out[...] = ref[start : start + count]
+
+    outs = [shape((count, block.shape[1]), block.dtype) for _, count in cuts]
+    return call(body, outs, [], [block], size=738000, limit=4)
+
+
 def row_sends(field, strip):
     row, _ = grid_place()
     starts = [(1 - (row + first) % 2) * (field.shape[0] - strip) for first in range(row_pairings())]
@@ -634,7 +659,7 @@
     units = in_weight.shape[0]
     groups, count = lax.axis_size("dp"), lax.axis_size("tile")
     place = lax.axis_index("tile")
-    member = place // 4 % 2 * 2 + place % 2
+    member = place % 4
 
     def mine(array):
         whole = lax.all_gather(array, ("dp", "tile"), axis=0, tiled=True)
@@ -670,35 +695,46 @@
     by_permutes = units % 16 == 0 and groups == 4 and count == 8 and units < width and 4 * own == width
     vectors = [v.reshape(1, own) for v in (conv_bias, norm_gain, norm_bias, layer_scale, out_bias)]
     if by_permutes:
-        held, joint, piece, *sends = first_sends(
-            field, in_weight, out_weight, hidden_bias, kernel, vectors, strip
+        held, cross, piece = first_sends(field, in_weight, out_weight, hidden_bias, kernel, vectors, strip)
+        cross, far_upstream = tile_swap(cross, 4), tile_swap(upstream, 2)
+        first, second, far = [across(held, bits) for bits in (1, 2, 3)]
+        cross, far_upstream, first, second, far = lax.optimization_barrier(
+            (cross, far_upstream, first, second, far)
         )
-        first, second, other = across(joint, 1), across(joint, 2), tile_swap(held, 2)
-        last = across(piece, 3)
-        bands = swap_rows(sends)
-        first, second, other, last, bands = lax.optimization_barrier((first, second, other, last, bands))
-        params = place_params(piece, [first, second], last)
-        other_first = across(after(other, first, second), 1)
-        other_second = across(after(other, first, second), 2)
-        far = across(after(first, other_first, other_second), 2)
-        other_far = across(after(other_second, other_first), 1)
-        shards = [held, first, second, far, other, other_first, other_second, other_far]
+        params = place_params(piece, [first, second, far])
+        bands = cut_rows(cross, [(0, strip)])
+        (other,) = cut_rows(cross, [(strip, 2 * units + BIAS_ROWS)])
+        other_first, other_second = across(other, 1), across(other, 2)
+        (part_in,) = cut_rows(other_first, [(0, units)])
+        (part_out,) = cut_rows(other_second, [(units, units + BIAS_ROWS)])
+        far_in, far_out = across(part_in, 2), across(part_out, 1)
+        after_params = 2 * units + TAP_ROWS // 2
+        shards = [
+            [(shard, 0, units), (shard, units, units), (shard, after_params, 1)]
+            for shard in (held, first, second, far)
+        ]
+        whole = [(0, units), (units, units), (2 * units, BIAS_ROWS)]
+        shards += [[(shard, *rows) for rows in whole] for shard in (other, other_first, other_second)]
+        shards.append([(far_in, 0, units), (far_out, 0, units), (far_out, units, BIAS_ROWS)])
     else:
         bands = swap_rows(row_sends(field, strip))
         params = gather_params(kernel, vectors)
+        far_upstream = tile_swap(upstream, 2)
         shards = [gathered_shard(in_weight, out_weight, hidden_bias)]
         units = shards[0].shape[0] // 2 - BIAS_ROWS // 2
-    far_upstream = tile_swap(after(upstream, *bands), 4)
+        shards = [[(shards[0], 0, units), (shards[0], units, units), (shards[0], 2 * units, BIAS_ROWS)]]
     sides = swap_cols(border_columns(field, bands, rows, cols))
     acts, standard, inverse, padded = forward(field, bands, sides, params, rows, cols)
-    far_acts = tile_swap(after(acts, far_upstream), 4)
+    far_acts = tile_swap(acts, 2)
+    if by_permutes:
+        far_acts = after(far_acts, far_in, far_out)
     normed = [acts, far_acts, tile_swap(acts, 1), tile_swap(far_acts, 1)]
     upstreams = [upstream, far_upstream, tile_swap(upstream, 1), tile_swap(far_upstream, 1)]
     hidden, back_own, back_send = hidden_values(normed, upstreams, params, shards, units)
 
     def group_sum(mine, theirs, *others):
         peer = tile_swap(theirs, 1)
-        return mine, peer, tile_swap(after(pair_sum(mine, peer), *others), 4)
+        return mine, peer, tile_swap(after(pair_sum(mine, peer), *others), 2)
 
     back_sums = group_sum(back_own, back_send)
     out_own, out_send, scale_part = project(hidden, upstreams, shards, units)
@@ -709,16 +745,19 @@
         padded, back_conv, vector_parts, scale_part, rows, cols, groups if by_permutes else 1
     )
     back_bands = swap_rows(back_sends)
-    block = block_output(*group_sum(out_own, out_send, *back_bands), params, field)
+    back_bands[0] = after(back_bands[0], parts[0])
     back_sides = swap_cols(border_columns(wire, back_bands, rows, cols))
     grad = input_gradient(wire, back_bands, back_sides, params, upstream, rows, cols)
     factor = 1.0 / math.sqrt(image_count * groups * count * pixels)
     if by_permutes:
         total = add_blocks([parts[0]] + [across(parts[bits], bits) for bits in range(1, groups)])
+        block = block_output(*group_sum(out_own, out_send, total), params, field)
+        total = after(total, *back_sides)
         total = add_blocks([total, tile_swap(total, 1)])
-        moved = [tile_swap(total, bits) for bits in range(2, count, 2)]
-        sums = finish(after(total, grad), moved, factor)
+        total = after(add_blocks([total, tile_swap(total, 4)]), grad)
+        sums = finish(after(total, block), [tile_swap(total, 2)], factor)
     else:
+        block = block_output(*group_sum(out_own, out_send), params, field)
         sums = sum_params(parts[0], factor)
     return (block.reshape(features.shape), grad.reshape(features.shape), *sums)
 

time: 104 us -> 94.1 us (0.905)
  starting transfers between devices: 35 us -> 29.7 us
  waiting for transfers between devices: 47.5 us -> 44.9 us
  local copies, waits for them, and re-layouts: 1.78 us -> 0.02 us
    ppermute x2 -> x1, waiting for transfers between devices: 6.56 us -> 0.01 us  [swap_rows(): moved.append(lax.ppermute(block, 'tile', route))]
    ppermute x15 -> x14, starting transfers between devices: 18.6 us -> 12.1 us  [tile_swap(): lax.ppermute(block, 'tile', [(i, i ^ bits) for i in range(lax.axis_size('...]
    ppermute x4, waiting for transfers between devices: 0.01 us -> 4.21 us  [swap_cols(): moved.append(lax.ppermute(block, 'tile', route))]
    ppermute x10, waiting for transfers between devices: 10.4 us -> 7.77 us  [across(): return lax.ppermute(block, 'dp', [(i, i ^ bits) for i in range(groups)])]
    ppermute x15 -> x14, waiting for transfers between devices: 30.5 us -> 32.9 us  [tile_swap(): lax.ppermute(block, 'tile', [(i, i ^ bits) for i in range(lax.axis_size('...]
    unnamed x10 -> x8, local copies, waits for them, and re-layouts: 1.78 us -> 0.02 us
    ppermute x2 -> x1, starting transfers between devices: 2.66 us -> 2.86 us  [swap_rows(): moved.append(lax.ppermute(block, 'tile', route))]
    pallas_call x15 -> x20, Pallas kernels: 15.6 us -> 15.6 us  [call(): pl.pallas_call(body, out_shape=outs, in_specs=[VMEM] * len(args), out_spe...]
  transfers between devices with their start and end apart: 31 -> 29, of which waited for: 14 -> 17; matrix products, arithmetic and copies ran while one was open for 0% -> 0% of each run, Pallas kernels for 11% -> 12%
where the time goes in v3:
time: 94.1 us; the launch traced here: 93.9 us
  waiting for transfers between devices  44.9 us (48%)
  starting transfers between devices  29.7 us (32%)
  Pallas kernels  18.5 us (20%)
    ppermute x14, waiting for transfers between devices, tile_swap(): lax.ppermute(block, 'tile', [(i, i ^ bits) for i in range(lax.axis_size('...  32.9 us
    pallas_call x20, Pallas kernels, call(): pl.pallas_call(body, out_shape=outs, in_specs=[VMEM] * len(args), out_spe...  15.6 us
    ppermute x10, starting transfers between devices, across(): return lax.ppermute(block, 'dp', [(i, i ^ bits) for i in range(groups)])  12.4 us
    ppermute x14, starting transfers between devices, tile_swap(): lax.ppermute(block, 'tile', [(i, i ^ bits) for i in range(lax.axis_size('...  12.1 us
    ppermute x10, waiting for transfers between devices, across(): return lax.ppermute(block, 'dp', [(i, i ^ bits) for i in range(groups)])  7.77 us
    ppermute x4, waiting for transfers between devices, swap_cols(): moved.append(lax.ppermute(block, 'tile', route))  4.21 us
    pallas_call x1, Pallas kernels, first_sends(): pl.pallas_call(body, out_shape=outs, in_specs=[VMEM] + [far] * (len(args)...  2.91 us
    ppermute x1, starting transfers between devices, swap_rows(): moved.append(lax.ppermute(block, 'tile', route))  2.86 us
  transfers between devices with their start and end apart: 29, of which 17 were waited for; matrix products, arithmetic and copies ran while one was open for 0% of the time, Pallas kernels for 12%

profile of v3, /device:TPU:0, one launch (start us, length us, event | category | flops | bytes accessed | tf_op | source)
XLA Modules:
  0.0 93.9 jit_solution(1904683353270047191)
XLA Ops:
  0.6 2.9 %shard_map.162 = (bf16[224,1024]{1,0:T(8,128)(2,1)}, bf16[256,1024]{1,0:T(8,128)(2,1)}, f32[2,56,128]{2,1,0:T(8,128)}) custom-call(bf16[1,96]{1,0:T(2,128)(2,1)} %bitcast.31, bf16[128,1024]{1,0:T(8,128)(2,1)} %bitcast.20, bf16[96,1024]{1,0:T(8,128)(2,1)} %in_ref.1, bf16[96,1024]{1,0:T(8,128)(2,1)} %out_ref.1, f32[49,256]{1,0:T(8,128)} %kernel_ref.1, ...), custom_call_target="tpu_custom_call" | custom-call | flops 10000 | bytes 1000000 | tf_op jit(solution)/shard_map/pallas_call | solution.py:628
  3.6 4.1 %collective-permute-start = (bf16[256,1024]{1,0:T(8,128)(2,1)}, bf16[256,1024]{1,0:T(8,128)(2,1)S(1)}, u32[]{:S(2)}, u32[]{:S(2)}) collective-permute-start(bf16[256,1024]{1,0:T(8,128)(2,1)} %get-tuple-element.48), channel_id=1, source_target_pairs={{0,4},{1,5},{2,6},{3,7},{4,0},{5,1},{6,2},{7,3},{8,12},{9,13},{10,... | collective-permute-start | bytes 1572872 | tf_op jit(solution)/shard_map/ppermute | solution.py:486
  7.7 1.5 %collective-permute-start.2 = (bf16[224,1024]{1,0:T(8,128)(2,1)}, bf16[224,1024]{1,0:T(8,128)(2,1)S(1)}, u32[]{:S(2)}, u32[]{:S(2)}) collective-permute-start(bf16[224,1024]{1,0:T(8,128)(2,1)} %get-tuple-element.49.refs_9_.refs_5_), channel_id=1, source_target_pairs={{0,8},{8,0},{16,24},{24,16},{1,9},{9,1},{17,25},{25,17},{2,10},{10... | collective-permute-start | bytes 1376264 | tf_op jit(solution)/shard_map/ppermute | solution.py:482
  9.2 1.5 %collective-permute-start.3 = (bf16[224,1024]{1,0:T(8,128)(2,1)}, bf16[224,1024]{1,0:T(8,128)(2,1)S(1)}, u32[]{:S(2)}, u32[]{:S(2)}) collective-permute-start(bf16[224,1024]{1,0:T(8,128)(2,1)} %get-tuple-element.49.refs_9_.refs_5_), channel_id=1, source_target_pairs={{0,16},{8,24},{16,0},{24,8},{1,17},{9,25},{17,1},{25,9},{2,18},{10... | collective-permute-start | bytes 1376264 | tf_op jit(solution)/shard_map/ppermute | solution.py:482
  11.2 1.6 %collective-permute-start.1 = (bf16[128,1024]{1,0:T(8,128)(2,1)}, bf16[128,1024]{1,0:T(8,128)(2,1)S(1)}, u32[]{:S(2)}, u32[]{:S(2)}) collective-permute-start(bf16[128,1024]{1,0:T(8,128)(2,1)} %bitcast.14), channel_id=1, source_target_pairs={{0,2},{1,3},{2,0},{3,1},{4,6},{5,7},{6,4},{7,5},{8,10},{9,11},{10,... | collective-permute-start | bytes 786440 | tf_op jit(solution)/shard_map/ppermute | solution.py:486
  12.7 12.1 %collective-permute-done.1.refs_5_.refs_2_ = bf16[128,1024]{1,0:T(8,128)(2,1)S(1)} collective-permute-done((bf16[128,1024]{1,0:T(8,128)(2,1)}, bf16[128,1024]{1,0:T(8,128)(2,1)S(1)}, u32[]{:S(2)}, u32[]{:S(2)}) %collective-permute-start.1) | collective-permute-done | bytes 262176 | tf_op jit(solution)/shard_map/ppermute | solution.py:486
  24.8 6.1 %collective-permute-done.3.refs_1_.refs_11_.refs_7_ = bf16[224,1024]{1,0:T(8,128)(2,1)S(1)} collective-permute-done((bf16[224,1024]{1,0:T(8,128)(2,1)}, bf16[224,1024]{1,0:T(8,128)(2,1)S(1)}, u32[]{:S(2)}, u32[]{:S(2)}) %collective-permute-start.3) | collective-permute-done | bytes 458784 | tf_op jit(solution)/shard_map/ppermute | solution.py:482
  31.1 1.6 %collective-permute-start.10 = (bf16[208,1024]{1,0:T(8,128)(2,1)S(1)}, bf16[208,1024]{1,0:T(8,128)(2,1)S(1)}, u32[]{:S(2)}, u32[]{:S(2)}) collective-permute-start(bf16[208,1024]{1,0:T(8,128)(2,1)S(1)} %shard_map.167.refs_13_.refs_9_), channel_id=1, source_target_pairs={{0,16},{8,24},{16,0},{24,8},{1,17},{9,25},{17,1},{25,9},{2,18},{10... | collective-permute-start | bytes 1277960 | tf_op jit(solution)/shard_map/ppermute | solution.py:482
  32.7 1.5 %collective-permute-start.8 = (bf16[208,1024]{1,0:T(8,128)(2,1)S(1)}, bf16[208,1024]{1,0:T(8,128)(2,1)S(1)}, u32[]{:S(2)}, u32[]{:S(2)}) collective-permute-start(bf16[208,1024]{1,0:T(8,128)(2,1)S(1)} %shard_map.167.refs_13_.refs_9_), channel_id=1, source_target_pairs={{0,8},{8,0},{16,24},{24,16},{1,9},{9,1},{17,25},{25,17},{2,10},{10... | collective-permute-start | bytes 1277960 | tf_op jit(solution)/shard_map/ppermute | solution.py:482
  35.8 3.3 %collective-permute-done.6.refs_3_ = bf16[48,1024]{1,0:T(8,128)(2,1)S(1)} collective-permute-done((bf16[48,1024]{1,0:T(8,128)(2,1)S(1)}, bf16[48,1024]{1,0:T(8,128)(2,1)S(1)}, u32[]{:S(2)}, u32[]{:S(2)}) %collective-permute-start.6) | collective-permute-done | bytes 98336 | tf_op jit(solution)/shard_map/ppermute | solution.py:75
  39.1 2.9 %shard_map.166 = (bf16[128,1024]{1,0:T(8,128)(2,1)S(1)}, f32[8,128,128]{2,1,0:T(8,128)S(1)}, f32[128,128]{1,0:T(8,128)S(1)}, f32[8,448,128]{2,1,0:T(8,128)S(1)}) custom-call(bf16[128,1024]{1,0:T(8,128)(2,1)S(1)} %bitcast.22, bf16[48,1024]{1,0:T(8,128)(2,1)S(1)} %shard_map.163.refs_0_.refs_1_, bf16[48,1024]{1,0:T(8,128)(2,1)S(1)} %collective-permute-done.5.refs_2_, ...), custom_call_target="tpu_custom_call" | custom-call | bytes 10701000 | tf_op jit(solution)/shard_map/pallas_call | solution.py:26
  42.8 1.2 %collective-permute-start.11 = (bf16[112,1024]{1,0:T(8,128)(2,1)S(1)}, bf16[112,1024]{1,0:T(8,128)(2,1)S(1)}, u32[]{:S(2)}, u32[]{:S(2)}) collective-permute-start(bf16[112,1024]{1,0:T(8,128)(2,1)S(1)} %shard_map.169), channel_id=1, source_target_pairs={{0,8},{8,0},{16,24},{24,16},{1,9},{9,1},{17,25},{25,17},{2,10},{10... | collective-permute-start | bytes 688136 | tf_op jit(solution)/shard_map/ppermute | solution.py:482
  45.6 5.3 %collective-permute-done.7.refs_1_ = bf16[128,1024]{1,0:T(8,128)(2,1)S(1)} collective-permute-done((bf16[128,1024]{1,0:T(8,128)(2,1)S(1)}, bf16[128,1024]{1,0:T(8,128)(2,1)S(1)}, u32[]{:S(2)}, u32[]{:S(2)}) %collective-permute-start.7) | collective-permute-done | bytes 262176 | tf_op jit(solution)/shard_map/ppermute | solution.py:486
  52.8 3.7 %shard_map.170 = (bf16[512,768]{1,0:T(8,128)(2,1)S(1)}, f32[256,1024]{1,0:T(8,128)S(1)}, bf16[256,1024]{1,0:T(8,128)(2,1)S(1)}) custom-call(bf16[128,1024]{1,0:T(8,128)(2,1)S(1)} %get-tuple-element.57.refs_0_, bf16[128,1024]{1,0:T(8,128)(2,1)S(1)} %collective-permute-done.7.refs_1_, bf16[128,1024]{1,0:T(8,128)(2,1)S(1)} %collective-permute-done.12.refs_2_, ...), custom_call_target="tpu_custom_call" | custom-call | bytes 13653000 | tf_op jit(solution)/shard_map/pallas_call | solution.py:26
  59.4 7.6 %collective-permute-done.18.far_ref = bf16[128,1024]{1,0:T(8,128)(2,1)S(1)} collective-permute-done((bf16[128,1024]{1,0:T(8,128)(2,1)S(1)}, bf16[128,1024]{1,0:T(8,128)(2,1)S(1)}, u32[]{:S(2)}, u32[]{:S(2)}) %collective-permute-start.18) | collective-permute-done | bytes 262176 | tf_op jit(solution)/shard_map/ppermute | solution.py:486
  67.5 2.9 %collective-permute-start.23 = (bf16[48,1024]{1,0:T(8,128)(2,1)S(1)}, bf16[48,1024]{1,0:T(8,128)(2,1)S(1)}, u32[]{:S(2)}, u32[]{:S(2)}) collective-permute-start(bf16[48,1024]{1,0:T(8,128)(2,1)S(1)} %get-tuple-element.77), channel_id=1, source_target_pairs={{0,4},{4,0},{1,5},{5,1},{2,6},{6,2},{3,7},{7,3},{8,12},{12,8},{9,1... | collective-permute-start | bytes 294920 | tf_op jit(solution)/shard_map/ppermute | solution.py:61
  70.4 2.0 %shard_map.175 = (f32[2,56,128]{2,1,0:T(8,128)S(1)}, f32[2,56,128]{2,1,0:T(8,128)S(1)}, f32[2,56,128]{2,1,0:T(8,128)S(1)}, f32[2,56,128]{2,1,0:T(8,128)S(1)}) custom-call(f32[8,448,128]{2,1,0:T(8,128)S(1)} %get-tuple-element.63.padded_ref, f32[8,128,128]{2,1,0:T(8,128)S(1)} %get-tuple-element.68.conv, f32[8,8,128]{2,1,0:T(8,128)S(1)} %get-tuple-element.69.vectors_ref, ...), custom_call_target="tpu_custom_call" | custom-call | bytes 7380000 | tf_op jit(solution)/shard_map/pallas_call | solution.py:26
  72.3 1.2 %collective-permute-start.19 = (f32[2,56,128]{2,1,0:T(8,128)S(1)}, f32[2,56,128]{2,1,0:T(8,128)S(1)}, u32[]{:S(2)}, u32[]{:S(2)}) collective-permute-start(f32[2,56,128]{2,1,0:T(8,128)S(1)} %get-tuple-element.72), channel_id=1, source_target_pairs={{0,8},{8,0},{16,24},{24,16},{1,9},{9,1},{17,25},{25,17},{2,10},{10... | collective-permute-start | bytes 172040 | tf_op jit(solution)/shard_map/ppermute | solution.py:482
  74.1 1.8 %collective-permute-start.21 = (f32[2,56,128]{2,1,0:T(8,128)S(1)}, f32[2,56,128]{2,1,0:T(8,128)S(1)}, u32[]{:S(2)}, u32[]{:S(2)}) collective-permute-start(f32[2,56,128]{2,1,0:T(8,128)S(1)} %get-tuple-element.74), channel_id=1, source_target_pairs={{0,24},{8,16},{16,8},{24,0},{1,25},{9,17},{17,9},{25,1},{2,26},{10... | collective-permute-start | bytes 172040 | tf_op jit(solution)/shard_map/ppermute | solution.py:482
  76.2 1.4 %collective-permute-start.25 = (bf16[48,1024]{1,0:T(8,128)(2,1)S(1)}, bf16[48,1024]{1,0:T(8,128)(2,1)S(1)}, u32[]{:S(2)}, u32[]{:S(2)}) collective-permute-start(bf16[48,1024]{1,0:T(8,128)(2,1)S(1)} %get-tuple-element.80), channel_id=1, source_target_pairs={{1,2},{2,1},{3,0},{0,3},{5,6},{6,5},{7,4},{4,7},{9,10},{10,9},{11,... | collective-permute-start | bytes 294920 | tf_op jit(solution)/shard_map/ppermute | solution.py:75
  77.8 1.4 %collective-permute-done.21.refs_3_ = f32[2,56,128]{2,1,0:T(8,128)S(1)} collective-permute-done((f32[2,56,128]{2,1,0:T(8,128)S(1)}, f32[2,56,128]{2,1,0:T(8,128)S(1)}, u32[]{:S(2)}, u32[]{:S(2)}) %collective-permute-start.21) | collective-permute-done | bytes 57376 | tf_op jit(solution)/shard_map/ppermute | solution.py:482
  83.5 3.4 %shard_map.179 = bf16[128,1024]{1,0:T(8,128)(2,1)} custom-call(bf16[128,1024]{1,0:T(8,128)(2,1)S(1)} %get-tuple-element.76.field_ref.refs_0_, bf16[48,1024]{1,0:T(8,128)(2,1)S(1)} %collective-permute-done.23.refs_0_.refs_1_, bf16[48,1024]{1,0:T(8,128)(2,1)S(1)} %collective-permute-done.24.refs_2_, bf16[48,1024]{1,0:T(8,128)(2,1)S(1)} %collective-permute-done.25.refs_3_, ...), custom_call_target="tpu_custom_call" | custom-call | bytes 12177000 | tf_op jit(solution)/shard_map/pallas_call | solution.py:26
  86.8 2.2 %collective-permute-done.27.refs_1_ = f32[2,56,128]{2,1,0:T(8,128)S(1)} collective-permute-done((f32[2,56,128]{2,1,0:T(8,128)S(1)}, f32[2,56,128]{2,1,0:T(8,128)S(1)}, u32[]{:S(2)}, u32[]{:S(2)}) %collective-permute-start.27) | collective-permute-done | bytes 57376 | tf_op jit(solution)/shard_map/ppermute | solution.py:486
  90.3 3.0 %collective-permute-done.28.refs_1_ = f32[2,56,128]{2,1,0:T(8,128)S(1)} collective-permute-done((f32[2,56,128]{2,1,0:T(8,128)S(1)}, f32[2,56,128]{2,1,0:T(8,128)S(1)}, u32[]{:S(2)}, u32[]{:S(2)}) %collective-permute-start.28) | collective-permute-done | bytes 57376 | tf_op jit(solution)/shard_map/ppermute | solution.py:486
  (63 shorter events, 17.0 us)
Async XLA Ops:
  3.6 27.5 %collective-permute-start = (bf16[256,1024]{1,0:T(8,128)(2,1)}, bf16[256,1024]{1,0:T(8,128)(2,1)S(1)}, u32[]{:S(2)}, u32[]{:S(2)}) collective-permute-start(bf16[256,1024]{1,0:T(8,128)(2,1)} %get-tuple-element.48), channel_id=1, source_target_pairs={{0,4},{1,5},{2,6},{3,7},{4,0},{5,1},{6,2},{7,3},{8,12},{9,13},{10,... | collective-permute-start | bytes 1572872 | tf_op jit(solution)/shard_map/ppermute | solution.py:486
  7.7 17.2 %collective-permute-start.2 = (bf16[224,1024]{1,0:T(8,128)(2,1)}, bf16[224,1024]{1,0:T(8,128)(2,1)S(1)}, u32[]{:S(2)}, u32[]{:S(2)}) collective-permute-start(bf16[224,1024]{1,0:T(8,128)(2,1)} %get-tuple-element.49.refs_9_.refs_5_), channel_id=1, source_target_pairs={{0,8},{8,0},{16,24},{24,16},{1,9},{9,1},{17,25},{25,17},{2,10},{10... | collective-permute-start | bytes 1376264 | tf_op jit(solution)/shard_map/ppermute | solution.py:482
  9.2 21.7 %collective-permute-start.3 = (bf16[224,1024]{1,0:T(8,128)(2,1)}, bf16[224,1024]{1,0:T(8,128)(2,1)S(1)}, u32[]{:S(2)}, u32[]{:S(2)}) collective-permute-start(bf16[224,1024]{1,0:T(8,128)(2,1)} %get-tuple-element.49.refs_9_.refs_5_), channel_id=1, source_target_pairs={{0,16},{8,24},{16,0},{24,8},{1,17},{9,25},{17,1},{25,9},{2,18},{10... | collective-permute-start | bytes 1376264 | tf_op jit(solution)/shard_map/ppermute | solution.py:482
  10.7 20.2 %collective-permute-start.4 = (bf16[224,1024]{1,0:T(8,128)(2,1)}, bf16[224,1024]{1,0:T(8,128)(2,1)S(1)}, u32[]{:S(2)}, u32[]{:S(2)}) collective-permute-start(bf16[224,1024]{1,0:T(8,128)(2,1)} %get-tuple-element.49.refs_9_.refs_5_), channel_id=1, source_target_pairs={{0,24},{8,16},{16,8},{24,0},{1,25},{9,17},{17,9},{25,1},{2,26},{10... | collective-permute-start | bytes 1376264 | tf_op jit(solution)/shard_map/ppermute | solution.py:482
  11.2 13.7 %collective-permute-start.1 = (bf16[128,1024]{1,0:T(8,128)(2,1)}, bf16[128,1024]{1,0:T(8,128)(2,1)S(1)}, u32[]{:S(2)}, u32[]{:S(2)}) collective-permute-start(bf16[128,1024]{1,0:T(8,128)(2,1)} %bitcast.14), channel_id=1, source_target_pairs={{0,2},{1,3},{2,0},{3,1},{4,6},{5,7},{6,4},{7,5},{8,10},{9,11},{10,... | collective-permute-start | bytes 786440 | tf_op jit(solution)/shard_map/ppermute | solution.py:486
  31.1 11.7 %collective-permute-start.10 = (bf16[208,1024]{1,0:T(8,128)(2,1)S(1)}, bf16[208,1024]{1,0:T(8,128)(2,1)S(1)}, u32[]{:S(2)}, u32[]{:S(2)}) collective-permute-start(bf16[208,1024]{1,0:T(8,128)(2,1)S(1)} %shard_map.167.refs_13_.refs_9_), channel_id=1, source_target_pairs={{0,16},{8,24},{16,0},{24,8},{1,17},{9,25},{17,1},{25,9},{2,18},{10... | collective-permute-start | bytes 1277960 | tf_op jit(solution)/shard_map/ppermute | solution.py:482
  32.7 11.3 %collective-permute-start.8 = (bf16[208,1024]{1,0:T(8,128)(2,1)S(1)}, bf16[208,1024]{1,0:T(8,128)(2,1)S(1)}, u32[]{:S(2)}, u32[]{:S(2)}) collective-permute-start(bf16[208,1024]{1,0:T(8,128)(2,1)S(1)} %shard_map.167.refs_13_.refs_9_), channel_id=1, source_target_pairs={{0,8},{8,0},{16,24},{24,16},{1,9},{9,1},{17,25},{25,17},{2,10},{10... | collective-permute-start | bytes 1277960 | tf_op jit(solution)/shard_map/ppermute | solution.py:482
  34.5 4.6 %collective-permute-start.6 = (bf16[48,1024]{1,0:T(8,128)(2,1)S(1)}, bf16[48,1024]{1,0:T(8,128)(2,1)S(1)}, u32[]{:S(2)}, u32[]{:S(2)}) collective-permute-start(bf16[48,1024]{1,0:T(8,128)(2,1)S(1)} %get-tuple-element.52), channel_id=1, source_target_pairs={{1,2},{2,1},{3,0},{0,3},{5,6},{6,5},{7,4},{4,7},{9,10},{10,9},{11,... | collective-permute-start | bytes 294920 | tf_op jit(solution)/shard_map/ppermute | solution.py:75
  42.0 9.0 %collective-permute-start.7 = (bf16[128,1024]{1,0:T(8,128)(2,1)S(1)}, bf16[128,1024]{1,0:T(8,128)(2,1)S(1)}, u32[]{:S(2)}, u32[]{:S(2)}) collective-permute-start(bf16[128,1024]{1,0:T(8,128)(2,1)S(1)} %get-tuple-element.57.refs_0_), channel_id=1, source_target_pairs={{0,2},{1,3},{2,0},{3,1},{4,6},{5,7},{6,4},{7,5},{8,10},{9,11},{10,... | collective-permute-start | bytes 786440 | tf_op jit(solution)/shard_map/ppermute | solution.py:486
  42.8 8.3 %collective-permute-start.11 = (bf16[112,1024]{1,0:T(8,128)(2,1)S(1)}, bf16[112,1024]{1,0:T(8,128)(2,1)S(1)}, u32[]{:S(2)}, u32[]{:S(2)}) collective-permute-start(bf16[112,1024]{1,0:T(8,128)(2,1)S(1)} %shard_map.169), channel_id=1, source_target_pairs={{0,8},{8,0},{16,24},{24,16},{1,9},{9,1},{17,25},{25,17},{2,10},{10... | collective-permute-start | bytes 688136 | tf_op jit(solution)/shard_map/ppermute | solution.py:482
  44.1 7.0 %collective-permute-start.9 = (bf16[96,1024]{1,0:T(8,128)(2,1)S(1)}, bf16[96,1024]{1,0:T(8,128)(2,1)S(1)}, u32[]{:S(2)}, u32[]{:S(2)}) collective-permute-start(bf16[96,1024]{1,0:T(8,128)(2,1)S(1)} %shard_map.168), channel_id=1, source_target_pairs={{0,16},{8,24},{16,0},{24,8},{1,17},{9,25},{17,1},{25,9},{2,18},{10... | collective-permute-start | bytes 589832 | tf_op jit(solution)/shard_map/ppermute | solution.py:482
  45.1 6.4 %collective-permute-start.14 = (bf16[128,1024]{1,0:T(8,128)(2,1)S(1)}, bf16[128,1024]{1,0:T(8,128)(2,1)S(1)}, u32[]{:S(2)}, u32[]{:S(2)}) collective-permute-start(bf16[128,1024]{1,0:T(8,128)(2,1)S(1)} %bitcast.15), channel_id=1, source_target_pairs={{0,1},{1,0},{2,3},{3,2},{4,5},{5,4},{6,7},{7,6},{8,9},{9,8},{10,11... | collective-permute-start | bytes 786440 | tf_op jit(solution)/shard_map/ppermute | solution.py:486
  45.1 6.4 %collective-permute-start.15 = (bf16[128,1024]{1,0:T(8,128)(2,1)S(1)}, bf16[128,1024]{1,0:T(8,128)(2,1)S(1)}, u32[]{:S(2)}, u32[]{:S(2)}) collective-permute-start(bf16[128,1024]{1,0:T(8,128)(2,1)S(1)} %collective-permute-done.1.refs_5_.refs_2_), channel_id=1, source_target_pairs={{0,1},{1,0},{2,3},{3,2},{4,5},{5,4},{6,7},{7,6},{8,9},{9,8},{10,11... | collective-permute-start | bytes 786440 | tf_op jit(solution)/shard_map/ppermute | solution.py:486
  57.8 18.4 %collective-permute-start.16 = (bf16[256,1024]{1,0:T(8,128)(2,1)S(1)}, bf16[256,1024]{1,0:T(8,128)(2,1)S(1)}, u32[]{:S(2)}, u32[]{:S(2)}) collective-permute-start(bf16[256,1024]{1,0:T(8,128)(2,1)S(1)} %get-tuple-element.62), channel_id=1, source_target_pairs={{0,1},{1,0},{2,3},{3,2},{4,5},{5,4},{6,7},{7,6},{8,9},{9,8},{10,11... | collective-permute-start | bytes 1572872 | tf_op jit(solution)/shard_map/ppermute | solution.py:486
  58.6 8.4 %collective-permute-start.18 = (bf16[128,1024]{1,0:T(8,128)(2,1)S(1)}, bf16[128,1024]{1,0:T(8,128)(2,1)S(1)}, u32[]{:S(2)}, u32[]{:S(2)}) collective-permute-start(bf16[128,1024]{1,0:T(8,128)(2,1)S(1)} %shard_map.173), channel_id=1, source_target_pairs={{0,2},{1,3},{2,0},{3,1},{4,6},{5,7},{6,4},{7,5},{8,10},{9,11},{10,... | collective-permute-start | bytes 786440 | tf_op jit(solution)/shard_map/ppermute | solution.py:486
  67.5 8.4 %collective-permute-start.23 = (bf16[48,1024]{1,0:T(8,128)(2,1)S(1)}, bf16[48,1024]{1,0:T(8,128)(2,1)S(1)}, u32[]{:S(2)}, u32[]{:S(2)}) collective-permute-start(bf16[48,1024]{1,0:T(8,128)(2,1)S(1)} %get-tuple-element.77), channel_id=1, source_target_pairs={{0,4},{4,0},{1,5},{5,1},{2,6},{6,2},{3,7},{7,3},{8,12},{12,8},{9,1... | collective-permute-start | bytes 294920 | tf_op jit(solution)/shard_map/ppermute | solution.py:61
  72.3 5.3 %collective-permute-start.19 = (f32[2,56,128]{2,1,0:T(8,128)S(1)}, f32[2,56,128]{2,1,0:T(8,128)S(1)}, u32[]{:S(2)}, u32[]{:S(2)}) collective-permute-start(f32[2,56,128]{2,1,0:T(8,128)S(1)} %get-tuple-element.72), channel_id=1, source_target_pairs={{0,8},{8,0},{16,24},{24,16},{1,9},{9,1},{17,25},{25,17},{2,10},{10... | collective-permute-start | bytes 172040 | tf_op jit(solution)/shard_map/ppermute | solution.py:482
  73.5 4.2 %collective-permute-start.20 = (f32[2,56,128]{2,1,0:T(8,128)S(1)}, f32[2,56,128]{2,1,0:T(8,128)S(1)}, u32[]{:S(2)}, u32[]{:S(2)}) collective-permute-start(f32[2,56,128]{2,1,0:T(8,128)S(1)} %get-tuple-element.73), channel_id=1, source_target_pairs={{0,16},{8,24},{16,0},{24,8},{1,17},{9,25},{17,1},{25,9},{2,18},{10... | collective-permute-start | bytes 172040 | tf_op jit(solution)/shard_map/ppermute | solution.py:482
  74.1 5.1 %collective-permute-start.21 = (f32[2,56,128]{2,1,0:T(8,128)S(1)}, f32[2,56,128]{2,1,0:T(8,128)S(1)}, u32[]{:S(2)}, u32[]{:S(2)}) collective-permute-start(f32[2,56,128]{2,1,0:T(8,128)S(1)} %get-tuple-element.74), channel_id=1, source_target_pairs={{0,24},{8,16},{16,8},{24,0},{1,25},{9,17},{17,9},{25,1},{2,26},{10... | collective-permute-start | bytes 172040 | tf_op jit(solution)/shard_map/ppermute | solution.py:482
  76.1 4.1 %collective-permute-start.24 = (bf16[48,1024]{1,0:T(8,128)(2,1)S(1)}, bf16[48,1024]{1,0:T(8,128)(2,1)S(1)}, u32[]{:S(2)}, u32[]{:S(2)}) collective-permute-start(bf16[48,1024]{1,0:T(8,128)(2,1)S(1)} %get-tuple-element.79), channel_id=1, source_target_pairs={{0,1},{1,0},{2,3},{3,2},{4,5},{5,4},{6,7},{7,6},{8,9},{9,8},{10,11... | collective-permute-start | bytes 294920 | tf_op jit(solution)/shard_map/ppermute | solution.py:75
  76.2 4.6 %collective-permute-start.25 = (bf16[48,1024]{1,0:T(8,128)(2,1)S(1)}, bf16[48,1024]{1,0:T(8,128)(2,1)S(1)}, u32[]{:S(2)}, u32[]{:S(2)}) collective-permute-start(bf16[48,1024]{1,0:T(8,128)(2,1)S(1)} %get-tuple-element.80), channel_id=1, source_target_pairs={{1,2},{2,1},{3,0},{0,3},{5,6},{6,5},{7,4},{4,7},{9,10},{10,9},{11,... | collective-permute-start | bytes 294920 | tf_op jit(solution)/shard_map/ppermute | solution.py:75
  79.2 10.2 %collective-permute-start.22 = (bf16[128,1024]{1,0:T(8,128)(2,1)S(1)}, bf16[128,1024]{1,0:T(8,128)(2,1)S(1)}, u32[]{:S(2)}, u32[]{:S(2)}) collective-permute-start(bf16[128,1024]{1,0:T(8,128)(2,1)S(1)} %shard_map.172), channel_id=1, source_target_pairs={{0,2},{1,3},{2,0},{3,1},{4,6},{5,7},{6,4},{7,5},{8,10},{9,11},{10,... | collective-permute-start | bytes 786440 | tf_op jit(solution)/shard_map/ppermute | solution.py:486
  82.6 6.4 %collective-permute-start.27 = (f32[2,56,128]{2,1,0:T(8,128)S(1)}, f32[2,56,128]{2,1,0:T(8,128)S(1)}, u32[]{:S(2)}, u32[]{:S(2)}) collective-permute-start(f32[2,56,128]{2,1,0:T(8,128)S(1)} %shard_map.180.refs_0_), channel_id=1, source_target_pairs={{0,4},{1,5},{2,6},{3,7},{4,0},{5,1},{6,2},{7,3},{8,12},{9,13},{10,... | collective-permute-start | bytes 172040 | tf_op jit(solution)/shard_map/ppermute | solution.py:486
  89.0 4.2 %collective-permute-start.28 = (f32[2,56,128]{2,1,0:T(8,128)S(1)}, f32[2,56,128]{2,1,0:T(8,128)S(1)}, u32[]{:S(2)}, u32[]{:S(2)}) collective-permute-start(f32[2,56,128]{2,1,0:T(8,128)S(1)} %shard_map.181.refs_0_), channel_id=1, source_target_pairs={{0,2},{1,3},{2,0},{3,1},{4,6},{5,7},{6,4},{7,5},{8,10},{9,11},{10,... | collective-permute-start | bytes 172040 | tf_op jit(solution)/shard_map/ppermute | solution.py:486
  (9 other events, 101.0 us)

commit v4 on v3

--- a/solution.py
+++ b/solution.py
@@ -123,12 +123,8 @@
     )
 
 
-def fill_padded(padded, edge, field_ref, band_refs, side_refs, rows, cols):
+def fill_middle(padded, field_ref, band_refs, rows, cols):
     width = field_ref.shape[1]
-    tall = rows + 2 * MARGIN
-    _, col = grid_place()
-    even = col % 2 == 0
-    inner = (col > 0) & (col < GX - 1)
     for tile in range(width // LANES):
         above, below = above_below(band_refs, tile)
         for row in range(MARGIN):
@@ -139,13 +135,40 @@
             padded[tile, pl.ds((MARGIN + row) * PITCH + INSET, cols)] = field_ref[
                 row * cols : (row + 1) * cols, lane_tile(tile)
             ].astype(F32)
-        first = side_refs[0][:, lane_tile(tile)].astype(F32)
-        second = jnp.where(inner, side_refs[1][:, lane_tile(tile)].astype(F32), 0.0)
-        edge[0] = jnp.where(even, second, first)
-        edge[1] = jnp.where(even, first, second)
-        for row in range(tall):
-            padded[tile, pl.ds(row * PITCH + INSET - MARGIN, MARGIN)] = edge[0, pl.ds(row * MARGIN, MARGIN)]
-            padded[tile, pl.ds(row * PITCH + INSET + cols, MARGIN)] = edge[1, pl.ds(row * MARGIN, MARGIN)]
+        for row in range(rows + 2 * MARGIN):
+            padded[tile, pl.ds(row * PITCH, INSET)] = jnp.zeros((INSET, LANES), F32)
+            padded[tile, pl.ds(row * PITCH + INSET + cols, INSET)] = jnp.zeros((INSET, LANES), F32)
+
+
+def left_right(edge, side_refs, lanes):
+    _, col = grid_place()
+    even = col % 2 == 0
+    inner = (col > 0) & (col < GX - 1)
+    first = side_refs[0][:, lanes].astype(F32)
+    second = jnp.where(inner, side_refs[1][:, lanes].astype(F32), 0.0)
+    edge[0] = jnp.where(even, second, first)
+    edge[1] = jnp.where(even, first, second)
+
+
+def side_sums(left, right, edge, taps, near, far, rows, cols, flipped):
+    for row in range(rows + 2 * MARGIN):
+        left[pl.ds(row * cols, MARGIN)] = edge[0, pl.ds(row * MARGIN, MARGIN)]
+        start = row * cols + cols + MARGIN - 8
+        right[pl.ds(start, MARGIN)] = edge[1, pl.ds(row * MARGIN, MARGIN)]
+    for side, sums, shifts in ((left, near, range(MARGIN)), (right, far, range(KS - MARGIN, KS))):
+        for b in shifts:
+            for r in range(rows + 2 * MARGIN):
+                pixels = side[pl.ds(r * cols + b, 8)]
+                for a in range(KS):
+                    if 0 <= r - a < rows:
+                        index = (KS - 1 - a) * KS + KS - 1 - b if flipped else a * KS + b
+                        sums[r - a] = sums[r - a] + taps[index] * pixels
+    return near, far
+
+
+def side_scratch(sides, rows, cols):
+    tall = rows + 2 * MARGIN
+    return [pltpu.VMEM((tall * cols + 8, LANES), F32)] * 2 + [pltpu.VMEM((2, sides[0].shape[0], LANES), F32)]
 
 
 def window(padded, tile, row, shift, cols):
@@ -163,17 +186,14 @@
     return sums
 
 
-def forward(field, bands, sides, params, rows, cols):
+def forward_middle(field, bands, params, rows, cols):
     pixels, width = field.shape
     tiles = width // LANES
     span = (rows + 2 * MARGIN) * PITCH
 
     def body(*refs):
-        field_ref = refs[0]
-        band_refs = refs[1 : 1 + len(bands)]
-        side_refs = refs[1 + len(bands) : 3 + len(bands)]
-        params_ref, acts, standard, inverse, padded, edge = refs[3 + len(bands) :]
-        fill_padded(padded, edge, field_ref, band_refs, side_refs, rows, cols)
+        field_ref, band_refs, (params_ref, padded, out) = refs[0], refs[1:-3], refs[-3:]
+        fill_middle(padded, field_ref, band_refs, rows, cols)
 
         @pl.loop(0, tiles)
         def _(tile):
@@ -181,7 +201,38 @@
             start = jnp.broadcast_to(params_ref[tile, pl.ds(KS * KS, 1), :], (cols, LANES))
             sums = tap_sums(padded, tile, taps, [start] * rows, rows, cols, False)
             for row in range(rows):
-                standard[tile, pl.ds(row * cols, cols), :] = sums[row]
+                out[tile, pl.ds(row * cols, cols), :] = sums[row]
+
+    return call(
+        body,
+        [shape((tiles, span, LANES), F32), shape((tiles, pixels, LANES), F32)],
+        [],
+        [field, *bands, params],
+        size=8000000,
+        limit=16,
+    )
+
+
+def forward_end(partial, sides, params, rows, cols):
+    tiles, pixels, _ = partial.shape
+    width = tiles * LANES
+
+    def body(partial_ref, first_ref, second_ref, params_ref, acts, standard, inverse, left, right, edge):
+        left[...] = jnp.zeros_like(left)
+        right[...] = jnp.zeros_like(right)
+
+        @pl.loop(0, tiles)
+        def _(tile):
+            left_right(edge, (first_ref, second_ref), pl.ds(pl.multiple_of(tile * LANES, LANES), LANES))
+            taps = [params_ref[tile, pl.ds(t, 1), :] for t in range(KS * KS)]
+            near = [partial_ref[tile, pl.ds(row * cols, 8), :] for row in range(rows)]
+            far = [partial_ref[tile, pl.ds((row + 1) * cols - 8, 8), :] for row in range(rows)]
+            if cols > 16:
+                standard[tile] = partial_ref[tile]
+            near, far = side_sums(left, right, edge, taps, near, far, rows, cols, False)
+            for row in range(rows):
+                standard[tile, pl.ds(row * cols, 8), :] = near[row]
+                standard[tile, pl.ds((row + 1) * cols - 8, 8), :] = far[row]
 
         total = standard[0]
         for tile in range(1, tiles):
@@ -206,13 +257,34 @@
             shape((pixels, width), BF16),
             shape((tiles, pixels, LANES), F32),
             shape((pixels, LANES), F32),
-            shape((tiles, span, LANES), F32),
         ],
+        side_scratch(sides, rows, cols),
+        [partial, *sides, params],
+        size=6000000,
+        limit=8,
+    )
+
+
+def with_sides(padded, sides, rows, cols):
+    tiles = padded.shape[0]
+
+    def body(padded_ref, first_ref, second_ref, out, edge):
+        for tile in range(tiles):
+            out[tile] = padded_ref[tile]
+            left_right(edge, (first_ref, second_ref), lane_tile(tile))
+            for row in range(rows + 2 * MARGIN):
+                here = pl.ds(row * MARGIN, MARGIN)
+                out[tile, pl.ds(row * PITCH + INSET - MARGIN, MARGIN)] = edge[0, here]
+                out[tile, pl.ds(row * PITCH + INSET + cols, MARGIN)] = edge[1, here]
+
+    return call(
+        body,
+        [shape(padded.shape, F32)],
         [pltpu.VMEM((2, sides[0].shape[0], LANES), F32)],
-        [field, *bands, *sides, params],
-        size=10701000,
-        limit=16,
-    )
+        [padded, *sides],
+        size=2000000,
+        limit=8,
+    )[0]
 
 
 def arrays_of(shards):
@@ -228,96 +300,163 @@
     return arrays, slots
 
 
-def hidden_values(normed, upstream, params, shards, units):
+def hidden_scratch(rows, units, width):
+    return [
+        pltpu.VMEM((rows, width), BF16),
+        pltpu.VMEM((rows, width), BF16),
+        pltpu.VMEM((rows, units), F32),
+        pltpu.VMEM((rows, units), F32),
+        pltpu.VMEM((rows, units), BF16),
+    ]
+
+
+def weight_scratch(units, width):
+    return [pltpu.VMEM((units, width), BF16), pltpu.VMEM((units, width), BF16)]
+
+
+def place_rows(norm, back, normed_refs, up_refs, starts, params_ref):
+    pixels = normed_refs[0].shape[0]
+    for index, start in enumerate(starts):
+        here = slice(index * pixels, (index + 1) * pixels)
+        norm[here] = normed_refs[index][...]
+        for tile in range(norm.shape[1] // LANES):
+            lanes = lane_tile(tile)
+            layer = params_ref[tile, KS * KS + 3 : KS * KS + 4, :]
+            rows = up_refs[index][start : start + pixels, lanes]
+            back[here, lanes] = (rows.astype(F32) * layer).astype(BF16)
+
+
+def place_weights(win, wout, shard_refs, slots, units):
+    for index, (rows_in, rows_out, _) in enumerate(slots):
+        here = slice(index * units, (index + 1) * units)
+        win[here] = shard_refs[rows_in[0]][rows_in[1] : rows_in[1] + units]
+        wout[here] = shard_refs[rows_out[0]][rows_out[1] : rows_out[1] + units]
+    lines = [shard_refs[bias[0]][bias[1] : bias[1] + 1, :units].astype(F32) for *_, bias in slots]
+    return lines[0] if len(lines) == 1 else jnp.concatenate(lines, axis=1)
+
+
+def hidden_block(norm, back, win, wout, line, hid, pre, slope, bpre):
+    step = 32
+    across = (((1,), (1,)), ((), ()))
+    pre[...] = lax.dot_general(norm[...], win[...], across, preferred_element_type=F32) + line
+    slope[...] = lax.dot_general(back[...], wout[...], across, preferred_element_type=F32)
+
+    @pl.loop(0, norm.shape[0] // step)
+    def _(part):
+        here = pl.ds(pl.multiple_of(part * step, step), step)
+        value = pre[here, :]
+        half = 0.5 * (1.0 + lax.erf(value * 0.7071067811865476))
+        hid[here, :] = (value * half).astype(BF16)
+        bell = jnp.exp(-0.5 * value * value) * 0.3989422804014327
+        bpre[here, :] = (slope[here, :] * (half + value * bell)).astype(BF16)
+
+    return jnp.dot(bpre[...], win[...], preferred_element_type=F32)
+
+
+def hidden_near(normed, upstream, params, shards, units):
+    pixels, width = normed[0].shape
+    arrays, slots = arrays_of(shards)
+    members, count, every = len(normed), len(arrays), len(shards) * units
+    rows = members * pixels
+
+    def body(*refs):
+        normed_refs, up_refs, params_ref = refs[:members], refs[members : 2 * members], refs[2 * members]
+        shard_refs, rest = refs[2 * members + 1 : 2 * members + 1 + count], refs[2 * members + 1 + count :]
+        hid, total, win, wout, norm, back, pre, slope, bpre = rest
+        place_rows(norm, back, normed_refs, up_refs, [start for _, start in upstream], params_ref)
+        line = place_weights(win, wout, shard_refs, slots, units)
+        total[...] = hidden_block(norm, back, win, wout, line, hid, pre, slope, bpre)
+
+    return call(
+        body,
+        [shape((rows, every), BF16), shape((rows, width), F32)],
+        weight_scratch(every, width) + hidden_scratch(rows, every, width),
+        [*normed, *[array for array, _ in upstream], params, *arrays],
+        size=7000000,
+        limit=20,
+    )
+
+
+def hidden_far(normed, upstream, params, shards, early, near_sum, units):
     pixels, width = normed[0].shape
     arrays, slots = arrays_of(shards)
     members, count = len(normed), len(arrays)
-    total, kept = members * pixels, members * pixels // 2
-    tiles = width // LANES
-    every = len(shards) * units
-    step = 32
+    half = members // 2
+    rows, every, late = half * pixels, len(shards) * units, (len(shards) - early) * units
 
     def body(*refs):
         normed_refs, up_refs, params_ref = refs[:members], refs[members : 2 * members], refs[2 * members]
         shard_refs, rest = refs[2 * members + 1 : 2 * members + 1 + count], refs[2 * members + 1 + count :]
-        hid, stay, send, norm, back, win, wout, pre, slope, bpre = rest
-        for index in range(members):
-            here = slice(index * pixels, (index + 1) * pixels)
-            norm[here] = normed_refs[index][...]
-            for tile in range(tiles):
-                lanes = lane_tile(tile)
-                layer = params_ref[tile, KS * KS + 3 : KS * KS + 4, :]
-                back[here, lanes] = (up_refs[index][:, lanes].astype(F32) * layer).astype(BF16)
-        for index, (rows_in, rows_out, _) in enumerate(slots):
-            here = slice(index * units, (index + 1) * units)
-            win[here] = shard_refs[rows_in[0]][rows_in[1] : rows_in[1] + units]
-            wout[here] = shard_refs[rows_out[0]][rows_out[1] : rows_out[1] + units]
-        row = jnp.concatenate(
-            [shard_refs[bias[0]][bias[1] : bias[1] + 1, :units].astype(F32) for *_, bias in slots], axis=1
+        sum_ref, near_hid, far_hid, stay, send = rest[:5]
+        win, wout, late_in, late_out = rest[5:9]
+        near_norm, near_back, near_pre, near_slope, near_bpre = rest[9:14]
+        norm, back, pre, slope, bpre = rest[14:]
+        starts = [start for _, start in upstream]
+        place_rows(near_norm, near_back, normed_refs[:half], up_refs[:half], starts[:half], params_ref)
+        place_rows(norm, back, normed_refs[half:], up_refs[half:], starts[half:], params_ref)
+        line = place_weights(win, wout, shard_refs, slots, units)
+        late_line = place_weights(late_in, late_out, shard_refs, slots[early:], units)
+        far = hidden_block(norm, back, win, wout, line, far_hid, pre, slope, bpre)
+        near = sum_ref[...] + hidden_block(
+            near_norm, near_back, late_in, late_out, late_line, near_hid, near_pre, near_slope, near_bpre
         )
-        across = (((1,), (1,)), ((), ()))
-        pre[...] = lax.dot_general(norm[...], win[...], across, preferred_element_type=F32) + row
-        slope[...] = lax.dot_general(back[...], wout[...], across, preferred_element_type=F32)
-
-        @pl.loop(0, total // step)
-        def _(part):
-            here = pl.ds(pl.multiple_of(part * step, step), step)
-            value = pre[here, :]
-            half = 0.5 * (1.0 + lax.erf(value * 0.7071067811865476))
-            hid[here, :] = (value * half).astype(BF16)
-            bell = jnp.exp(-0.5 * value * value) * 0.3989422804014327
-            bpre[here, :] = (slope[here, :] * (half + value * bell)).astype(BF16)
-
-        back_normed = jnp.dot(bpre[...], win[...], preferred_element_type=F32)
-        stay[...] = back_normed[:kept]
-        send[...] = back_normed[kept:].astype(BF16)
-
-    return call(
-        body,
-        [shape((total, every), BF16), shape((kept, width), F32), shape((kept, width), BF16)],
+        stay[:pixels] = near[:pixels]
+        stay[pixels:] = far[:pixels]
+        send[:pixels] = near[pixels:].astype(BF16)
+        send[pixels:] = far[pixels:].astype(BF16)
+
+    return call(
+        body,
         [
-            pltpu.VMEM((total, width), BF16),
-            pltpu.VMEM((total, width), BF16),
-            pltpu.VMEM((every, width), BF16),
-            pltpu.VMEM((every, width), BF16),
-            pltpu.VMEM((total, every), F32),
-            pltpu.VMEM((total, every), F32),
-            pltpu.VMEM((total, every), BF16),
+            shape((rows, late), BF16),
+            shape((rows, every), BF16),
+            shape((rows, width), F32),
+            shape((rows, width), BF16),
         ],
-        [*normed, *upstream, params, *arrays],
-        size=13653000,
+        weight_scratch(every, width)
+        + weight_scratch(late, width)
+        + hidden_scratch(rows, late, width)
+        + hidden_scratch(rows, every, width),
+        [*normed, *[array for array, _ in upstream], params, *arrays, near_sum],
+        size=9000000,
         limit=28,
     )
 
 
-def project(hidden, upstream, shards, units):
-    pixels, width = upstream[0].shape
+def project(hiddens, upstream, shards, units):
+    pixels, width = upstream[0][0].shape[0], upstream[0][0].shape[1]
     arrays, slots = arrays_of([[rows_out] for _, rows_out, _ in shards])
-    members, count = len(upstream), len(arrays)
-    total, kept = members * pixels, members * pixels // 2
-    tiles = width // LANES
-
-    def body(*refs):
-        hidden_ref, up_refs, shard_refs = refs[0], refs[1 : 1 + members], refs[1 + members : 1 + members + count]
-        stay, send, scale, wout = refs[1 + members + count :]
+    members, count, every = len(upstream), len(arrays), len(shards) * units
+    half = members // 2 * pixels
+    early, late, _ = hiddens
+
+    def body(early_ref, late_ref, far_ref, *refs):
+        up_refs, shard_refs = refs[:members], refs[members : members + count]
+        stay, send, scale, wout, hid = refs[members + count :]
         for index, ((slot, start),) in enumerate(slots):
             wout[index * units : (index + 1) * units] = shard_refs[slot][start : start + units]
-        projected = jnp.dot(hidden_ref[...], wout[...], preferred_element_type=F32)
-        stay[...] = projected[:kept]
-        send[...] = projected[kept:].astype(BF16)
-        for tile in range(tiles):
+        hid[:half, : early.shape[1]] = early_ref[...]
+        hid[:half, early.shape[1] :] = late_ref[...]
+        hid[half:] = far_ref[...]
+        projected = jnp.dot(hid[...], wout[...], preferred_element_type=F32)
+        stay[:pixels] = projected[:pixels]
+        stay[pixels:] = projected[half : half + pixels]
+        send[:pixels] = projected[pixels:half].astype(BF16)
+        send[pixels:] = projected[half + pixels :].astype(BF16)
+        for tile in range(width // LANES):
             lanes = lane_tile(tile)
             sums = jnp.zeros((pixels, LANES), F32)
             for index in range(members):
                 rows = projected[index * pixels : (index + 1) * pixels, lanes]
-                sums = sums + up_refs[index][:, lanes].astype(F32) * rows
+                start = upstream[index][1]
+                sums = sums + up_refs[index][start : start + pixels, lanes].astype(F32) * rows
             scale[tile] = jnp.broadcast_to(jnp.sum(sums, axis=0, keepdims=True), (8, LANES))
 
     return call(
         body,
-        [shape((kept, width), F32), shape((kept, width), BF16), shape((tiles, 8, LANES), F32)],
-        [pltpu.VMEM((len(shards) * units, width), BF16)],
-        [hidden, *upstream, *arrays],
+        [shape((half, width), F32), shape((half, width), BF16), shape((width // LANES, 8, LANES), F32)],
+        [pltpu.VMEM((every, width), BF16), pltpu.VMEM((2 * half, every), BF16)],
+        [*hiddens, *[array for array, _ in upstream], *arrays],
         size=3911400,
         limit=20,
     )
@@ -446,17 +585,14 @@
     )
 
 
-def input_gradient(wire, bands, sides, params, upstream, rows, cols):
+def gradient_middle(wire, bands, params, upstream, rows, cols):
     pixels, width = wire.shape
     tiles = width // LANES
     span = (rows + 2 * MARGIN) * PITCH
 
     def body(*refs):
-        wire_ref = refs[0]
-        band_refs = refs[1 : 1 + len(bands)]
-        side_refs = refs[1 + len(bands) : 3 + len(bands)]
-        params_ref, up_ref, out, padded, edge = refs[3 + len(bands) :]
-        fill_padded(padded, edge, wire_ref, band_refs, side_refs, rows, cols)
+        wire_ref, band_refs, (params_ref, up_ref, out, padded) = refs[0], refs[1:-4], refs[-4:]
+        fill_middle(padded, wire_ref, band_refs, rows, cols)
 
         @pl.loop(0, tiles)
         def _(tile):
@@ -465,15 +601,45 @@
             start = [up_ref[pl.ds(row * cols, cols), lanes].astype(F32) for row in range(rows)]
             sums = tap_sums(padded, tile, taps, start, rows, cols, True)
             for row in range(rows):
-                out[pl.ds(row * cols, cols), lanes] = sums[row].astype(BF16)
-
-    return call(
-        body,
-        [shape((pixels, width), BF16)],
-        [pltpu.VMEM((tiles, span, LANES), F32), pltpu.VMEM((2, sides[0].shape[0], LANES), F32)],
-        [wire, *bands, *sides, params, upstream],
-        size=12177000,
+                out[tile, pl.ds(row * cols, cols), :] = sums[row]
+
+    return call(
+        body,
+        [shape((tiles, pixels, LANES), F32)],
+        [pltpu.VMEM((tiles, span, LANES), F32)],
+        [wire, *bands, params, upstream],
+        size=8000000,
         limit=16,
+    )[0]
+
+
+def gradient_end(partial, sides, params, rows, cols):
+    tiles, pixels, _ = partial.shape
+
+    def body(partial_ref, first_ref, second_ref, params_ref, out, left, right, edge):
+        left[...] = jnp.zeros_like(left)
+        right[...] = jnp.zeros_like(right)
+
+        @pl.loop(0, tiles)
+        def _(tile):
+            lanes = pl.ds(pl.multiple_of(tile * LANES, LANES), LANES)
+            left_right(edge, (first_ref, second_ref), lanes)
+            taps = [params_ref[tile, pl.ds(t, 1), :] for t in range(KS * KS)]
+            near = [partial_ref[tile, pl.ds(row * cols, 8), :] for row in range(rows)]
+            far = [partial_ref[tile, pl.ds((row + 1) * cols - 8, 8), :] for row in range(rows)]
+            near, far = side_sums(left, right, edge, taps, near, far, rows, cols, True)
+            for row in range(rows):
+                middle = partial_ref[tile, pl.ds(row * cols + 8, cols - 16), :] if cols > 16 else None
+                whole = [near[row]] + ([middle] if cols > 16 else []) + [far[row]]
+                out[pl.ds(row * cols, cols), lanes] = jnp.concatenate(whole).astype(BF16)
+
+    return call(
+        body,
+        [shape((pixels, tiles * LANES), BF16)],
+        side_scratch(sides, rows, cols),
+        [partial, *sides, params],
+        size=5000000,
+        limit=8,
     )[0]
 
 
@@ -724,38 +890,56 @@
         units = shards[0].shape[0] // 2 - BIAS_ROWS // 2
         shards = [[(shards[0], 0, units), (shards[0], units, units), (shards[0], 2 * units, BIAS_ROWS)]]
     sides = swap_cols(border_columns(field, bands, rows, cols))
-    acts, standard, inverse, padded = forward(field, bands, sides, params, rows, cols)
-    far_acts = tile_swap(acts, 2)
+    padded, partial = forward_middle(field, bands, params, rows, cols)
+    acts, standard, inverse = forward_end(partial, sides, params, rows, cols)
+    padded = with_sides(padded, sides, rows, cols)
+    near_acts, far_acts = tile_swap(acts, 1), tile_swap(acts, 2)
+    near_upstream = tile_swap(upstream, 1)
+    early = max(1, len(shards) - 1)
     if by_permutes:
-        far_acts = after(far_acts, far_in, far_out)
-    normed = [acts, far_acts, tile_swap(acts, 1), tile_swap(far_acts, 1)]
-    upstreams = [upstream, far_upstream, tile_swap(upstream, 1), tile_swap(far_upstream, 1)]
-    hidden, back_own, back_send = hidden_values(normed, upstreams, params, shards, units)
+        chip = [(upstream, 0), (near_upstream, 0)]
+        near_hidden, near_sum = hidden_near([acts, near_acts], chip, params, shards[:early], units)
+        far_acts = after(far_acts, far_in, far_out, padded, near_sum)
+    else:
+        half = units // 2
+        cuts = [[(array, first + at, half) for array, first, _ in shards[0][:2]] for at in (0, half)]
+        bias, row, _ = shards[0][2]
+        lines = [jnp.pad(bias[row : row + 1, at : at + half], ((0, 0), (0, 0))) for at in (0, half)]
+        shards = [[*cut, (line, 0, 1)] for cut, line in zip(cuts, lines)]
+        units = half
+        chip = [(upstream, 0), (near_upstream, 0)]
+        near_hidden, near_sum = hidden_near([acts, near_acts], chip, params, shards[:early], units)
+    normed = [acts, near_acts, far_acts, tile_swap(far_acts, 1)]
+    upstreams = [*chip, (far_upstream, 0), (tile_swap(far_upstream, 1), 0)]
+    late_hidden, far_hidden, back_own, back_send = hidden_far(
+        normed, upstreams, params, shards, early, near_sum, units
+    )
+    hiddens = [near_hidden, late_hidden, far_hidden]
 
     def group_sum(mine, theirs, *others):
         peer = tile_swap(theirs, 1)
         return mine, peer, tile_swap(after(pair_sum(mine, peer), *others), 2)
 
     back_sums = group_sum(back_own, back_send)
-    out_own, out_send, scale_part = project(hidden, upstreams, shards, units)
+    out_own, out_send, scale_part = project(hiddens, upstreams, shards, units)
     back_conv, wire, vector_parts, *back_sends = norm_backward(
         *back_sums, standard, inverse, params, upstream, rows, cols
     )
     parts = kernel_gradient(
         padded, back_conv, vector_parts, scale_part, rows, cols, groups if by_permutes else 1
     )
-    back_bands = swap_rows(back_sends)
-    back_bands[0] = after(back_bands[0], parts[0])
+    back_bands = swap_rows([after(send, parts[0]) for send in back_sends])
     back_sides = swap_cols(border_columns(wire, back_bands, rows, cols))
-    grad = input_gradient(wire, back_bands, back_sides, params, upstream, rows, cols)
+    middle = gradient_middle(wire, back_bands, params, upstream, rows, cols)
+    grad = gradient_end(middle, back_sides, params, rows, cols)
     factor = 1.0 / math.sqrt(image_count * groups * count * pixels)
     if by_permutes:
         total = add_blocks([parts[0]] + [across(parts[bits], bits) for bits in range(1, groups)])
         block = block_output(*group_sum(out_own, out_send, total), params, field)
-        total = after(total, *back_sides)
+        total = after(total, *back_bands)
         total = add_blocks([total, tile_swap(total, 1)])
-        total = after(add_blocks([total, tile_swap(total, 4)]), grad)
-        sums = finish(after(total, block), [tile_swap(total, 2)], factor)
+        total = after(add_blocks([total, tile_swap(total, 4)]), middle, *back_sides)
+        sums = finish(after(total, block, grad), [tile_swap(total, 2)], factor)
     else:
         block = block_output(*group_sum(out_own, out_send), params, field)
         sums = sum_params(parts[0], factor)

time: 94.1 us -> 91 us (0.967)
  waiting for transfers between devices: 44.9 us -> 31.5 us
  starting transfers between devices: 29.7 us -> 35.8 us
  Pallas kernels: 18.5 us -> 22 us
    ppermute x14, waiting for transfers between devices: 32.9 us -> 22.4 us  [tile_swap(): lax.ppermute(block, 'tile', [(i, i ^ bits) for i in range(lax.axis_size('...]
    ppermute x14, starting transfers between devices: 12.1 us -> 17.3 us  [tile_swap(): lax.ppermute(block, 'tile', [(i, i ^ bits) for i in range(lax.axis_size('...]
    pallas_call x20 -> x24, Pallas kernels: 15.6 us -> 19.1 us  [call(): pl.pallas_call(body, out_shape=outs, in_specs=[VMEM] * len(args), out_spe...]
    ppermute x4, waiting for transfers between devices: 4.21 us -> 1.02 us  [swap_cols(): moved.append(lax.ppermute(block, 'tile', route))]
  transfers between devices with their start and end apart: 29 -> 29, of which waited for: 17 -> 13; matrix products, arithmetic and copies ran while one was open for 0% -> 0% of each run, Pallas kernels for 12% -> 17%
where the time goes in v4:
time: 91 us; the launch traced here: 90.8 us
  starting transfers between devices  35.8 us (39%)
  waiting for transfers between devices  31.5 us (35%)
  Pallas kernels  22 us (24%)
    ppermute x14, waiting for transfers between devices, tile_swap(): lax.ppermute(block, 'tile', [(i, i ^ bits) for i in range(lax.axis_size('...  22.4 us
    pallas_call x24, Pallas kernels, call(): pl.pallas_call(body, out_shape=outs, in_specs=[VMEM] * len(args), out_spe...  19.1 us
    ppermute x14, starting transfers between devices, tile_swap(): lax.ppermute(block, 'tile', [(i, i ^ bits) for i in range(lax.axis_size('...  17.3 us
    ppermute x10, starting transfers between devices, across(): return lax.ppermute(block, 'dp', [(i, i ^ bits) for i in range(groups)])  12.8 us
    ppermute x10, waiting for transfers between devices, across(): return lax.ppermute(block, 'dp', [(i, i ^ bits) for i in range(groups)])  7.46 us
    pallas_call x1, Pallas kernels, first_sends(): pl.pallas_call(body, out_shape=outs, in_specs=[VMEM] + [far] * (len(args)...  2.92 us
    ppermute x1, starting transfers between devices, swap_rows(): moved.append(lax.ppermute(block, 'tile', route))  2.83 us
    ppermute x4, starting transfers between devices, swap_cols(): moved.append(lax.ppermute(block, 'tile', route))  2.82 us
  transfers between devices with their start and end apart: 29, of which 13 were waited for; matrix products, arithmetic and copies ran while one was open for 0% of the time, Pallas kernels for 17%

profile of v4, /device:TPU:0, one launch (start us, length us, event | category | flops | bytes accessed | tf_op | source)
XLA Modules:
  0.0 90.8 jit_solution(677917364157255294)
XLA Ops:
  0.7 2.9 %shard_map.162 = (bf16[224,1024]{1,0:T(8,128)(2,1)}, bf16[256,1024]{1,0:T(8,128)(2,1)}, f32[2,56,128]{2,1,0:T(8,128)}) custom-call(bf16[1,96]{1,0:T(2,128)(2,1)} %bitcast.32, bf16[128,1024]{1,0:T(8,128)(2,1)} %bitcast.21, bf16[96,1024]{1,0:T(8,128)(2,1)} %in_ref.1, bf16[96,1024]{1,0:T(8,128)(2,1)} %out_ref.1, f32[49,256]{1,0:T(8,128)} %kernel_ref.1, ...), custom_call_target="tpu_custom_call" | custom-call | flops 10000 | bytes 1000000 | tf_op jit(solution)/shard_map/pallas_call | solution.py:794
  3.6 4.1 %collective-permute-start = (bf16[256,1024]{1,0:T(8,128)(2,1)}, bf16[256,1024]{1,0:T(8,128)(2,1)S(1)}, u32[]{:S(2)}, u32[]{:S(2)}) collective-permute-start(bf16[256,1024]{1,0:T(8,128)(2,1)} %get-tuple-element.52), channel_id=1, source_target_pairs={{0,4},{1,5},{2,6},{3,7},{4,0},{5,1},{6,2},{7,3},{8,12},{9,13},{10,... | collective-permute-start | bytes 1572872 | tf_op jit(solution)/shard_map/ppermute | solution.py:652
  7.7 2.4 %collective-permute-start.4 = (bf16[224,1024]{1,0:T(8,128)(2,1)}, bf16[224,1024]{1,0:T(8,128)(2,1)S(1)}, u32[]{:S(2)}, u32[]{:S(2)}) collective-permute-start(bf16[224,1024]{1,0:T(8,128)(2,1)} %get-tuple-element.53.refs_5_.refs_9_.refs_4_), channel_id=1, source_target_pairs={{0,24},{8,16},{16,8},{24,0},{1,25},{9,17},{17,9},{25,1},{2,26},{10... | collective-permute-start | bytes 1376264 | tf_op jit(solution)/shard_map/ppermute | solution.py:648
  11.2 1.6 %collective-permute-start.1 = (bf16[128,1024]{1,0:T(8,128)(2,1)}, bf16[128,1024]{1,0:T(8,128)(2,1)S(1)}, u32[]{:S(2)}, u32[]{:S(2)}) collective-permute-start(bf16[128,1024]{1,0:T(8,128)(2,1)} %bitcast.14), channel_id=1, source_target_pairs={{0,2},{1,3},{2,0},{3,1},{4,6},{5,7},{6,4},{7,5},{8,10},{9,11},{10,... | collective-permute-start | bytes 786440 | tf_op jit(solution)/shard_map/ppermute | solution.py:652
  12.8 12.1 %collective-permute-done.1.refs_6_.refs_2_ = bf16[128,1024]{1,0:T(8,128)(2,1)S(1)} collective-permute-done((bf16[128,1024]{1,0:T(8,128)(2,1)}, bf16[128,1024]{1,0:T(8,128)(2,1)S(1)}, u32[]{:S(2)}, u32[]{:S(2)}) %collective-permute-start.1) | collective-permute-done | bytes 262176 | tf_op jit(solution)/shard_map/ppermute | solution.py:652
  24.9 5.8 %collective-permute-done.3.refs_1_.refs_7_.refs_11_.refs_6_ = bf16[224,1024]{1,0:T(8,128)(2,1)S(1)} collective-permute-done((bf16[224,1024]{1,0:T(8,128)(2,1)}, bf16[224,1024]{1,0:T(8,128)(2,1)S(1)}, u32[]{:S(2)}, u32[]{:S(2)}) %collective-permute-start.3) | collective-permute-done | bytes 458784 | tf_op jit(solution)/shard_map/ppermute | solution.py:648
  31.1 1.6 %collective-permute-start.10 = (bf16[208,1024]{1,0:T(8,128)(2,1)S(1)}, bf16[208,1024]{1,0:T(8,128)(2,1)S(1)}, u32[]{:S(2)}, u32[]{:S(2)}) collective-permute-start(bf16[208,1024]{1,0:T(8,128)(2,1)S(1)} %shard_map.168.refs_9_.refs_13_.refs_8_), channel_id=1, source_target_pairs={{0,16},{8,24},{16,0},{24,8},{1,17},{9,25},{17,1},{25,9},{2,18},{10... | collective-permute-start | bytes 1277960 | tf_op jit(solution)/shard_map/ppermute | solution.py:648
  32.7 1.5 %collective-permute-start.9 = (bf16[208,1024]{1,0:T(8,128)(2,1)S(1)}, bf16[208,1024]{1,0:T(8,128)(2,1)S(1)}, u32[]{:S(2)}, u32[]{:S(2)}) collective-permute-start(bf16[208,1024]{1,0:T(8,128)(2,1)S(1)} %shard_map.168.refs_9_.refs_13_.refs_8_), channel_id=1, source_target_pairs={{0,8},{8,0},{16,24},{24,16},{1,9},{9,1},{17,25},{25,17},{2,10},{10... | collective-permute-start | bytes 1277960 | tf_op jit(solution)/shard_map/ppermute | solution.py:648
  35.5 2.6 %shard_map.165 = (f32[8,448,128]{2,1,0:T(8,128)S(1)}, f32[8,128,128]{2,1,0:T(8,128)S(1)}) custom-call(bf16[128,1024]{1,0:T(8,128)(2,1)S(1)} %bitcast.23, bf16[48,1024]{1,0:T(8,128)(2,1)S(1)} %shard_map.163.refs_1_.refs_0_, f32[8,56,128]{2,1,0:T(8,128)S(1)} %shard_map.164.refs_2_.params_ref.refs_4_.refs_8_), custom_call_target="tpu_custom_call" | custom-call | bytes 8000000 | tf_op jit(solution)/shard_map/pallas_call | solution.py:26
  42.5 1.6 %collective-permute-start.13 = (bf16[112,1024]{1,0:T(8,128)(2,1)S(1)}, bf16[112,1024]{1,0:T(8,128)(2,1)S(1)}, u32[]{:S(2)}, u32[]{:S(2)}) collective-permute-start(bf16[112,1024]{1,0:T(8,128)(2,1)S(1)} %shard_map.171), channel_id=1, source_target_pairs={{0,8},{8,0},{16,24},{24,16},{1,9},{9,1},{17,25},{25,17},{2,10},{10... | collective-permute-start | bytes 688136 | tf_op jit(solution)/shard_map/ppermute | solution.py:648
  46.1 2.1 %shard_map.169 = (bf16[256,672]{1,0:T(8,128)(2,1)S(1)}, f32[256,1024]{1,0:T(8,128)S(1)}) custom-call(bf16[128,1024]{1,0:T(8,128)(2,1)S(1)} %get-tuple-element.62.refs_0_, bf16[128,1024]{1,0:T(8,128)(2,1)S(1)} %collective-permute-done.7.refs_1_, bf16[128,1024]{1,0:T(8,128)(2,1)S(1)} %bitcast.16, ...), custom_call_target="tpu_custom_call" | custom-call | bytes 7000000 | tf_op jit(solution)/shard_map/pallas_call | solution.py:26
  49.8 1.5 %collective-permute-done.14.refs_3_ = bf16[128,1024]{1,0:T(8,128)(2,1)S(1)} collective-permute-done((bf16[128,1024]{1,0:T(8,128)(2,1)S(1)}, bf16[128,1024]{1,0:T(8,128)(2,1)S(1)}, u32[]{:S(2)}, u32[]{:S(2)}) %collective-permute-start.14) | collective-permute-done | bytes 262176 | tf_op jit(solution)/shard_map/ppermute | solution.py:652
  51.3 3.0 %shard_map.173 = (bf16[256,96]{1,0:T(8,128)(2,1)S(1)}, bf16[256,768]{1,0:T(8,128)(2,1)S(1)}, f32[256,1024]{1,0:T(8,128)S(1)}, bf16[256,1024]{1,0:T(8,128)(2,1)S(1)}) custom-call(bf16[128,1024]{1,0:T(8,128)(2,1)S(1)} %get-tuple-element.62.refs_0_, bf16[128,1024]{1,0:T(8,128)(2,1)S(1)} %collective-permute-done.7.refs_1_, ...), custom_call_target="tpu_custom_call" | custom-call | bytes 9000000 | tf_op jit(solution)/shard_map/pallas_call | solution.py:26
  56.4 1.6 %collective-permute-start.18 = (bf16[128,1024]{1,0:T(8,128)(2,1)S(1)}, bf16[128,1024]{1,0:T(8,128)(2,1)S(1)}, u32[]{:S(2)}, u32[]{:S(2)}) collective-permute-start(bf16[128,1024]{1,0:T(8,128)(2,1)S(1)} %shard_map.176), channel_id=1, source_target_pairs={{0,2},{1,3},{2,0},{3,1},{4,6},{5,7},{6,4},{7,5},{8,10},{9,11},{10,... | collective-permute-start | bytes 786440 | tf_op jit(solution)/shard_map/ppermute | solution.py:652
  58.0 6.8 %collective-permute-done.18.far_ref = bf16[128,1024]{1,0:T(8,128)(2,1)S(1)} collective-permute-done((bf16[128,1024]{1,0:T(8,128)(2,1)S(1)}, bf16[128,1024]{1,0:T(8,128)(2,1)S(1)}, u32[]{:S(2)}, u32[]{:S(2)}) %collective-permute-start.18) | collective-permute-done | bytes 262176 | tf_op jit(solution)/shard_map/ppermute | solution.py:652
  65.3 2.0 %shard_map.178 = (f32[2,56,128]{2,1,0:T(8,128)S(1)}, f32[2,56,128]{2,1,0:T(8,128)S(1)}, f32[2,56,128]{2,1,0:T(8,128)S(1)}, f32[2,56,128]{2,1,0:T(8,128)S(1)}) custom-call(f32[8,448,128]{2,1,0:T(8,128)S(1)} %shard_map.172.padded_ref, f32[8,128,128]{2,1,0:T(8,128)S(1)} %get-tuple-element.76.conv, f32[8,8,128]{2,1,0:T(8,128)S(1)} %get-tuple-element.77.vectors_ref, ...), custom_call_target="tpu_custom_call" | custom-call | bytes 7380000 | tf_op jit(solution)/shard_map/pallas_call | solution.py:26
  68.0 1.4 %collective-permute-start.20 = (f32[2,56,128]{2,1,0:T(8,128)S(1)}, f32[2,56,128]{2,1,0:T(8,128)S(1)}, u32[]{:S(2)}, u32[]{:S(2)}) collective-permute-start(f32[2,56,128]{2,1,0:T(8,128)S(1)} %get-tuple-element.81), channel_id=1, source_target_pairs={{0,16},{8,24},{16,0},{24,8},{1,17},{9,25},{17,1},{25,9},{2,18},{10... | collective-permute-start | bytes 172040 | tf_op jit(solution)/shard_map/ppermute | solution.py:648
  69.4 1.4 %collective-permute-start.21 = (f32[2,56,128]{2,1,0:T(8,128)S(1)}, f32[2,56,128]{2,1,0:T(8,128)S(1)}, u32[]{:S(2)}, u32[]{:S(2)}) collective-permute-start(f32[2,56,128]{2,1,0:T(8,128)S(1)} %get-tuple-element.82), channel_id=1, source_target_pairs={{0,24},{8,16},{16,8},{24,0},{1,25},{9,17},{17,9},{25,1},{2,26},{10... | collective-permute-start | bytes 172040 | tf_op jit(solution)/shard_map/ppermute | solution.py:648
  70.8 2.8 %collective-permute-start.23 = (bf16[48,1024]{1,0:T(8,128)(2,1)S(1)}, bf16[48,1024]{1,0:T(8,128)(2,1)S(1)}, u32[]{:S(2)}, u32[]{:S(2)}) collective-permute-start(bf16[48,1024]{1,0:T(8,128)(2,1)S(1)} %get-tuple-element.86), channel_id=1, source_target_pairs={{0,4},{4,0},{1,5},{5,1},{2,6},{6,2},{3,7},{7,3},{8,12},{12,8},{9,1... | collective-permute-start | bytes 294920 | tf_op jit(solution)/shard_map/ppermute | solution.py:61
  74.5 1.7 %collective-permute-start.22 = (bf16[128,1024]{1,0:T(8,128)(2,1)S(1)}, bf16[128,1024]{1,0:T(8,128)(2,1)S(1)}, u32[]{:S(2)}, u32[]{:S(2)}) collective-permute-start(bf16[128,1024]{1,0:T(8,128)(2,1)S(1)} %shard_map.175), channel_id=1, source_target_pairs={{0,2},{1,3},{2,0},{3,1},{4,6},{5,7},{6,4},{7,5},{8,10},{9,11},{10,... | collective-permute-start | bytes 786440 | tf_op jit(solution)/shard_map/ppermute | solution.py:652
  78.9 3.6 %collective-permute-start.27 = (f32[2,56,128]{2,1,0:T(8,128)S(1)}, f32[2,56,128]{2,1,0:T(8,128)S(1)}, u32[]{:S(2)}, u32[]{:S(2)}) collective-permute-start(f32[2,56,128]{2,1,0:T(8,128)S(1)} %shard_map.184.refs_0_), channel_id=1, source_target_pairs={{0,4},{1,5},{2,6},{3,7},{4,0},{5,1},{6,2},{7,3},{8,12},{9,13},{10,... | collective-permute-start | bytes 172040 | tf_op jit(solution)/shard_map/ppermute | solution.py:652
  82.5 2.6 %shard_map.181.partial_ref = f32[8,128,128]{2,1,0:T(8,128)S(1)} custom-call(bf16[128,1024]{1,0:T(8,128)(2,1)S(1)} %get-tuple-element.84.refs_0_.field_ref, bf16[48,1024]{1,0:T(8,128)(2,1)S(1)} %collective-permute-done.23.refs_1_.refs_0_, f32[8,56,128]{2,1,0:T(8,128)S(1)} %shard_map.164.refs_2_.params_ref.refs_4_.refs_8_, bf16[128,1024]{1,0:T(8,128)(2,1)S(1)} %bitcast.20), custom_call_target="tpu_custom_call" | custom-call | bytes 8000000 | tf_op jit(solution)/shard_map/pallas_call | solution.py:26
  85.1 2.5 %collective-permute-start.28 = (f32[2,56,128]{2,1,0:T(8,128)S(1)}, f32[2,56,128]{2,1,0:T(8,128)S(1)}, u32[]{:S(2)}, u32[]{:S(2)}) collective-permute-start(f32[2,56,128]{2,1,0:T(8,128)S(1)} %shard_map.185.refs_0_), channel_id=1, source_target_pairs={{0,2},{1,3},{2,0},{3,1},{4,6},{5,7},{6,4},{7,5},{8,10},{9,11},{10,... | collective-permute-start | bytes 172040 | tf_op jit(solution)/shard_map/ppermute | solution.py:652
  87.6 1.7 %shard_map.183 = bf16[128,1024]{1,0:T(8,128)(2,1)} custom-call(f32[8,128,128]{2,1,0:T(8,128)S(1)} %shard_map.181.partial_ref, bf16[48,1024]{1,0:T(8,128)(2,1)S(1)} %collective-permute-done.24.first_ref, bf16[48,1024]{1,0:T(8,128)(2,1)S(1)} %collective-permute-done.25.second_ref, f32[8,56,128]{2,1,0:T(8,128)S(1)} %shard_map.164.refs_2_.params_ref.refs_4_.refs_8_), custom_call_target="tpu_custom_call" | custom-call | bytes 5000000 | tf_op jit(solution)/shard_map/pallas_call | solution.py:26
  (67 shorter events, 19.1 us)
Async XLA Ops:
  3.6 27.5 %collective-permute-start = (bf16[256,1024]{1,0:T(8,128)(2,1)}, bf16[256,1024]{1,0:T(8,128)(2,1)S(1)}, u32[]{:S(2)}, u32[]{:S(2)}) collective-permute-start(bf16[256,1024]{1,0:T(8,128)(2,1)} %get-tuple-element.52), channel_id=1, source_target_pairs={{0,4},{1,5},{2,6},{3,7},{4,0},{5,1},{6,2},{7,3},{8,12},{9,13},{10,... | collective-permute-start | bytes 1572872 | tf_op jit(solution)/shard_map/ppermute | solution.py:652
  7.7 17.2 %collective-permute-start.4 = (bf16[224,1024]{1,0:T(8,128)(2,1)}, bf16[224,1024]{1,0:T(8,128)(2,1)S(1)}, u32[]{:S(2)}, u32[]{:S(2)}) collective-permute-start(bf16[224,1024]{1,0:T(8,128)(2,1)} %get-tuple-element.53.refs_5_.refs_9_.refs_4_), channel_id=1, source_target_pairs={{0,24},{8,16},{16,8},{24,0},{1,25},{9,17},{17,9},{25,1},{2,26},{10... | collective-permute-start | bytes 1376264 | tf_op jit(solution)/shard_map/ppermute | solution.py:648
  10.1 20.5 %collective-permute-start.3 = (bf16[224,1024]{1,0:T(8,128)(2,1)}, bf16[224,1024]{1,0:T(8,128)(2,1)S(1)}, u32[]{:S(2)}, u32[]{:S(2)}) collective-permute-start(bf16[224,1024]{1,0:T(8,128)(2,1)} %get-tuple-element.53.refs_5_.refs_9_.refs_4_), channel_id=1, source_target_pairs={{0,16},{8,24},{16,0},{24,8},{1,17},{9,25},{17,1},{25,9},{2,18},{10... | collective-permute-start | bytes 1376264 | tf_op jit(solution)/shard_map/ppermute | solution.py:648
  10.7 20.1 %collective-permute-start.2 = (bf16[224,1024]{1,0:T(8,128)(2,1)}, bf16[224,1024]{1,0:T(8,128)(2,1)S(1)}, u32[]{:S(2)}, u32[]{:S(2)}) collective-permute-start(bf16[224,1024]{1,0:T(8,128)(2,1)} %get-tuple-element.53.refs_5_.refs_9_.refs_4_), channel_id=1, source_target_pairs={{0,8},{8,0},{16,24},{24,16},{1,9},{9,1},{17,25},{25,17},{2,10},{10... | collective-permute-start | bytes 1376264 | tf_op jit(solution)/shard_map/ppermute | solution.py:648
  11.2 13.7 %collective-permute-start.1 = (bf16[128,1024]{1,0:T(8,128)(2,1)}, bf16[128,1024]{1,0:T(8,128)(2,1)S(1)}, u32[]{:S(2)}, u32[]{:S(2)}) collective-permute-start(bf16[128,1024]{1,0:T(8,128)(2,1)} %bitcast.14), channel_id=1, source_target_pairs={{0,2},{1,3},{2,0},{3,1},{4,6},{5,7},{6,4},{7,5},{8,10},{9,11},{10,... | collective-permute-start | bytes 786440 | tf_op jit(solution)/shard_map/ppermute | solution.py:652
  31.1 11.4 %collective-permute-start.10 = (bf16[208,1024]{1,0:T(8,128)(2,1)S(1)}, bf16[208,1024]{1,0:T(8,128)(2,1)S(1)}, u32[]{:S(2)}, u32[]{:S(2)}) collective-permute-start(bf16[208,1024]{1,0:T(8,128)(2,1)S(1)} %shard_map.168.refs_9_.refs_13_.refs_8_), channel_id=1, source_target_pairs={{0,16},{8,24},{16,0},{24,8},{1,17},{9,25},{17,1},{25,9},{2,18},{10... | collective-permute-start | bytes 1277960 | tf_op jit(solution)/shard_map/ppermute | solution.py:648
  32.7 11.3 %collective-permute-start.9 = (bf16[208,1024]{1,0:T(8,128)(2,1)S(1)}, bf16[208,1024]{1,0:T(8,128)(2,1)S(1)}, u32[]{:S(2)}, u32[]{:S(2)}) collective-permute-start(bf16[208,1024]{1,0:T(8,128)(2,1)S(1)} %shard_map.168.refs_9_.refs_13_.refs_8_), channel_id=1, source_target_pairs={{0,8},{8,0},{16,24},{24,16},{1,9},{9,1},{17,25},{25,17},{2,10},{10... | collective-permute-start | bytes 1277960 | tf_op jit(solution)/shard_map/ppermute | solution.py:648
  34.5 4.6 %collective-permute-start.6 = (bf16[48,1024]{1,0:T(8,128)(2,1)S(1)}, bf16[48,1024]{1,0:T(8,128)(2,1)S(1)}, u32[]{:S(2)}, u32[]{:S(2)}) collective-permute-start(bf16[48,1024]{1,0:T(8,128)(2,1)S(1)} %get-tuple-element.61), channel_id=1, source_target_pairs={{1,2},{2,1},{3,0},{0,3},{5,6},{6,5},{7,4},{4,7},{9,10},{10,9},{11,... | collective-permute-start | bytes 294920 | tf_op jit(solution)/shard_map/ppermute | solution.py:75
  35.4 9.9 %collective-permute-start.8 = (bf16[128,1024]{1,0:T(8,128)(2,1)S(1)}, bf16[128,1024]{1,0:T(8,128)(2,1)S(1)}, u32[]{:S(2)}, u32[]{:S(2)}) collective-permute-start(bf16[128,1024]{1,0:T(8,128)(2,1)S(1)} %bitcast.15), channel_id=1, source_target_pairs={{0,1},{1,0},{2,3},{3,2},{4,5},{5,4},{6,7},{7,6},{8,9},{9,8},{10,11... | collective-permute-start | bytes 786440 | tf_op jit(solution)/shard_map/ppermute | solution.py:652
  40.4 5.0 %collective-permute-start.7 = (bf16[128,1024]{1,0:T(8,128)(2,1)S(1)}, bf16[128,1024]{1,0:T(8,128)(2,1)S(1)}, u32[]{:S(2)}, u32[]{:S(2)}) collective-permute-start(bf16[128,1024]{1,0:T(8,128)(2,1)S(1)} %get-tuple-element.62.refs_0_), channel_id=1, source_target_pairs={{0,1},{1,0},{2,3},{3,2},{4,5},{5,4},{6,7},{7,6},{8,9},{9,8},{10,11... | collective-permute-start | bytes 786440 | tf_op jit(solution)/shard_map/ppermute | solution.py:652
  41.2 8.3 %collective-permute-start.11 = (bf16[128,1024]{1,0:T(8,128)(2,1)S(1)}, bf16[128,1024]{1,0:T(8,128)(2,1)S(1)}, u32[]{:S(2)}, u32[]{:S(2)}) collective-permute-start(bf16[128,1024]{1,0:T(8,128)(2,1)S(1)} %get-tuple-element.62.refs_0_), channel_id=1, source_target_pairs={{0,2},{1,3},{2,0},{3,1},{4,6},{5,7},{6,4},{7,5},{8,10},{9,11},{10,... | collective-permute-start | bytes 786440 | tf_op jit(solution)/shard_map/ppermute | solution.py:652
  42.5 7.3 %collective-permute-start.13 = (bf16[112,1024]{1,0:T(8,128)(2,1)S(1)}, bf16[112,1024]{1,0:T(8,128)(2,1)S(1)}, u32[]{:S(2)}, u32[]{:S(2)}) collective-permute-start(bf16[112,1024]{1,0:T(8,128)(2,1)S(1)} %shard_map.171), channel_id=1, source_target_pairs={{0,8},{8,0},{16,24},{24,16},{1,9},{9,1},{17,25},{25,17},{2,10},{10... | collective-permute-start | bytes 688136 | tf_op jit(solution)/shard_map/ppermute | solution.py:648
  44.1 5.7 %collective-permute-start.12 = (bf16[96,1024]{1,0:T(8,128)(2,1)S(1)}, bf16[96,1024]{1,0:T(8,128)(2,1)S(1)}, u32[]{:S(2)}, u32[]{:S(2)}) collective-permute-start(bf16[96,1024]{1,0:T(8,128)(2,1)S(1)} %shard_map.170), channel_id=1, source_target_pairs={{0,16},{8,24},{16,0},{24,8},{1,17},{9,25},{17,1},{25,9},{2,18},{10... | collective-permute-start | bytes 589832 | tf_op jit(solution)/shard_map/ppermute | solution.py:648
  55.6 18.1 %collective-permute-start.16 = (bf16[256,1024]{1,0:T(8,128)(2,1)S(1)}, bf16[256,1024]{1,0:T(8,128)(2,1)S(1)}, u32[]{:S(2)}, u32[]{:S(2)}) collective-permute-start(bf16[256,1024]{1,0:T(8,128)(2,1)S(1)} %get-tuple-element.71), channel_id=1, source_target_pairs={{0,1},{1,0},{2,3},{3,2},{4,5},{5,4},{6,7},{7,6},{8,9},{9,8},{10,11... | collective-permute-start | bytes 1572872 | tf_op jit(solution)/shard_map/ppermute | solution.py:652
  56.4 8.4 %collective-permute-start.18 = (bf16[128,1024]{1,0:T(8,128)(2,1)S(1)}, bf16[128,1024]{1,0:T(8,128)(2,1)S(1)}, u32[]{:S(2)}, u32[]{:S(2)}) collective-permute-start(bf16[128,1024]{1,0:T(8,128)(2,1)S(1)} %shard_map.176), channel_id=1, source_target_pairs={{0,2},{1,3},{2,0},{3,1},{4,6},{5,7},{6,4},{7,5},{8,10},{9,11},{10,... | collective-permute-start | bytes 786440 | tf_op jit(solution)/shard_map/ppermute | solution.py:652
  67.3 6.4 %collective-permute-start.19 = (f32[2,56,128]{2,1,0:T(8,128)S(1)}, f32[2,56,128]{2,1,0:T(8,128)S(1)}, u32[]{:S(2)}, u32[]{:S(2)}) collective-permute-start(f32[2,56,128]{2,1,0:T(8,128)S(1)} %get-tuple-element.80), channel_id=1, source_target_pairs={{0,8},{8,0},{16,24},{24,16},{1,9},{9,1},{17,25},{25,17},{2,10},{10... | collective-permute-start | bytes 172040 | tf_op jit(solution)/shard_map/ppermute | solution.py:648
  68.0 5.7 %collective-permute-start.20 = (f32[2,56,128]{2,1,0:T(8,128)S(1)}, f32[2,56,128]{2,1,0:T(8,128)S(1)}, u32[]{:S(2)}, u32[]{:S(2)}) collective-permute-start(f32[2,56,128]{2,1,0:T(8,128)S(1)} %get-tuple-element.81), channel_id=1, source_target_pairs={{0,16},{8,24},{16,0},{24,8},{1,17},{9,25},{17,1},{25,9},{2,18},{10... | collective-permute-start | bytes 172040 | tf_op jit(solution)/shard_map/ppermute | solution.py:648
  69.4 5.1 %collective-permute-start.21 = (f32[2,56,128]{2,1,0:T(8,128)S(1)}, f32[2,56,128]{2,1,0:T(8,128)S(1)}, u32[]{:S(2)}, u32[]{:S(2)}) collective-permute-start(f32[2,56,128]{2,1,0:T(8,128)S(1)} %get-tuple-element.82), channel_id=1, source_target_pairs={{0,24},{8,16},{16,8},{24,0},{1,25},{9,17},{17,9},{25,1},{2,26},{10... | collective-permute-start | bytes 172040 | tf_op jit(solution)/shard_map/ppermute | solution.py:648
  70.8 6.0 %collective-permute-start.23 = (bf16[48,1024]{1,0:T(8,128)(2,1)S(1)}, bf16[48,1024]{1,0:T(8,128)(2,1)S(1)}, u32[]{:S(2)}, u32[]{:S(2)}) collective-permute-start(bf16[48,1024]{1,0:T(8,128)(2,1)S(1)} %get-tuple-element.86), channel_id=1, source_target_pairs={{0,4},{4,0},{1,5},{5,1},{2,6},{6,2},{3,7},{7,3},{8,12},{12,8},{9,1... | collective-permute-start | bytes 294920 | tf_op jit(solution)/shard_map/ppermute | solution.py:61
  74.5 14.8 %collective-permute-start.22 = (bf16[128,1024]{1,0:T(8,128)(2,1)S(1)}, bf16[128,1024]{1,0:T(8,128)(2,1)S(1)}, u32[]{:S(2)}, u32[]{:S(2)}) collective-permute-start(bf16[128,1024]{1,0:T(8,128)(2,1)S(1)} %shard_map.175), channel_id=1, source_target_pairs={{0,2},{1,3},{2,0},{3,1},{4,6},{5,7},{6,4},{7,5},{8,10},{9,11},{10,... | collective-permute-start | bytes 786440 | tf_op jit(solution)/shard_map/ppermute | solution.py:652
  77.1 8.1 %collective-permute-start.24 = (bf16[48,1024]{1,0:T(8,128)(2,1)S(1)}, bf16[48,1024]{1,0:T(8,128)(2,1)S(1)}, u32[]{:S(2)}, u32[]{:S(2)}) collective-permute-start(bf16[48,1024]{1,0:T(8,128)(2,1)S(1)} %get-tuple-element.87), channel_id=1, source_target_pairs={{0,1},{1,0},{2,3},{3,2},{4,5},{5,4},{6,7},{7,6},{8,9},{9,8},{10,11... | collective-permute-start | bytes 294920 | tf_op jit(solution)/shard_map/ppermute | solution.py:75
  77.6 7.5 %collective-permute-start.25 = (bf16[48,1024]{1,0:T(8,128)(2,1)S(1)}, bf16[48,1024]{1,0:T(8,128)(2,1)S(1)}, u32[]{:S(2)}, u32[]{:S(2)}) collective-permute-start(bf16[48,1024]{1,0:T(8,128)(2,1)S(1)} %get-tuple-element.88), channel_id=1, source_target_pairs={{1,2},{2,1},{3,0},{0,3},{5,6},{6,5},{7,4},{4,7},{9,10},{10,9},{11,... | collective-permute-start | bytes 294920 | tf_op jit(solution)/shard_map/ppermute | solution.py:75
  78.9 6.2 %collective-permute-start.27 = (f32[2,56,128]{2,1,0:T(8,128)S(1)}, f32[2,56,128]{2,1,0:T(8,128)S(1)}, u32[]{:S(2)}, u32[]{:S(2)}) collective-permute-start(f32[2,56,128]{2,1,0:T(8,128)S(1)} %shard_map.184.refs_0_), channel_id=1, source_target_pairs={{0,4},{1,5},{2,6},{3,7},{4,0},{5,1},{6,2},{7,3},{8,12},{9,13},{10,... | collective-permute-start | bytes 172040 | tf_op jit(solution)/shard_map/ppermute | solution.py:652
  85.1 5.1 %collective-permute-start.28 = (f32[2,56,128]{2,1,0:T(8,128)S(1)}, f32[2,56,128]{2,1,0:T(8,128)S(1)}, u32[]{:S(2)}, u32[]{:S(2)}) collective-permute-start(f32[2,56,128]{2,1,0:T(8,128)S(1)} %shard_map.185.refs_0_), channel_id=1, source_target_pairs={{0,2},{1,3},{2,0},{3,1},{4,6},{5,7},{6,4},{7,5},{8,10},{9,11},{10,... | collective-permute-start | bytes 172040 | tf_op jit(solution)/shard_map/ppermute | solution.py:652
  (9 other events, 115.0 us)

commit v5 on v4

--- a/solution.py
+++ b/solution.py
@@ -14,7 +14,7 @@
 PITCH = 32
 INSET = 8
 TAP_ROWS = 56
-BIAS_ROWS = 16
+BIAS_ROWS = 8
 PARAM_ROWS = 32
 F32 = jnp.float32
 BF16 = jnp.bfloat16

time: 91 us -> 90.1 us (level)
  starting transfers between devices: 35.8 us -> 34.3 us
    ppermute x10, waiting for transfers between devices: 7.46 us -> 8.93 us  [across(): return lax.ppermute(block, 'dp', [(i, i ^ bits) for i in range(groups)])]
    ppermute x10, starting transfers between devices: 12.8 us -> 11.7 us  [across(): return lax.ppermute(block, 'dp', [(i, i ^ bits) for i in range(groups)])]
  transfers between devices with their start and end apart: 29 -> 29, of which waited for: 13 -> 12; matrix products, arithmetic and copies ran while one was open for 0% -> 0% of each run, Pallas kernels for 17% -> 17%
where the time goes in v5:
time: 90.1 us; the launch traced here: 89.9 us
  starting transfers between devices  34.3 us (38%)
  waiting for transfers between devices  31.9 us (35%)
  Pallas kernels  22 us (24%)
    ppermute x14, waiting for transfers between devices, tile_swap(): lax.ppermute(block, 'tile', [(i, i ^ bits) for i in range(lax.axis_size('...  22 us
    pallas_call x24, Pallas kernels, call(): pl.pallas_call(body, out_shape=outs, in_specs=[VMEM] * len(args), out_spe...  19.1 us
    ppermute x14, starting transfers between devices, tile_swap(): lax.ppermute(block, 'tile', [(i, i ^ bits) for i in range(lax.axis_size('...  17.1 us
    ppermute x10, starting transfers between devices, across(): return lax.ppermute(block, 'dp', [(i, i ^ bits) for i in range(groups)])  11.7 us
    ppermute x10, waiting for transfers between devices, across(): return lax.ppermute(block, 'dp', [(i, i ^ bits) for i in range(groups)])  8.93 us
    ppermute x4, starting transfers between devices, swap_cols(): moved.append(lax.ppermute(block, 'tile', route))  3.4 us
    pallas_call x1, Pallas kernels, first_sends(): pl.pallas_call(body, out_shape=outs, in_specs=[VMEM] + [far] * (len(args)...  2.92 us
    ppermute x1, starting transfers between devices, swap_rows(): moved.append(lax.ppermute(block, 'tile', route))  2.13 us
  transfers between devices with their start and end apart: 29, of which 12 were waited for; matrix products, arithmetic and copies ran while one was open for 0% of the time, Pallas kernels for 17%

profile of v5, /device:TPU:0, one launch (start us, length us, event | category | flops | bytes accessed | tf_op | source)
XLA Modules:
  0.0 89.9 jit_solution(8558722642207240695)
XLA Ops:
  0.7 2.9 %shard_map.162 = (bf16[224,1024]{1,0:T(8,128)(2,1)}, bf16[248,1024]{1,0:T(8,128)(2,1)}, f32[2,56,128]{2,1,0:T(8,128)}) custom-call(bf16[1,96]{1,0:T(2,128)(2,1)} %bitcast.32, bf16[128,1024]{1,0:T(8,128)(2,1)} %bitcast.21, bf16[96,1024]{1,0:T(8,128)(2,1)} %in_ref.1, bf16[96,1024]{1,0:T(8,128)(2,1)} %out_ref.1, f32[49,256]{1,0:T(8,128)} %kernel_ref.1, ...), custom_call_target="tpu_custom_call" | custom-call | flops 10000 | bytes 1000000 | tf_op jit(solution)/shard_map/pallas_call | solution.py:794
  3.6 4.1 %collective-permute-start = (bf16[248,1024]{1,0:T(8,128)(2,1)}, bf16[248,1024]{1,0:T(8,128)(2,1)S(1)}, u32[]{:S(2)}, u32[]{:S(2)}) collective-permute-start(bf16[248,1024]{1,0:T(8,128)(2,1)} %get-tuple-element.52), channel_id=1, source_target_pairs={{0,4},{1,5},{2,6},{3,7},{4,0},{5,1},{6,2},{7,3},{8,12},{9,13},{10,... | collective-permute-start | bytes 1523720 | tf_op jit(solution)/shard_map/ppermute | solution.py:652
  7.7 2.4 %collective-permute-start.4 = (bf16[224,1024]{1,0:T(8,128)(2,1)}, bf16[224,1024]{1,0:T(8,128)(2,1)S(1)}, u32[]{:S(2)}, u32[]{:S(2)}) collective-permute-start(bf16[224,1024]{1,0:T(8,128)(2,1)} %get-tuple-element.53.refs_5_.refs_9_.refs_4_), channel_id=1, source_target_pairs={{0,24},{8,16},{16,8},{24,0},{1,25},{9,17},{17,9},{25,1},{2,26},{10... | collective-permute-start | bytes 1376264 | tf_op jit(solution)/shard_map/ppermute | solution.py:648
  11.2 1.6 %collective-permute-start.1 = (bf16[128,1024]{1,0:T(8,128)(2,1)}, bf16[128,1024]{1,0:T(8,128)(2,1)S(1)}, u32[]{:S(2)}, u32[]{:S(2)}) collective-permute-start(bf16[128,1024]{1,0:T(8,128)(2,1)} %bitcast.14), channel_id=1, source_target_pairs={{0,2},{1,3},{2,0},{3,1},{4,6},{5,7},{6,4},{7,5},{8,10},{9,11},{10,... | collective-permute-start | bytes 786440 | tf_op jit(solution)/shard_map/ppermute | solution.py:652
  12.8 11.7 %collective-permute-done.1.refs_6_.refs_2_ = bf16[128,1024]{1,0:T(8,128)(2,1)S(1)} collective-permute-done((bf16[128,1024]{1,0:T(8,128)(2,1)}, bf16[128,1024]{1,0:T(8,128)(2,1)S(1)}, u32[]{:S(2)}, u32[]{:S(2)}) %collective-permute-start.1) | collective-permute-done | bytes 262176 | tf_op jit(solution)/shard_map/ppermute | solution.py:652
  24.5 6.1 %collective-permute-done.3.refs_1_.refs_7_.refs_11_.refs_6_ = bf16[224,1024]{1,0:T(8,128)(2,1)S(1)} collective-permute-done((bf16[224,1024]{1,0:T(8,128)(2,1)}, bf16[224,1024]{1,0:T(8,128)(2,1)S(1)}, u32[]{:S(2)}, u32[]{:S(2)}) %collective-permute-start.3) | collective-permute-done | bytes 458784 | tf_op jit(solution)/shard_map/ppermute | solution.py:648
  30.8 1.5 %collective-permute-start.10 = (bf16[200,1024]{1,0:T(8,128)(2,1)S(1)}, bf16[200,1024]{1,0:T(8,128)(2,1)S(1)}, u32[]{:S(2)}, u32[]{:S(2)}) collective-permute-start(bf16[200,1024]{1,0:T(8,128)(2,1)S(1)} %shard_map.168.refs_9_.refs_13_.refs_8_), channel_id=1, source_target_pairs={{0,16},{8,24},{16,0},{24,8},{1,17},{9,25},{17,1},{25,9},{2,18},{10... | collective-permute-start | bytes 1228808 | tf_op jit(solution)/shard_map/ppermute | solution.py:648
  35.1 2.6 %shard_map.165 = (f32[8,448,128]{2,1,0:T(8,128)S(1)}, f32[8,128,128]{2,1,0:T(8,128)S(1)}) custom-call(bf16[128,1024]{1,0:T(8,128)(2,1)S(1)} %bitcast.23, bf16[48,1024]{1,0:T(8,128)(2,1)S(1)} %shard_map.163.refs_1_.refs_0_, f32[8,56,128]{2,1,0:T(8,128)S(1)} %shard_map.164.refs_2_.params_ref.refs_4_.refs_8_), custom_call_target="tpu_custom_call" | custom-call | bytes 8000000 | tf_op jit(solution)/shard_map/pallas_call | solution.py:26
  42.1 1.6 %collective-permute-start.13 = (bf16[104,1024]{1,0:T(8,128)(2,1)S(1)}, bf16[104,1024]{1,0:T(8,128)(2,1)S(1)}, u32[]{:S(2)}, u32[]{:S(2)}) collective-permute-start(bf16[104,1024]{1,0:T(8,128)(2,1)S(1)} %shard_map.171), channel_id=1, source_target_pairs={{0,8},{8,0},{16,24},{24,16},{1,9},{9,1},{17,25},{25,17},{2,10},{10... | collective-permute-start | bytes 638984 | tf_op jit(solution)/shard_map/ppermute | solution.py:648
  45.1 2.1 %shard_map.169 = (bf16[256,672]{1,0:T(8,128)(2,1)S(1)}, f32[256,1024]{1,0:T(8,128)S(1)}) custom-call(bf16[128,1024]{1,0:T(8,128)(2,1)S(1)} %get-tuple-element.62.refs_0_, bf16[128,1024]{1,0:T(8,128)(2,1)S(1)} %collective-permute-done.7.refs_1_, bf16[128,1024]{1,0:T(8,128)(2,1)S(1)} %bitcast.16, ...), custom_call_target="tpu_custom_call" | custom-call | bytes 7000000 | tf_op jit(solution)/shard_map/pallas_call | solution.py:26
  47.1 1.6 %collective-permute-done.11.refs_2_ = bf16[128,1024]{1,0:T(8,128)(2,1)S(1)} collective-permute-done((bf16[128,1024]{1,0:T(8,128)(2,1)S(1)}, bf16[128,1024]{1,0:T(8,128)(2,1)S(1)}, u32[]{:S(2)}, u32[]{:S(2)}) %collective-permute-start.11) | collective-permute-done | bytes 262176 | tf_op jit(solution)/shard_map/ppermute | solution.py:652
  49.5 1.5 %collective-permute-done.14.refs_3_ = bf16[128,1024]{1,0:T(8,128)(2,1)S(1)} collective-permute-done((bf16[128,1024]{1,0:T(8,128)(2,1)S(1)}, bf16[128,1024]{1,0:T(8,128)(2,1)S(1)}, u32[]{:S(2)}, u32[]{:S(2)}) %collective-permute-start.14) | collective-permute-done | bytes 262176 | tf_op jit(solution)/shard_map/ppermute | solution.py:652
  51.0 3.0 %shard_map.173 = (bf16[256,96]{1,0:T(8,128)(2,1)S(1)}, bf16[256,768]{1,0:T(8,128)(2,1)S(1)}, f32[256,1024]{1,0:T(8,128)S(1)}, bf16[256,1024]{1,0:T(8,128)(2,1)S(1)}) custom-call(bf16[128,1024]{1,0:T(8,128)(2,1)S(1)} %get-tuple-element.62.refs_0_, bf16[128,1024]{1,0:T(8,128)(2,1)S(1)} %collective-permute-done.7.refs_1_, ...), custom_call_target="tpu_custom_call" | custom-call | bytes 9000000 | tf_op jit(solution)/shard_map/pallas_call | solution.py:26
  56.0 1.6 %collective-permute-start.18 = (bf16[128,1024]{1,0:T(8,128)(2,1)S(1)}, bf16[128,1024]{1,0:T(8,128)(2,1)S(1)}, u32[]{:S(2)}, u32[]{:S(2)}) collective-permute-start(bf16[128,1024]{1,0:T(8,128)(2,1)S(1)} %shard_map.176), channel_id=1, source_target_pairs={{0,2},{1,3},{2,0},{3,1},{4,6},{5,7},{6,4},{7,5},{8,10},{9,11},{10,... | collective-permute-start | bytes 786440 | tf_op jit(solution)/shard_map/ppermute | solution.py:652
  57.7 6.8 %collective-permute-done.18.far_ref = bf16[128,1024]{1,0:T(8,128)(2,1)S(1)} collective-permute-done((bf16[128,1024]{1,0:T(8,128)(2,1)S(1)}, bf16[128,1024]{1,0:T(8,128)(2,1)S(1)}, u32[]{:S(2)}, u32[]{:S(2)}) %collective-permute-start.18) | collective-permute-done | bytes 262176 | tf_op jit(solution)/shard_map/ppermute | solution.py:652
  64.9 2.0 %shard_map.178 = (f32[2,56,128]{2,1,0:T(8,128)S(1)}, f32[2,56,128]{2,1,0:T(8,128)S(1)}, f32[2,56,128]{2,1,0:T(8,128)S(1)}, f32[2,56,128]{2,1,0:T(8,128)S(1)}) custom-call(f32[8,448,128]{2,1,0:T(8,128)S(1)} %shard_map.172.padded_ref, f32[8,128,128]{2,1,0:T(8,128)S(1)} %get-tuple-element.76.conv, f32[8,8,128]{2,1,0:T(8,128)S(1)} %get-tuple-element.77.vectors_ref, ...), custom_call_target="tpu_custom_call" | custom-call | bytes 7380000 | tf_op jit(solution)/shard_map/pallas_call | solution.py:26
  70.5 2.1 %collective-permute-start.23 = (bf16[48,1024]{1,0:T(8,128)(2,1)S(1)}, bf16[48,1024]{1,0:T(8,128)(2,1)S(1)}, u32[]{:S(2)}, u32[]{:S(2)}) collective-permute-start(bf16[48,1024]{1,0:T(8,128)(2,1)S(1)} %get-tuple-element.86), channel_id=1, source_target_pairs={{0,4},{4,0},{1,5},{5,1},{2,6},{6,2},{3,7},{7,3},{8,12},{12,8},{9,1... | collective-permute-start | bytes 294920 | tf_op jit(solution)/shard_map/ppermute | solution.py:61
  72.7 1.5 %collective-permute-done.21.refs_3_ = f32[2,56,128]{2,1,0:T(8,128)S(1)} collective-permute-done((f32[2,56,128]{2,1,0:T(8,128)S(1)}, f32[2,56,128]{2,1,0:T(8,128)S(1)}, u32[]{:S(2)}, u32[]{:S(2)}) %collective-permute-start.21) | collective-permute-done | bytes 57376 | tf_op jit(solution)/shard_map/ppermute | solution.py:648
  74.2 1.6 %collective-permute-start.22 = (bf16[128,1024]{1,0:T(8,128)(2,1)S(1)}, bf16[128,1024]{1,0:T(8,128)(2,1)S(1)}, u32[]{:S(2)}, u32[]{:S(2)}) collective-permute-start(bf16[128,1024]{1,0:T(8,128)(2,1)S(1)} %shard_map.175), channel_id=1, source_target_pairs={{0,2},{1,3},{2,0},{3,1},{4,6},{5,7},{6,4},{7,5},{8,10},{9,11},{10,... | collective-permute-start | bytes 786440 | tf_op jit(solution)/shard_map/ppermute | solution.py:652
  76.9 1.6 %collective-permute-start.25 = (bf16[48,1024]{1,0:T(8,128)(2,1)S(1)}, bf16[48,1024]{1,0:T(8,128)(2,1)S(1)}, u32[]{:S(2)}, u32[]{:S(2)}) collective-permute-start(bf16[48,1024]{1,0:T(8,128)(2,1)S(1)} %get-tuple-element.88), channel_id=1, source_target_pairs={{1,2},{2,1},{3,0},{0,3},{5,6},{6,5},{7,4},{4,7},{9,10},{10,9},{11,... | collective-permute-start | bytes 294920 | tf_op jit(solution)/shard_map/ppermute | solution.py:75
  78.5 3.0 %collective-permute-start.27 = (f32[2,56,128]{2,1,0:T(8,128)S(1)}, f32[2,56,128]{2,1,0:T(8,128)S(1)}, u32[]{:S(2)}, u32[]{:S(2)}) collective-permute-start(f32[2,56,128]{2,1,0:T(8,128)S(1)} %shard_map.184.refs_0_), channel_id=1, source_target_pairs={{0,4},{1,5},{2,6},{3,7},{4,0},{5,1},{6,2},{7,3},{8,12},{9,13},{10,... | collective-permute-start | bytes 172040 | tf_op jit(solution)/shard_map/ppermute | solution.py:652
  81.4 2.6 %shard_map.181.partial_ref = f32[8,128,128]{2,1,0:T(8,128)S(1)} custom-call(bf16[128,1024]{1,0:T(8,128)(2,1)S(1)} %get-tuple-element.84.refs_0_.field_ref, bf16[48,1024]{1,0:T(8,128)(2,1)S(1)} %collective-permute-done.23.refs_1_.refs_0_, f32[8,56,128]{2,1,0:T(8,128)S(1)} %shard_map.164.refs_2_.params_ref.refs_4_.refs_8_, bf16[128,1024]{1,0:T(8,128)(2,1)S(1)} %bitcast.20), custom_call_target="tpu_custom_call" | custom-call | bytes 8000000 | tf_op jit(solution)/shard_map/pallas_call | solution.py:26
  84.1 2.5 %collective-permute-start.28 = (f32[2,56,128]{2,1,0:T(8,128)S(1)}, f32[2,56,128]{2,1,0:T(8,128)S(1)}, u32[]{:S(2)}, u32[]{:S(2)}) collective-permute-start(f32[2,56,128]{2,1,0:T(8,128)S(1)} %shard_map.185.refs_0_), channel_id=1, source_target_pairs={{0,2},{1,3},{2,0},{3,1},{4,6},{5,7},{6,4},{7,5},{8,10},{9,11},{10,... | collective-permute-start | bytes 172040 | tf_op jit(solution)/shard_map/ppermute | solution.py:652
  86.6 1.7 %shard_map.183 = bf16[128,1024]{1,0:T(8,128)(2,1)} custom-call(f32[8,128,128]{2,1,0:T(8,128)S(1)} %shard_map.181.partial_ref, bf16[48,1024]{1,0:T(8,128)(2,1)S(1)} %collective-permute-done.24.first_ref, bf16[48,1024]{1,0:T(8,128)(2,1)S(1)} %collective-permute-done.25.second_ref, f32[8,56,128]{2,1,0:T(8,128)S(1)} %shard_map.164.refs_2_.params_ref.refs_4_.refs_8_), custom_call_target="tpu_custom_call" | custom-call | bytes 5000000 | tf_op jit(solution)/shard_map/pallas_call | solution.py:26
  (67 shorter events, 19.3 us)
Async XLA Ops:
  3.6 27.1 %collective-permute-start = (bf16[248,1024]{1,0:T(8,128)(2,1)}, bf16[248,1024]{1,0:T(8,128)(2,1)S(1)}, u32[]{:S(2)}, u32[]{:S(2)}) collective-permute-start(bf16[248,1024]{1,0:T(8,128)(2,1)} %get-tuple-element.52), channel_id=1, source_target_pairs={{0,4},{1,5},{2,6},{3,7},{4,0},{5,1},{6,2},{7,3},{8,12},{9,13},{10,... | collective-permute-start | bytes 1523720 | tf_op jit(solution)/shard_map/ppermute | solution.py:652
  7.7 16.8 %collective-permute-start.4 = (bf16[224,1024]{1,0:T(8,128)(2,1)}, bf16[224,1024]{1,0:T(8,128)(2,1)S(1)}, u32[]{:S(2)}, u32[]{:S(2)}) collective-permute-start(bf16[224,1024]{1,0:T(8,128)(2,1)} %get-tuple-element.53.refs_5_.refs_9_.refs_4_), channel_id=1, source_target_pairs={{0,24},{8,16},{16,8},{24,0},{1,25},{9,17},{17,9},{25,1},{2,26},{10... | collective-permute-start | bytes 1376264 | tf_op jit(solution)/shard_map/ppermute | solution.py:648
  10.1 20.5 %collective-permute-start.3 = (bf16[224,1024]{1,0:T(8,128)(2,1)}, bf16[224,1024]{1,0:T(8,128)(2,1)S(1)}, u32[]{:S(2)}, u32[]{:S(2)}) collective-permute-start(bf16[224,1024]{1,0:T(8,128)(2,1)} %get-tuple-element.53.refs_5_.refs_9_.refs_4_), channel_id=1, source_target_pairs={{0,16},{8,24},{16,0},{24,8},{1,17},{9,25},{17,1},{25,9},{2,18},{10... | collective-permute-start | bytes 1376264 | tf_op jit(solution)/shard_map/ppermute | solution.py:648
  10.7 20.1 %collective-permute-start.2 = (bf16[224,1024]{1,0:T(8,128)(2,1)}, bf16[224,1024]{1,0:T(8,128)(2,1)S(1)}, u32[]{:S(2)}, u32[]{:S(2)}) collective-permute-start(bf16[224,1024]{1,0:T(8,128)(2,1)} %get-tuple-element.53.refs_5_.refs_9_.refs_4_), channel_id=1, source_target_pairs={{0,8},{8,0},{16,24},{24,16},{1,9},{9,1},{17,25},{25,17},{2,10},{10... | collective-permute-start | bytes 1376264 | tf_op jit(solution)/shard_map/ppermute | solution.py:648
  11.2 13.3 %collective-permute-start.1 = (bf16[128,1024]{1,0:T(8,128)(2,1)}, bf16[128,1024]{1,0:T(8,128)(2,1)S(1)}, u32[]{:S(2)}, u32[]{:S(2)}) collective-permute-start(bf16[128,1024]{1,0:T(8,128)(2,1)} %bitcast.14), channel_id=1, source_target_pairs={{0,2},{1,3},{2,0},{3,1},{4,6},{5,7},{6,4},{7,5},{8,10},{9,11},{10,... | collective-permute-start | bytes 786440 | tf_op jit(solution)/shard_map/ppermute | solution.py:652
  30.8 11.4 %collective-permute-start.10 = (bf16[200,1024]{1,0:T(8,128)(2,1)S(1)}, bf16[200,1024]{1,0:T(8,128)(2,1)S(1)}, u32[]{:S(2)}, u32[]{:S(2)}) collective-permute-start(bf16[200,1024]{1,0:T(8,128)(2,1)S(1)} %shard_map.168.refs_9_.refs_13_.refs_8_), channel_id=1, source_target_pairs={{0,16},{8,24},{16,0},{24,8},{1,17},{9,25},{17,1},{25,9},{2,18},{10... | collective-permute-start | bytes 1228808 | tf_op jit(solution)/shard_map/ppermute | solution.py:648
  32.2 11.4 %collective-permute-start.9 = (bf16[200,1024]{1,0:T(8,128)(2,1)S(1)}, bf16[200,1024]{1,0:T(8,128)(2,1)S(1)}, u32[]{:S(2)}, u32[]{:S(2)}) collective-permute-start(bf16[200,1024]{1,0:T(8,128)(2,1)S(1)} %shard_map.168.refs_9_.refs_13_.refs_8_), channel_id=1, source_target_pairs={{0,8},{8,0},{16,24},{24,16},{1,9},{9,1},{17,25},{25,17},{2,10},{10... | collective-permute-start | bytes 1228808 | tf_op jit(solution)/shard_map/ppermute | solution.py:648
  35.0 9.3 %collective-permute-start.8 = (bf16[128,1024]{1,0:T(8,128)(2,1)S(1)}, bf16[128,1024]{1,0:T(8,128)(2,1)S(1)}, u32[]{:S(2)}, u32[]{:S(2)}) collective-permute-start(bf16[128,1024]{1,0:T(8,128)(2,1)S(1)} %bitcast.15), channel_id=1, source_target_pairs={{0,1},{1,0},{2,3},{3,2},{4,5},{5,4},{6,7},{7,6},{8,9},{9,8},{10,11... | collective-permute-start | bytes 786440 | tf_op jit(solution)/shard_map/ppermute | solution.py:652
  39.7 4.7 %collective-permute-start.7 = (bf16[128,1024]{1,0:T(8,128)(2,1)S(1)}, bf16[128,1024]{1,0:T(8,128)(2,1)S(1)}, u32[]{:S(2)}, u32[]{:S(2)}) collective-permute-start(bf16[128,1024]{1,0:T(8,128)(2,1)S(1)} %get-tuple-element.62.refs_0_), channel_id=1, source_target_pairs={{0,1},{1,0},{2,3},{3,2},{4,5},{5,4},{6,7},{7,6},{8,9},{9,8},{10,11... | collective-permute-start | bytes 786440 | tf_op jit(solution)/shard_map/ppermute | solution.py:652
  40.5 8.3 %collective-permute-start.11 = (bf16[128,1024]{1,0:T(8,128)(2,1)S(1)}, bf16[128,1024]{1,0:T(8,128)(2,1)S(1)}, u32[]{:S(2)}, u32[]{:S(2)}) collective-permute-start(bf16[128,1024]{1,0:T(8,128)(2,1)S(1)} %get-tuple-element.62.refs_0_), channel_id=1, source_target_pairs={{0,2},{1,3},{2,0},{3,1},{4,6},{5,7},{6,4},{7,5},{8,10},{9,11},{10,... | collective-permute-start | bytes 786440 | tf_op jit(solution)/shard_map/ppermute | solution.py:652
  42.1 7.3 %collective-permute-start.13 = (bf16[104,1024]{1,0:T(8,128)(2,1)S(1)}, bf16[104,1024]{1,0:T(8,128)(2,1)S(1)}, u32[]{:S(2)}, u32[]{:S(2)}) collective-permute-start(bf16[104,1024]{1,0:T(8,128)(2,1)S(1)} %shard_map.171), channel_id=1, source_target_pairs={{0,8},{8,0},{16,24},{24,16},{1,9},{9,1},{17,25},{25,17},{2,10},{10... | collective-permute-start | bytes 638984 | tf_op jit(solution)/shard_map/ppermute | solution.py:648
  43.7 5.7 %collective-permute-start.12 = (bf16[96,1024]{1,0:T(8,128)(2,1)S(1)}, bf16[96,1024]{1,0:T(8,128)(2,1)S(1)}, u32[]{:S(2)}, u32[]{:S(2)}) collective-permute-start(bf16[96,1024]{1,0:T(8,128)(2,1)S(1)} %shard_map.170), channel_id=1, source_target_pairs={{0,16},{8,24},{16,0},{24,8},{1,17},{9,25},{17,1},{25,9},{2,18},{10... | collective-permute-start | bytes 589832 | tf_op jit(solution)/shard_map/ppermute | solution.py:648
  44.3 5.2 %collective-permute-start.15 = (bf16[128,1024]{1,0:T(8,128)(2,1)S(1)}, bf16[128,1024]{1,0:T(8,128)(2,1)S(1)}, u32[]{:S(2)}, u32[]{:S(2)}) collective-permute-start(bf16[128,1024]{1,0:T(8,128)(2,1)S(1)} %collective-permute-done.1.refs_6_.refs_2_), channel_id=1, source_target_pairs={{0,1},{1,0},{2,3},{3,2},{4,5},{5,4},{6,7},{7,6},{8,9},{9,8},{10,11... | collective-permute-start | bytes 786440 | tf_op jit(solution)/shard_map/ppermute | solution.py:652
  55.2 17.4 %collective-permute-start.16 = (bf16[256,1024]{1,0:T(8,128)(2,1)S(1)}, bf16[256,1024]{1,0:T(8,128)(2,1)S(1)}, u32[]{:S(2)}, u32[]{:S(2)}) collective-permute-start(bf16[256,1024]{1,0:T(8,128)(2,1)S(1)} %get-tuple-element.71), channel_id=1, source_target_pairs={{0,1},{1,0},{2,3},{3,2},{4,5},{5,4},{6,7},{7,6},{8,9},{9,8},{10,11... | collective-permute-start | bytes 1572872 | tf_op jit(solution)/shard_map/ppermute | solution.py:652
  56.0 8.4 %collective-permute-start.18 = (bf16[128,1024]{1,0:T(8,128)(2,1)S(1)}, bf16[128,1024]{1,0:T(8,128)(2,1)S(1)}, u32[]{:S(2)}, u32[]{:S(2)}) collective-permute-start(bf16[128,1024]{1,0:T(8,128)(2,1)S(1)} %shard_map.176), channel_id=1, source_target_pairs={{0,2},{1,3},{2,0},{3,1},{4,6},{5,7},{6,4},{7,5},{8,10},{9,11},{10,... | collective-permute-start | bytes 786440 | tf_op jit(solution)/shard_map/ppermute | solution.py:652
  66.9 5.7 %collective-permute-start.19 = (f32[2,56,128]{2,1,0:T(8,128)S(1)}, f32[2,56,128]{2,1,0:T(8,128)S(1)}, u32[]{:S(2)}, u32[]{:S(2)}) collective-permute-start(f32[2,56,128]{2,1,0:T(8,128)S(1)} %get-tuple-element.80), channel_id=1, source_target_pairs={{0,8},{8,0},{16,24},{24,16},{1,9},{9,1},{17,25},{25,17},{2,10},{10... | collective-permute-start | bytes 172040 | tf_op jit(solution)/shard_map/ppermute | solution.py:648
  67.6 5.0 %collective-permute-start.20 = (f32[2,56,128]{2,1,0:T(8,128)S(1)}, f32[2,56,128]{2,1,0:T(8,128)S(1)}, u32[]{:S(2)}, u32[]{:S(2)}) collective-permute-start(f32[2,56,128]{2,1,0:T(8,128)S(1)} %get-tuple-element.81), channel_id=1, source_target_pairs={{0,16},{8,24},{16,0},{24,8},{1,17},{9,25},{17,1},{25,9},{2,18},{10... | collective-permute-start | bytes 172040 | tf_op jit(solution)/shard_map/ppermute | solution.py:648
  69.1 5.1 %collective-permute-start.21 = (f32[2,56,128]{2,1,0:T(8,128)S(1)}, f32[2,56,128]{2,1,0:T(8,128)S(1)}, u32[]{:S(2)}, u32[]{:S(2)}) collective-permute-start(f32[2,56,128]{2,1,0:T(8,128)S(1)} %get-tuple-element.82), channel_id=1, source_target_pairs={{0,24},{8,16},{16,8},{24,0},{1,25},{9,17},{17,9},{25,1},{2,26},{10... | collective-permute-start | bytes 172040 | tf_op jit(solution)/shard_map/ppermute | solution.py:648
  70.5 5.6 %collective-permute-start.23 = (bf16[48,1024]{1,0:T(8,128)(2,1)S(1)}, bf16[48,1024]{1,0:T(8,128)(2,1)S(1)}, u32[]{:S(2)}, u32[]{:S(2)}) collective-permute-start(bf16[48,1024]{1,0:T(8,128)(2,1)S(1)} %get-tuple-element.86), channel_id=1, source_target_pairs={{0,4},{4,0},{1,5},{5,1},{2,6},{6,2},{3,7},{7,3},{8,12},{12,8},{9,1... | collective-permute-start | bytes 294920 | tf_op jit(solution)/shard_map/ppermute | solution.py:61
  74.2 14.2 %collective-permute-start.22 = (bf16[128,1024]{1,0:T(8,128)(2,1)S(1)}, bf16[128,1024]{1,0:T(8,128)(2,1)S(1)}, u32[]{:S(2)}, u32[]{:S(2)}) collective-permute-start(bf16[128,1024]{1,0:T(8,128)(2,1)S(1)} %shard_map.175), channel_id=1, source_target_pairs={{0,2},{1,3},{2,0},{3,1},{4,6},{5,7},{6,4},{7,5},{8,10},{9,11},{10,... | collective-permute-start | bytes 786440 | tf_op jit(solution)/shard_map/ppermute | solution.py:652
  76.3 7.8 %collective-permute-start.24 = (bf16[48,1024]{1,0:T(8,128)(2,1)S(1)}, bf16[48,1024]{1,0:T(8,128)(2,1)S(1)}, u32[]{:S(2)}, u32[]{:S(2)}) collective-permute-start(bf16[48,1024]{1,0:T(8,128)(2,1)S(1)} %get-tuple-element.87), channel_id=1, source_target_pairs={{0,1},{1,0},{2,3},{3,2},{4,5},{5,4},{6,7},{7,6},{8,9},{9,8},{10,11... | collective-permute-start | bytes 294920 | tf_op jit(solution)/shard_map/ppermute | solution.py:75
  76.9 7.2 %collective-permute-start.25 = (bf16[48,1024]{1,0:T(8,128)(2,1)S(1)}, bf16[48,1024]{1,0:T(8,128)(2,1)S(1)}, u32[]{:S(2)}, u32[]{:S(2)}) collective-permute-start(bf16[48,1024]{1,0:T(8,128)(2,1)S(1)} %get-tuple-element.88), channel_id=1, source_target_pairs={{1,2},{2,1},{3,0},{0,3},{5,6},{6,5},{7,4},{4,7},{9,10},{10,9},{11,... | collective-permute-start | bytes 294920 | tf_op jit(solution)/shard_map/ppermute | solution.py:75
  78.5 5.6 %collective-permute-start.27 = (f32[2,56,128]{2,1,0:T(8,128)S(1)}, f32[2,56,128]{2,1,0:T(8,128)S(1)}, u32[]{:S(2)}, u32[]{:S(2)}) collective-permute-start(f32[2,56,128]{2,1,0:T(8,128)S(1)} %shard_map.184.refs_0_), channel_id=1, source_target_pairs={{0,4},{1,5},{2,6},{3,7},{4,0},{5,1},{6,2},{7,3},{8,12},{9,13},{10,... | collective-permute-start | bytes 172040 | tf_op jit(solution)/shard_map/ppermute | solution.py:652
  84.1 5.2 %collective-permute-start.28 = (f32[2,56,128]{2,1,0:T(8,128)S(1)}, f32[2,56,128]{2,1,0:T(8,128)S(1)}, u32[]{:S(2)}, u32[]{:S(2)}) collective-permute-start(f32[2,56,128]{2,1,0:T(8,128)S(1)} %shard_map.185.refs_0_), channel_id=1, source_target_pairs={{0,2},{1,3},{2,0},{3,1},{4,6},{5,7},{6,4},{7,5},{8,10},{9,11},{10,... | collective-permute-start | bytes 172040 | tf_op jit(solution)/shard_map/ppermute | solution.py:652
  (9 other events, 114.2 us)

commit v6 on v5

--- a/solution.py
+++ b/solution.py
@@ -377,29 +377,23 @@
     )
 
 
-def hidden_far(normed, upstream, params, shards, early, near_sum, units):
+def hidden_far(normed, upstream, params, shards, near_sums, units):
     pixels, width = normed[0].shape
     arrays, slots = arrays_of(shards)
-    members, count = len(normed), len(arrays)
-    half = members // 2
-    rows, every, late = half * pixels, len(shards) * units, (len(shards) - early) * units
+    members, count, every = len(normed), len(arrays), len(shards) * units
+    rows = members * pixels
 
     def body(*refs):
         normed_refs, up_refs, params_ref = refs[:members], refs[members : 2 * members], refs[2 * members]
         shard_refs, rest = refs[2 * members + 1 : 2 * members + 1 + count], refs[2 * members + 1 + count :]
-        sum_ref, near_hid, far_hid, stay, send = rest[:5]
-        win, wout, late_in, late_out = rest[5:9]
-        near_norm, near_back, near_pre, near_slope, near_bpre = rest[9:14]
-        norm, back, pre, slope, bpre = rest[14:]
-        starts = [start for _, start in upstream]
-        place_rows(near_norm, near_back, normed_refs[:half], up_refs[:half], starts[:half], params_ref)
-        place_rows(norm, back, normed_refs[half:], up_refs[half:], starts[half:], params_ref)
+        sum_refs, rest = rest[: len(near_sums)], rest[len(near_sums) :]
+        hid, stay, send, win, wout, norm, back, pre, slope, bpre = rest
+        place_rows(norm, back, normed_refs, up_refs, [start for _, start in upstream], params_ref)
         line = place_weights(win, wout, shard_refs, slots, units)
-        late_line = place_weights(late_in, late_out, shard_refs, slots[early:], units)
-        far = hidden_block(norm, back, win, wout, line, far_hid, pre, slope, bpre)
-        near = sum_ref[...] + hidden_block(
-            near_norm, near_back, late_in, late_out, late_line, near_hid, near_pre, near_slope, near_bpre
-        )
+        far = hidden_block(norm, back, win, wout, line, hid, pre, slope, bpre)
+        near = sum_refs[0][...]
+        for ref in sum_refs[1:]:
+            near = near + ref[...]
         stay[:pixels] = near[:pixels]
         stay[pixels:] = far[:pixels]
         send[:pixels] = near[pixels:].astype(BF16)
@@ -407,18 +401,10 @@
 
     return call(
         body,
-        [
-            shape((rows, late), BF16),
-            shape((rows, every), BF16),
-            shape((rows, width), F32),
-            shape((rows, width), BF16),
-        ],
-        weight_scratch(every, width)
-        + weight_scratch(late, width)
-        + hidden_scratch(rows, late, width)
-        + hidden_scratch(rows, every, width),
-        [*normed, *[array for array, _ in upstream], params, *arrays, near_sum],
-        size=9000000,
+        [shape((rows, every), BF16), shape((rows, width), F32), shape((rows, width), BF16)],
+        weight_scratch(every, width) + hidden_scratch(rows, every, width),
+        [*normed, *[array for array, _ in upstream], params, *arrays, *near_sums],
+        size=8000000,
         limit=28,
     )
 
@@ -911,8 +897,9 @@
         near_hidden, near_sum = hidden_near([acts, near_acts], chip, params, shards[:early], units)
     normed = [acts, near_acts, far_acts, tile_swap(far_acts, 1)]
     upstreams = [*chip, (far_upstream, 0), (tile_swap(far_upstream, 1), 0)]
-    late_hidden, far_hidden, back_own, back_send = hidden_far(
-        normed, upstreams, params, shards, early, near_sum, units
+    late_hidden, late_sum = hidden_near(normed[:2], chip, params, shards[early:], units)
+    far_hidden, back_own, back_send = hidden_far(
+        normed[2:], upstreams[2:], params, shards, [near_sum, late_sum], units
     )
     hiddens = [near_hidden, late_hidden, far_hidden]
 

time: 90.1 us -> 89.2 us (0.990)
    pallas_call x24 -> x25, Pallas kernels: 19.1 us -> 19.1 us  [call(): pl.pallas_call(body, out_shape=outs, in_specs=[VMEM] * len(args), out_spe...]
  transfers between devices with their start and end apart: 29 -> 29, of which waited for: 12 -> 12; matrix products, arithmetic and copies ran while one was open for 0% -> 0% of each run, Pallas kernels for 17% -> 18%
where the time goes in v6:
time: 89.2 us; the launch traced here: 89 us
  starting transfers between devices  34.3 us (38%)
  waiting for transfers between devices  31.1 us (35%)
  Pallas kernels  22 us (25%)
    ppermute x14, waiting for transfers between devices, tile_swap(): lax.ppermute(block, 'tile', [(i, i ^ bits) for i in range(lax.axis_size('...  21.1 us
    pallas_call x25, Pallas kernels, call(): pl.pallas_call(body, out_shape=outs, in_specs=[VMEM] * len(args), out_spe...  19.1 us
    ppermute x14, starting transfers between devices, tile_swap(): lax.ppermute(block, 'tile', [(i, i ^ bits) for i in range(lax.axis_size('...  17.1 us
    ppermute x10, starting transfers between devices, across(): return lax.ppermute(block, 'dp', [(i, i ^ bits) for i in range(groups)])  11.7 us
    ppermute x10, waiting for transfers between devices, across(): return lax.ppermute(block, 'dp', [(i, i ^ bits) for i in range(groups)])  8.94 us
    ppermute x4, starting transfers between devices, swap_cols(): moved.append(lax.ppermute(block, 'tile', route))  3.4 us
    pallas_call x1, Pallas kernels, first_sends(): pl.pallas_call(body, out_shape=outs, in_specs=[VMEM] + [far] * (len(args)...  2.91 us
    ppermute x1, starting transfers between devices, swap_rows(): moved.append(lax.ppermute(block, 'tile', route))  2.13 us
  transfers between devices with their start and end apart: 29, of which 12 were waited for; matrix products, arithmetic and copies ran while one was open for 0% of the time, Pallas kernels for 18%

profile of v6, /device:TPU:0, one launch (start us, length us, event | category | flops | bytes accessed | tf_op | source)
XLA Modules:
  0.0 89.0 jit_solution(16813247192907839025)
XLA Ops:
  0.7 2.9 %shard_map.162 = (bf16[224,1024]{1,0:T(8,128)(2,1)}, bf16[248,1024]{1,0:T(8,128)(2,1)}, f32[2,56,128]{2,1,0:T(8,128)}) custom-call(bf16[1,96]{1,0:T(2,128)(2,1)} %bitcast.32, bf16[128,1024]{1,0:T(8,128)(2,1)} %bitcast.21, bf16[96,1024]{1,0:T(8,128)(2,1)} %in_ref.1, bf16[96,1024]{1,0:T(8,128)(2,1)} %out_ref.1, f32[49,256]{1,0:T(8,128)} %kernel_ref.1, ...), custom_call_target="tpu_custom_call" | custom-call | flops 10000 | bytes 1000000 | tf_op jit(solution)/shard_map/pallas_call | solution.py:780
  3.6 4.1 %collective-permute-start = (bf16[248,1024]{1,0:T(8,128)(2,1)}, bf16[248,1024]{1,0:T(8,128)(2,1)S(1)}, u32[]{:S(2)}, u32[]{:S(2)}) collective-permute-start(bf16[248,1024]{1,0:T(8,128)(2,1)} %get-tuple-element.53), channel_id=1, source_target_pairs={{0,4},{1,5},{2,6},{3,7},{4,0},{5,1},{6,2},{7,3},{8,12},{9,13},{10,... | collective-permute-start | bytes 1523720 | tf_op jit(solution)/shard_map/ppermute | solution.py:638
  7.7 2.4 %collective-permute-start.4 = (bf16[224,1024]{1,0:T(8,128)(2,1)}, bf16[224,1024]{1,0:T(8,128)(2,1)S(1)}, u32[]{:S(2)}, u32[]{:S(2)}) collective-permute-start(bf16[224,1024]{1,0:T(8,128)(2,1)} %get-tuple-element.54.refs_5_.refs_4_), channel_id=1, source_target_pairs={{0,24},{8,16},{16,8},{24,0},{1,25},{9,17},{17,9},{25,1},{2,26},{10... | collective-permute-start | bytes 1376264 | tf_op jit(solution)/shard_map/ppermute | solution.py:634
  11.2 1.6 %collective-permute-start.1 = (bf16[128,1024]{1,0:T(8,128)(2,1)}, bf16[128,1024]{1,0:T(8,128)(2,1)S(1)}, u32[]{:S(2)}, u32[]{:S(2)}) collective-permute-start(bf16[128,1024]{1,0:T(8,128)(2,1)} %bitcast.14), channel_id=1, source_target_pairs={{0,2},{1,3},{2,0},{3,1},{4,6},{5,7},{6,4},{7,5},{8,10},{9,11},{10,... | collective-permute-start | bytes 786440 | tf_op jit(solution)/shard_map/ppermute | solution.py:638
  12.8 11.7 %collective-permute-done.1.refs_2_ = bf16[128,1024]{1,0:T(8,128)(2,1)S(1)} collective-permute-done((bf16[128,1024]{1,0:T(8,128)(2,1)}, bf16[128,1024]{1,0:T(8,128)(2,1)S(1)}, u32[]{:S(2)}, u32[]{:S(2)}) %collective-permute-start.1) | collective-permute-done | bytes 262176 | tf_op jit(solution)/shard_map/ppermute | solution.py:638
  24.5 6.1 %collective-permute-done.3.refs_1_.refs_7_.refs_6_ = bf16[224,1024]{1,0:T(8,128)(2,1)S(1)} collective-permute-done((bf16[224,1024]{1,0:T(8,128)(2,1)}, bf16[224,1024]{1,0:T(8,128)(2,1)S(1)}, u32[]{:S(2)}, u32[]{:S(2)}) %collective-permute-start.3) | collective-permute-done | bytes 458784 | tf_op jit(solution)/shard_map/ppermute | solution.py:634
  30.7 1.5 %collective-permute-start.10 = (bf16[200,1024]{1,0:T(8,128)(2,1)S(1)}, bf16[200,1024]{1,0:T(8,128)(2,1)S(1)}, u32[]{:S(2)}, u32[]{:S(2)}) collective-permute-start(bf16[200,1024]{1,0:T(8,128)(2,1)S(1)} %shard_map.168.refs_9_.refs_8_), channel_id=1, source_target_pairs={{0,16},{8,24},{16,0},{24,8},{1,17},{9,25},{17,1},{25,9},{2,18},{10... | collective-permute-start | bytes 1228808 | tf_op jit(solution)/shard_map/ppermute | solution.py:634
  35.1 2.6 %shard_map.165 = (f32[8,448,128]{2,1,0:T(8,128)S(1)}, f32[8,128,128]{2,1,0:T(8,128)S(1)}) custom-call(bf16[128,1024]{1,0:T(8,128)(2,1)S(1)} %bitcast.23, bf16[48,1024]{1,0:T(8,128)(2,1)S(1)} %shard_map.163.refs_1_.refs_0_, f32[8,56,128]{2,1,0:T(8,128)S(1)} %shard_map.164.refs_2_.params_ref.refs_4_), custom_call_target="tpu_custom_call" | custom-call | bytes 8000000 | tf_op jit(solution)/shard_map/pallas_call | solution.py:26
  42.1 1.6 %collective-permute-start.12 = (bf16[104,1024]{1,0:T(8,128)(2,1)S(1)}, bf16[104,1024]{1,0:T(8,128)(2,1)S(1)}, u32[]{:S(2)}, u32[]{:S(2)}) collective-permute-start(bf16[104,1024]{1,0:T(8,128)(2,1)S(1)} %shard_map.171), channel_id=1, source_target_pairs={{0,8},{8,0},{16,24},{24,16},{1,9},{9,1},{17,25},{25,17},{2,10},{10... | collective-permute-start | bytes 638984 | tf_op jit(solution)/shard_map/ppermute | solution.py:634
  45.1 2.1 %shard_map.169 = (bf16[256,672]{1,0:T(8,128)(2,1)S(1)}, f32[256,1024]{1,0:T(8,128)S(1)}) custom-call(bf16[128,1024]{1,0:T(8,128)(2,1)S(1)} %get-tuple-element.63.refs_0_, bf16[128,1024]{1,0:T(8,128)(2,1)S(1)} %collective-permute-done.7.refs_1_, bf16[128,1024]{1,0:T(8,128)(2,1)S(1)} %bitcast.16, bf16[128,1024]{1,0:T(8,128)(2,1)S(1)} %collective-permute-done.8.refs_3_.refs_1_, ...), custom_call_target="tpu_custom_call" | custom-call | bytes 7000000 | tf_op jit(solution)/shard_map/pallas_call | solution.py:26
  47.1 1.6 %collective-permute-done.13.refs_0_ = bf16[128,1024]{1,0:T(8,128)(2,1)S(1)} collective-permute-done((bf16[128,1024]{1,0:T(8,128)(2,1)S(1)}, bf16[128,1024]{1,0:T(8,128)(2,1)S(1)}, u32[]{:S(2)}, u32[]{:S(2)}) %collective-permute-start.13) | collective-permute-done | bytes 262176 | tf_op jit(solution)/shard_map/ppermute | solution.py:638
  51.0 2.1 %shard_map.174 = (bf16[256,768]{1,0:T(8,128)(2,1)S(1)}, f32[256,1024]{1,0:T(8,128)S(1)}, bf16[256,1024]{1,0:T(8,128)(2,1)S(1)}) custom-call(bf16[128,1024]{1,0:T(8,128)(2,1)S(1)} %collective-permute-done.13.refs_0_, bf16[128,1024]{1,0:T(8,128)(2,1)S(1)} %collective-permute-done.14.refs_1_, bf16[128,1024]{1,0:T(8,128)(2,1)S(1)} %collective-permute-done.1.refs_2_, ...), custom_call_target="tpu_custom_call" | custom-call | bytes 8000000 | tf_op jit(solution)/shard_map/pallas_call | solution.py:26
  55.1 1.6 %collective-permute-start.18 = (bf16[128,1024]{1,0:T(8,128)(2,1)S(1)}, bf16[128,1024]{1,0:T(8,128)(2,1)S(1)}, u32[]{:S(2)}, u32[]{:S(2)}) collective-permute-start(bf16[128,1024]{1,0:T(8,128)(2,1)S(1)} %shard_map.177), channel_id=1, source_target_pairs={{0,2},{1,3},{2,0},{3,1},{4,6},{5,7},{6,4},{7,5},{8,10},{9,11},{10,... | collective-permute-start | bytes 786440 | tf_op jit(solution)/shard_map/ppermute | solution.py:638
  56.8 6.8 %collective-permute-done.18.far_ref = bf16[128,1024]{1,0:T(8,128)(2,1)S(1)} collective-permute-done((bf16[128,1024]{1,0:T(8,128)(2,1)S(1)}, bf16[128,1024]{1,0:T(8,128)(2,1)S(1)}, u32[]{:S(2)}, u32[]{:S(2)}) %collective-permute-start.18) | collective-permute-done | bytes 262176 | tf_op jit(solution)/shard_map/ppermute | solution.py:638
  64.0 2.0 %shard_map.179 = (f32[2,56,128]{2,1,0:T(8,128)S(1)}, f32[2,56,128]{2,1,0:T(8,128)S(1)}, f32[2,56,128]{2,1,0:T(8,128)S(1)}, f32[2,56,128]{2,1,0:T(8,128)S(1)}) custom-call(f32[8,448,128]{2,1,0:T(8,128)S(1)} %shard_map.173.padded_ref, f32[8,128,128]{2,1,0:T(8,128)S(1)} %get-tuple-element.78.conv, f32[8,8,128]{2,1,0:T(8,128)S(1)} %get-tuple-element.79.vectors_ref, ...), custom_call_target="tpu_custom_call" | custom-call | bytes 7380000 | tf_op jit(solution)/shard_map/pallas_call | solution.py:26
  66.7 1.4 %collective-permute-start.20 = (f32[2,56,128]{2,1,0:T(8,128)S(1)}, f32[2,56,128]{2,1,0:T(8,128)S(1)}, u32[]{:S(2)}, u32[]{:S(2)}) collective-permute-start(f32[2,56,128]{2,1,0:T(8,128)S(1)} %get-tuple-element.83), channel_id=1, source_target_pairs={{0,16},{8,24},{16,0},{24,8},{1,17},{9,25},{17,1},{25,9},{2,18},{10... | collective-permute-start | bytes 172040 | tf_op jit(solution)/shard_map/ppermute | solution.py:634
  69.6 2.1 %collective-permute-start.23 = (bf16[48,1024]{1,0:T(8,128)(2,1)S(1)}, bf16[48,1024]{1,0:T(8,128)(2,1)S(1)}, u32[]{:S(2)}, u32[]{:S(2)}) collective-permute-start(bf16[48,1024]{1,0:T(8,128)(2,1)S(1)} %get-tuple-element.88), channel_id=1, source_target_pairs={{0,4},{4,0},{1,5},{5,1},{2,6},{6,2},{3,7},{7,3},{8,12},{12,8},{9,1... | collective-permute-start | bytes 294920 | tf_op jit(solution)/shard_map/ppermute | solution.py:61
  71.8 1.5 %collective-permute-done.21.refs_3_ = f32[2,56,128]{2,1,0:T(8,128)S(1)} collective-permute-done((f32[2,56,128]{2,1,0:T(8,128)S(1)}, f32[2,56,128]{2,1,0:T(8,128)S(1)}, u32[]{:S(2)}, u32[]{:S(2)}) %collective-permute-start.21) | collective-permute-done | bytes 57376 | tf_op jit(solution)/shard_map/ppermute | solution.py:634
  73.3 1.6 %collective-permute-start.22 = (bf16[128,1024]{1,0:T(8,128)(2,1)S(1)}, bf16[128,1024]{1,0:T(8,128)(2,1)S(1)}, u32[]{:S(2)}, u32[]{:S(2)}) collective-permute-start(bf16[128,1024]{1,0:T(8,128)(2,1)S(1)} %shard_map.176), channel_id=1, source_target_pairs={{0,2},{1,3},{2,0},{3,1},{4,6},{5,7},{6,4},{7,5},{8,10},{9,11},{10,... | collective-permute-start | bytes 786440 | tf_op jit(solution)/shard_map/ppermute | solution.py:638
  76.0 1.6 %collective-permute-start.25 = (bf16[48,1024]{1,0:T(8,128)(2,1)S(1)}, bf16[48,1024]{1,0:T(8,128)(2,1)S(1)}, u32[]{:S(2)}, u32[]{:S(2)}) collective-permute-start(bf16[48,1024]{1,0:T(8,128)(2,1)S(1)} %get-tuple-element.90), channel_id=1, source_target_pairs={{1,2},{2,1},{3,0},{0,3},{5,6},{6,5},{7,4},{4,7},{9,10},{10,9},{11,... | collective-permute-start | bytes 294920 | tf_op jit(solution)/shard_map/ppermute | solution.py:75
  77.6 3.0 %collective-permute-start.27 = (f32[2,56,128]{2,1,0:T(8,128)S(1)}, f32[2,56,128]{2,1,0:T(8,128)S(1)}, u32[]{:S(2)}, u32[]{:S(2)}) collective-permute-start(f32[2,56,128]{2,1,0:T(8,128)S(1)} %shard_map.185.refs_0_), channel_id=1, source_target_pairs={{0,4},{1,5},{2,6},{3,7},{4,0},{5,1},{6,2},{7,3},{8,12},{9,13},{10,... | collective-permute-start | bytes 172040 | tf_op jit(solution)/shard_map/ppermute | solution.py:638
  80.5 2.6 %shard_map.182.partial_ref = f32[8,128,128]{2,1,0:T(8,128)S(1)} custom-call(bf16[128,1024]{1,0:T(8,128)(2,1)S(1)} %get-tuple-element.86.refs_0_.field_ref, bf16[48,1024]{1,0:T(8,128)(2,1)S(1)} %collective-permute-done.23.refs_1_.refs_0_, f32[8,56,128]{2,1,0:T(8,128)S(1)} %shard_map.164.refs_2_.params_ref.refs_4_, bf16[128,1024]{1,0:T(8,128)(2,1)S(1)} %bitcast.20), custom_call_target="tpu_custom_call" | custom-call | bytes 8000000 | tf_op jit(solution)/shard_map/pallas_call | solution.py:26
  83.2 2.5 %collective-permute-start.28 = (f32[2,56,128]{2,1,0:T(8,128)S(1)}, f32[2,56,128]{2,1,0:T(8,128)S(1)}, u32[]{:S(2)}, u32[]{:S(2)}) collective-permute-start(f32[2,56,128]{2,1,0:T(8,128)S(1)} %shard_map.186.refs_0_), channel_id=1, source_target_pairs={{0,2},{1,3},{2,0},{3,1},{4,6},{5,7},{6,4},{7,5},{8,10},{9,11},{10,... | collective-permute-start | bytes 172040 | tf_op jit(solution)/shard_map/ppermute | solution.py:638
  85.7 1.7 %shard_map.184 = bf16[128,1024]{1,0:T(8,128)(2,1)} custom-call(f32[8,128,128]{2,1,0:T(8,128)S(1)} %shard_map.182.partial_ref, bf16[48,1024]{1,0:T(8,128)(2,1)S(1)} %collective-permute-done.24.first_ref, bf16[48,1024]{1,0:T(8,128)(2,1)S(1)} %collective-permute-done.25.second_ref, f32[8,56,128]{2,1,0:T(8,128)S(1)} %shard_map.164.refs_2_.params_ref.refs_4_), custom_call_target="tpu_custom_call" | custom-call | bytes 5000000 | tf_op jit(solution)/shard_map/pallas_call | solution.py:26
  (68 shorter events, 19.3 us)
Async XLA Ops:
  3.6 27.1 %collective-permute-start = (bf16[248,1024]{1,0:T(8,128)(2,1)}, bf16[248,1024]{1,0:T(8,128)(2,1)S(1)}, u32[]{:S(2)}, u32[]{:S(2)}) collective-permute-start(bf16[248,1024]{1,0:T(8,128)(2,1)} %get-tuple-element.53), channel_id=1, source_target_pairs={{0,4},{1,5},{2,6},{3,7},{4,0},{5,1},{6,2},{7,3},{8,12},{9,13},{10,... | collective-permute-start | bytes 1523720 | tf_op jit(solution)/shard_map/ppermute | solution.py:638
  7.7 16.8 %collective-permute-start.4 = (bf16[224,1024]{1,0:T(8,128)(2,1)}, bf16[224,1024]{1,0:T(8,128)(2,1)S(1)}, u32[]{:S(2)}, u32[]{:S(2)}) collective-permute-start(bf16[224,1024]{1,0:T(8,128)(2,1)} %get-tuple-element.54.refs_5_.refs_4_), channel_id=1, source_target_pairs={{0,24},{8,16},{16,8},{24,0},{1,25},{9,17},{17,9},{25,1},{2,26},{10... | collective-permute-start | bytes 1376264 | tf_op jit(solution)/shard_map/ppermute | solution.py:634
  10.1 20.5 %collective-permute-start.3 = (bf16[224,1024]{1,0:T(8,128)(2,1)}, bf16[224,1024]{1,0:T(8,128)(2,1)S(1)}, u32[]{:S(2)}, u32[]{:S(2)}) collective-permute-start(bf16[224,1024]{1,0:T(8,128)(2,1)} %get-tuple-element.54.refs_5_.refs_4_), channel_id=1, source_target_pairs={{0,16},{8,24},{16,0},{24,8},{1,17},{9,25},{17,1},{25,9},{2,18},{10... | collective-permute-start | bytes 1376264 | tf_op jit(solution)/shard_map/ppermute | solution.py:634
  10.6 20.1 %collective-permute-start.2 = (bf16[224,1024]{1,0:T(8,128)(2,1)}, bf16[224,1024]{1,0:T(8,128)(2,1)S(1)}, u32[]{:S(2)}, u32[]{:S(2)}) collective-permute-start(bf16[224,1024]{1,0:T(8,128)(2,1)} %get-tuple-element.54.refs_5_.refs_4_), channel_id=1, source_target_pairs={{0,8},{8,0},{16,24},{24,16},{1,9},{9,1},{17,25},{25,17},{2,10},{10... | collective-permute-start | bytes 1376264 | tf_op jit(solution)/shard_map/ppermute | solution.py:634
  11.2 13.3 %collective-permute-start.1 = (bf16[128,1024]{1,0:T(8,128)(2,1)}, bf16[128,1024]{1,0:T(8,128)(2,1)S(1)}, u32[]{:S(2)}, u32[]{:S(2)}) collective-permute-start(bf16[128,1024]{1,0:T(8,128)(2,1)} %bitcast.14), channel_id=1, source_target_pairs={{0,2},{1,3},{2,0},{3,1},{4,6},{5,7},{6,4},{7,5},{8,10},{9,11},{10,... | collective-permute-start | bytes 786440 | tf_op jit(solution)/shard_map/ppermute | solution.py:638
  30.7 11.4 %collective-permute-start.10 = (bf16[200,1024]{1,0:T(8,128)(2,1)S(1)}, bf16[200,1024]{1,0:T(8,128)(2,1)S(1)}, u32[]{:S(2)}, u32[]{:S(2)}) collective-permute-start(bf16[200,1024]{1,0:T(8,128)(2,1)S(1)} %shard_map.168.refs_9_.refs_8_), channel_id=1, source_target_pairs={{0,16},{8,24},{16,0},{24,8},{1,17},{9,25},{17,1},{25,9},{2,18},{10... | collective-permute-start | bytes 1228808 | tf_op jit(solution)/shard_map/ppermute | solution.py:634
  32.2 11.4 %collective-permute-start.9 = (bf16[200,1024]{1,0:T(8,128)(2,1)S(1)}, bf16[200,1024]{1,0:T(8,128)(2,1)S(1)}, u32[]{:S(2)}, u32[]{:S(2)}) collective-permute-start(bf16[200,1024]{1,0:T(8,128)(2,1)S(1)} %shard_map.168.refs_9_.refs_8_), channel_id=1, source_target_pairs={{0,8},{8,0},{16,24},{24,16},{1,9},{9,1},{17,25},{25,17},{2,10},{10... | collective-permute-start | bytes 1228808 | tf_op jit(solution)/shard_map/ppermute | solution.py:634
  35.0 9.3 %collective-permute-start.8 = (bf16[128,1024]{1,0:T(8,128)(2,1)S(1)}, bf16[128,1024]{1,0:T(8,128)(2,1)S(1)}, u32[]{:S(2)}, u32[]{:S(2)}) collective-permute-start(bf16[128,1024]{1,0:T(8,128)(2,1)S(1)} %bitcast.15), channel_id=1, source_target_pairs={{0,1},{1,0},{2,3},{3,2},{4,5},{5,4},{6,7},{7,6},{8,9},{9,8},{10,11... | collective-permute-start | bytes 786440 | tf_op jit(solution)/shard_map/ppermute | solution.py:638
  39.7 4.7 %collective-permute-start.7 = (bf16[128,1024]{1,0:T(8,128)(2,1)S(1)}, bf16[128,1024]{1,0:T(8,128)(2,1)S(1)}, u32[]{:S(2)}, u32[]{:S(2)}) collective-permute-start(bf16[128,1024]{1,0:T(8,128)(2,1)S(1)} %get-tuple-element.63.refs_0_), channel_id=1, source_target_pairs={{0,1},{1,0},{2,3},{3,2},{4,5},{5,4},{6,7},{7,6},{8,9},{9,8},{10,11... | collective-permute-start | bytes 786440 | tf_op jit(solution)/shard_map/ppermute | solution.py:638
  40.5 8.3 %collective-permute-start.13 = (bf16[128,1024]{1,0:T(8,128)(2,1)S(1)}, bf16[128,1024]{1,0:T(8,128)(2,1)S(1)}, u32[]{:S(2)}, u32[]{:S(2)}) collective-permute-start(bf16[128,1024]{1,0:T(8,128)(2,1)S(1)} %get-tuple-element.63.refs_0_), channel_id=1, source_target_pairs={{0,2},{1,3},{2,0},{3,1},{4,6},{5,7},{6,4},{7,5},{8,10},{9,11},{10,... | collective-permute-start | bytes 786440 | tf_op jit(solution)/shard_map/ppermute | solution.py:638
  42.1 7.3 %collective-permute-start.12 = (bf16[104,1024]{1,0:T(8,128)(2,1)S(1)}, bf16[104,1024]{1,0:T(8,128)(2,1)S(1)}, u32[]{:S(2)}, u32[]{:S(2)}) collective-permute-start(bf16[104,1024]{1,0:T(8,128)(2,1)S(1)} %shard_map.171), channel_id=1, source_target_pairs={{0,8},{8,0},{16,24},{24,16},{1,9},{9,1},{17,25},{25,17},{2,10},{10... | collective-permute-start | bytes 638984 | tf_op jit(solution)/shard_map/ppermute | solution.py:634
  43.7 5.7 %collective-permute-start.11 = (bf16[96,1024]{1,0:T(8,128)(2,1)S(1)}, bf16[96,1024]{1,0:T(8,128)(2,1)S(1)}, u32[]{:S(2)}, u32[]{:S(2)}) collective-permute-start(bf16[96,1024]{1,0:T(8,128)(2,1)S(1)} %shard_map.170), channel_id=1, source_target_pairs={{0,16},{8,24},{16,0},{24,8},{1,17},{9,25},{17,1},{25,9},{2,18},{10... | collective-permute-start | bytes 589832 | tf_op jit(solution)/shard_map/ppermute | solution.py:634
  44.3 6.0 %collective-permute-start.15 = (bf16[128,1024]{1,0:T(8,128)(2,1)S(1)}, bf16[128,1024]{1,0:T(8,128)(2,1)S(1)}, u32[]{:S(2)}, u32[]{:S(2)}) collective-permute-start(bf16[128,1024]{1,0:T(8,128)(2,1)S(1)} %collective-permute-done.1.refs_2_), channel_id=1, source_target_pairs={{0,1},{1,0},{2,3},{3,2},{4,5},{5,4},{6,7},{7,6},{8,9},{9,8},{10,11... | collective-permute-start | bytes 786440 | tf_op jit(solution)/shard_map/ppermute | solution.py:638
  54.4 17.4 %collective-permute-start.16 = (bf16[256,1024]{1,0:T(8,128)(2,1)S(1)}, bf16[256,1024]{1,0:T(8,128)(2,1)S(1)}, u32[]{:S(2)}, u32[]{:S(2)}) collective-permute-start(bf16[256,1024]{1,0:T(8,128)(2,1)S(1)} %get-tuple-element.73), channel_id=1, source_target_pairs={{0,1},{1,0},{2,3},{3,2},{4,5},{5,4},{6,7},{7,6},{8,9},{9,8},{10,11... | collective-permute-start | bytes 1572872 | tf_op jit(solution)/shard_map/ppermute | solution.py:638
  55.1 8.4 %collective-permute-start.18 = (bf16[128,1024]{1,0:T(8,128)(2,1)S(1)}, bf16[128,1024]{1,0:T(8,128)(2,1)S(1)}, u32[]{:S(2)}, u32[]{:S(2)}) collective-permute-start(bf16[128,1024]{1,0:T(8,128)(2,1)S(1)} %shard_map.177), channel_id=1, source_target_pairs={{0,2},{1,3},{2,0},{3,1},{4,6},{5,7},{6,4},{7,5},{8,10},{9,11},{10,... | collective-permute-start | bytes 786440 | tf_op jit(solution)/shard_map/ppermute | solution.py:638
  66.1 5.7 %collective-permute-start.19 = (f32[2,56,128]{2,1,0:T(8,128)S(1)}, f32[2,56,128]{2,1,0:T(8,128)S(1)}, u32[]{:S(2)}, u32[]{:S(2)}) collective-permute-start(f32[2,56,128]{2,1,0:T(8,128)S(1)} %get-tuple-element.82), channel_id=1, source_target_pairs={{0,8},{8,0},{16,24},{24,16},{1,9},{9,1},{17,25},{25,17},{2,10},{10... | collective-permute-start | bytes 172040 | tf_op jit(solution)/shard_map/ppermute | solution.py:634
  66.7 5.1 %collective-permute-start.20 = (f32[2,56,128]{2,1,0:T(8,128)S(1)}, f32[2,56,128]{2,1,0:T(8,128)S(1)}, u32[]{:S(2)}, u32[]{:S(2)}) collective-permute-start(f32[2,56,128]{2,1,0:T(8,128)S(1)} %get-tuple-element.83), channel_id=1, source_target_pairs={{0,16},{8,24},{16,0},{24,8},{1,17},{9,25},{17,1},{25,9},{2,18},{10... | collective-permute-start | bytes 172040 | tf_op jit(solution)/shard_map/ppermute | solution.py:634
  68.2 5.1 %collective-permute-start.21 = (f32[2,56,128]{2,1,0:T(8,128)S(1)}, f32[2,56,128]{2,1,0:T(8,128)S(1)}, u32[]{:S(2)}, u32[]{:S(2)}) collective-permute-start(f32[2,56,128]{2,1,0:T(8,128)S(1)} %get-tuple-element.84), channel_id=1, source_target_pairs={{0,24},{8,16},{16,8},{24,0},{1,25},{9,17},{17,9},{25,1},{2,26},{10... | collective-permute-start | bytes 172040 | tf_op jit(solution)/shard_map/ppermute | solution.py:634
  69.6 5.6 %collective-permute-start.23 = (bf16[48,1024]{1,0:T(8,128)(2,1)S(1)}, bf16[48,1024]{1,0:T(8,128)(2,1)S(1)}, u32[]{:S(2)}, u32[]{:S(2)}) collective-permute-start(bf16[48,1024]{1,0:T(8,128)(2,1)S(1)} %get-tuple-element.88), channel_id=1, source_target_pairs={{0,4},{4,0},{1,5},{5,1},{2,6},{6,2},{3,7},{7,3},{8,12},{12,8},{9,1... | collective-permute-start | bytes 294920 | tf_op jit(solution)/shard_map/ppermute | solution.py:61
  73.3 14.2 %collective-permute-start.22 = (bf16[128,1024]{1,0:T(8,128)(2,1)S(1)}, bf16[128,1024]{1,0:T(8,128)(2,1)S(1)}, u32[]{:S(2)}, u32[]{:S(2)}) collective-permute-start(bf16[128,1024]{1,0:T(8,128)(2,1)S(1)} %shard_map.176), channel_id=1, source_target_pairs={{0,2},{1,3},{2,0},{3,1},{4,6},{5,7},{6,4},{7,5},{8,10},{9,11},{10,... | collective-permute-start | bytes 786440 | tf_op jit(solution)/shard_map/ppermute | solution.py:638
  75.4 7.7 %collective-permute-start.24 = (bf16[48,1024]{1,0:T(8,128)(2,1)S(1)}, bf16[48,1024]{1,0:T(8,128)(2,1)S(1)}, u32[]{:S(2)}, u32[]{:S(2)}) collective-permute-start(bf16[48,1024]{1,0:T(8,128)(2,1)S(1)} %get-tuple-element.89), channel_id=1, source_target_pairs={{0,1},{1,0},{2,3},{3,2},{4,5},{5,4},{6,7},{7,6},{8,9},{9,8},{10,11... | collective-permute-start | bytes 294920 | tf_op jit(solution)/shard_map/ppermute | solution.py:75
  76.0 7.2 %collective-permute-start.25 = (bf16[48,1024]{1,0:T(8,128)(2,1)S(1)}, bf16[48,1024]{1,0:T(8,128)(2,1)S(1)}, u32[]{:S(2)}, u32[]{:S(2)}) collective-permute-start(bf16[48,1024]{1,0:T(8,128)(2,1)S(1)} %get-tuple-element.90), channel_id=1, source_target_pairs={{1,2},{2,1},{3,0},{0,3},{5,6},{6,5},{7,4},{4,7},{9,10},{10,9},{11,... | collective-permute-start | bytes 294920 | tf_op jit(solution)/shard_map/ppermute | solution.py:75
  77.6 5.6 %collective-permute-start.27 = (f32[2,56,128]{2,1,0:T(8,128)S(1)}, f32[2,56,128]{2,1,0:T(8,128)S(1)}, u32[]{:S(2)}, u32[]{:S(2)}) collective-permute-start(f32[2,56,128]{2,1,0:T(8,128)S(1)} %shard_map.185.refs_0_), channel_id=1, source_target_pairs={{0,4},{1,5},{2,6},{3,7},{4,0},{5,1},{6,2},{7,3},{8,12},{9,13},{10,... | collective-permute-start | bytes 172040 | tf_op jit(solution)/shard_map/ppermute | solution.py:638
  83.2 5.2 %collective-permute-start.28 = (f32[2,56,128]{2,1,0:T(8,128)S(1)}, f32[2,56,128]{2,1,0:T(8,128)S(1)}, u32[]{:S(2)}, u32[]{:S(2)}) collective-permute-start(f32[2,56,128]{2,1,0:T(8,128)S(1)} %shard_map.186.refs_0_), channel_id=1, source_target_pairs={{0,2},{1,3},{2,0},{3,1},{4,6},{5,7},{6,4},{7,5},{8,10},{9,11},{10,... | collective-permute-start | bytes 172040 | tf_op jit(solution)/shard_map/ppermute | solution.py:638
  (9 other events, 114.2 us)

commit v7 on v6

--- a/solution.py
+++ b/solution.py
@@ -336,7 +336,7 @@
 
 
 def hidden_block(norm, back, win, wout, line, hid, pre, slope, bpre):
-    step = 32
+    step = 16
     across = (((1,), (1,)), ((), ()))
     pre[...] = lax.dot_general(norm[...], win[...], across, preferred_element_type=F32) + line
     slope[...] = lax.dot_general(back[...], wout[...], across, preferred_element_type=F32)

time: 89.2 us -> 89.3 us (level)
  transfers between devices with their start and end apart: 29 -> 29, of which waited for: 12 -> 12; matrix products, arithmetic and copies ran while one was open for 0% -> 0% of each run, Pallas kernels for 18% -> 19%
where the time goes in v7:
time: 89.3 us; the launch traced here: 89.1 us
  starting transfers between devices  34.3 us (38%)
  waiting for transfers between devices  30.8 us (34%)
  Pallas kernels  22.4 us (25%)
    ppermute x14, waiting for transfers between devices, tile_swap(): lax.ppermute(block, 'tile', [(i, i ^ bits) for i in range(lax.axis_size('...  20.9 us
    pallas_call x25, Pallas kernels, call(): pl.pallas_call(body, out_shape=outs, in_specs=[VMEM] * len(args), out_spe...  19.5 us
    ppermute x14, starting transfers between devices, tile_swap(): lax.ppermute(block, 'tile', [(i, i ^ bits) for i in range(lax.axis_size('...  17.1 us
    ppermute x10, starting transfers between devices, across(): return lax.ppermute(block, 'dp', [(i, i ^ bits) for i in range(groups)])  11.7 us
    ppermute x10, waiting for transfers between devices, across(): return lax.ppermute(block, 'dp', [(i, i ^ bits) for i in range(groups)])  8.94 us
    ppermute x4, starting transfers between devices, swap_cols(): moved.append(lax.ppermute(block, 'tile', route))  3.4 us
    pallas_call x1, Pallas kernels, first_sends(): pl.pallas_call(body, out_shape=outs, in_specs=[VMEM] + [far] * (len(args)...  2.91 us
    ppermute x1, starting transfers between devices, swap_rows(): moved.append(lax.ppermute(block, 'tile', route))  2.13 us
  transfers between devices with their start and end apart: 29, of which 12 were waited for; matrix products, arithmetic and copies ran while one was open for 0% of the time, Pallas kernels for 19%

profile of v7, /device:TPU:0, one launch (start us, length us, event | category | flops | bytes accessed | tf_op | source)
XLA Modules:
  0.0 89.1 jit_solution(2590780583555335228)
XLA Ops:
  0.7 2.9 %shard_map.162 = (bf16[224,1024]{1,0:T(8,128)(2,1)}, bf16[248,1024]{1,0:T(8,128)(2,1)}, f32[2,56,128]{2,1,0:T(8,128)}) custom-call(bf16[1,96]{1,0:T(2,128)(2,1)} %bitcast.32, bf16[128,1024]{1,0:T(8,128)(2,1)} %bitcast.21, bf16[96,1024]{1,0:T(8,128)(2,1)} %in_ref.1, bf16[96,1024]{1,0:T(8,128)(2,1)} %out_ref.1, f32[49,256]{1,0:T(8,128)} %kernel_ref.1, ...), custom_call_target="tpu_custom_call" | custom-call | flops 10000 | bytes 1000000 | tf_op jit(solution)/shard_map/pallas_call | solution.py:780
  3.6 4.1 %collective-permute-start = (bf16[248,1024]{1,0:T(8,128)(2,1)}, bf16[248,1024]{1,0:T(8,128)(2,1)S(1)}, u32[]{:S(2)}, u32[]{:S(2)}) collective-permute-start(bf16[248,1024]{1,0:T(8,128)(2,1)} %get-tuple-element.53), channel_id=1, source_target_pairs={{0,4},{1,5},{2,6},{3,7},{4,0},{5,1},{6,2},{7,3},{8,12},{9,13},{10,... | collective-permute-start | bytes 1523720 | tf_op jit(solution)/shard_map/ppermute | solution.py:638
  7.7 2.4 %collective-permute-start.4 = (bf16[224,1024]{1,0:T(8,128)(2,1)}, bf16[224,1024]{1,0:T(8,128)(2,1)S(1)}, u32[]{:S(2)}, u32[]{:S(2)}) collective-permute-start(bf16[224,1024]{1,0:T(8,128)(2,1)} %get-tuple-element.54.refs_5_.refs_4_), channel_id=1, source_target_pairs={{0,24},{8,16},{16,8},{24,0},{1,25},{9,17},{17,9},{25,1},{2,26},{10... | collective-permute-start | bytes 1376264 | tf_op jit(solution)/shard_map/ppermute | solution.py:634
  11.2 1.6 %collective-permute-start.1 = (bf16[128,1024]{1,0:T(8,128)(2,1)}, bf16[128,1024]{1,0:T(8,128)(2,1)S(1)}, u32[]{:S(2)}, u32[]{:S(2)}) collective-permute-start(bf16[128,1024]{1,0:T(8,128)(2,1)} %bitcast.14), channel_id=1, source_target_pairs={{0,2},{1,3},{2,0},{3,1},{4,6},{5,7},{6,4},{7,5},{8,10},{9,11},{10,... | collective-permute-start | bytes 786440 | tf_op jit(solution)/shard_map/ppermute | solution.py:638
  12.8 11.7 %collective-permute-done.1.refs_2_ = bf16[128,1024]{1,0:T(8,128)(2,1)S(1)} collective-permute-done((bf16[128,1024]{1,0:T(8,128)(2,1)}, bf16[128,1024]{1,0:T(8,128)(2,1)S(1)}, u32[]{:S(2)}, u32[]{:S(2)}) %collective-permute-start.1) | collective-permute-done | bytes 262176 | tf_op jit(solution)/shard_map/ppermute | solution.py:638
  24.5 6.1 %collective-permute-done.3.refs_1_.refs_7_.refs_6_ = bf16[224,1024]{1,0:T(8,128)(2,1)S(1)} collective-permute-done((bf16[224,1024]{1,0:T(8,128)(2,1)}, bf16[224,1024]{1,0:T(8,128)(2,1)S(1)}, u32[]{:S(2)}, u32[]{:S(2)}) %collective-permute-start.3) | collective-permute-done | bytes 458784 | tf_op jit(solution)/shard_map/ppermute | solution.py:634
  30.7 1.5 %collective-permute-start.10 = (bf16[200,1024]{1,0:T(8,128)(2,1)S(1)}, bf16[200,1024]{1,0:T(8,128)(2,1)S(1)}, u32[]{:S(2)}, u32[]{:S(2)}) collective-permute-start(bf16[200,1024]{1,0:T(8,128)(2,1)S(1)} %shard_map.168.refs_9_.refs_8_), channel_id=1, source_target_pairs={{0,16},{8,24},{16,0},{24,8},{1,17},{9,25},{17,1},{25,9},{2,18},{10... | collective-permute-start | bytes 1228808 | tf_op jit(solution)/shard_map/ppermute | solution.py:634
  35.1 2.6 %shard_map.165 = (f32[8,448,128]{2,1,0:T(8,128)S(1)}, f32[8,128,128]{2,1,0:T(8,128)S(1)}) custom-call(bf16[128,1024]{1,0:T(8,128)(2,1)S(1)} %bitcast.23, bf16[48,1024]{1,0:T(8,128)(2,1)S(1)} %shard_map.163.refs_1_.refs_0_, f32[8,56,128]{2,1,0:T(8,128)S(1)} %shard_map.164.refs_2_.params_ref.refs_4_), custom_call_target="tpu_custom_call" | custom-call | bytes 8000000 | tf_op jit(solution)/shard_map/pallas_call | solution.py:26
  42.1 1.6 %collective-permute-start.12 = (bf16[104,1024]{1,0:T(8,128)(2,1)S(1)}, bf16[104,1024]{1,0:T(8,128)(2,1)S(1)}, u32[]{:S(2)}, u32[]{:S(2)}) collective-permute-start(bf16[104,1024]{1,0:T(8,128)(2,1)S(1)} %shard_map.171), channel_id=1, source_target_pairs={{0,8},{8,0},{16,24},{24,16},{1,9},{9,1},{17,25},{25,17},{2,10},{10... | collective-permute-start | bytes 638984 | tf_op jit(solution)/shard_map/ppermute | solution.py:634
  45.1 2.2 %shard_map.169 = (bf16[256,672]{1,0:T(8,128)(2,1)S(1)}, f32[256,1024]{1,0:T(8,128)S(1)}) custom-call(bf16[128,1024]{1,0:T(8,128)(2,1)S(1)} %get-tuple-element.63.refs_0_, bf16[128,1024]{1,0:T(8,128)(2,1)S(1)} %collective-permute-done.7.refs_1_, bf16[128,1024]{1,0:T(8,128)(2,1)S(1)} %bitcast.16, bf16[128,1024]{1,0:T(8,128)(2,1)S(1)} %collective-permute-done.8.refs_3_.refs_1_, ...), custom_call_target="tpu_custom_call" | custom-call | bytes 7000000 | tf_op jit(solution)/shard_map/pallas_call | solution.py:26
  47.2 1.5 %collective-permute-done.13.refs_0_ = bf16[128,1024]{1,0:T(8,128)(2,1)S(1)} collective-permute-done((bf16[128,1024]{1,0:T(8,128)(2,1)S(1)}, bf16[128,1024]{1,0:T(8,128)(2,1)S(1)}, u32[]{:S(2)}, u32[]{:S(2)}) %collective-permute-start.13) | collective-permute-done | bytes 262176 | tf_op jit(solution)/shard_map/ppermute | solution.py:638
  51.0 2.3 %shard_map.174 = (bf16[256,768]{1,0:T(8,128)(2,1)S(1)}, f32[256,1024]{1,0:T(8,128)S(1)}, bf16[256,1024]{1,0:T(8,128)(2,1)S(1)}) custom-call(bf16[128,1024]{1,0:T(8,128)(2,1)S(1)} %collective-permute-done.13.refs_0_, bf16[128,1024]{1,0:T(8,128)(2,1)S(1)} %collective-permute-done.14.refs_1_, bf16[128,1024]{1,0:T(8,128)(2,1)S(1)} %collective-permute-done.1.refs_2_, ...), custom_call_target="tpu_custom_call" | custom-call | bytes 8000000 | tf_op jit(solution)/shard_map/pallas_call | solution.py:26
  55.3 1.6 %collective-permute-start.18 = (bf16[128,1024]{1,0:T(8,128)(2,1)S(1)}, bf16[128,1024]{1,0:T(8,128)(2,1)S(1)}, u32[]{:S(2)}, u32[]{:S(2)}) collective-permute-start(bf16[128,1024]{1,0:T(8,128)(2,1)S(1)} %shard_map.177), channel_id=1, source_target_pairs={{0,2},{1,3},{2,0},{3,1},{4,6},{5,7},{6,4},{7,5},{8,10},{9,11},{10,... | collective-permute-start | bytes 786440 | tf_op jit(solution)/shard_map/ppermute | solution.py:638
  56.9 6.8 %collective-permute-done.18.far_ref = bf16[128,1024]{1,0:T(8,128)(2,1)S(1)} collective-permute-done((bf16[128,1024]{1,0:T(8,128)(2,1)S(1)}, bf16[128,1024]{1,0:T(8,128)(2,1)S(1)}, u32[]{:S(2)}, u32[]{:S(2)}) %collective-permute-start.18) | collective-permute-done | bytes 262176 | tf_op jit(solution)/shard_map/ppermute | solution.py:638
  64.2 2.0 %shard_map.179 = (f32[2,56,128]{2,1,0:T(8,128)S(1)}, f32[2,56,128]{2,1,0:T(8,128)S(1)}, f32[2,56,128]{2,1,0:T(8,128)S(1)}, f32[2,56,128]{2,1,0:T(8,128)S(1)}) custom-call(f32[8,448,128]{2,1,0:T(8,128)S(1)} %shard_map.173.padded_ref, f32[8,128,128]{2,1,0:T(8,128)S(1)} %get-tuple-element.78.conv, f32[8,8,128]{2,1,0:T(8,128)S(1)} %get-tuple-element.79.vectors_ref, ...), custom_call_target="tpu_custom_call" | custom-call | bytes 7380000 | tf_op jit(solution)/shard_map/pallas_call | solution.py:26
  66.9 1.5 %collective-permute-start.20 = (f32[2,56,128]{2,1,0:T(8,128)S(1)}, f32[2,56,128]{2,1,0:T(8,128)S(1)}, u32[]{:S(2)}, u32[]{:S(2)}) collective-permute-start(f32[2,56,128]{2,1,0:T(8,128)S(1)} %get-tuple-element.83), channel_id=1, source_target_pairs={{0,16},{8,24},{16,0},{24,8},{1,17},{9,25},{17,1},{25,9},{2,18},{10... | collective-permute-start | bytes 172040 | tf_op jit(solution)/shard_map/ppermute | solution.py:634
  69.7 2.1 %collective-permute-start.23 = (bf16[48,1024]{1,0:T(8,128)(2,1)S(1)}, bf16[48,1024]{1,0:T(8,128)(2,1)S(1)}, u32[]{:S(2)}, u32[]{:S(2)}) collective-permute-start(bf16[48,1024]{1,0:T(8,128)(2,1)S(1)} %get-tuple-element.88), channel_id=1, source_target_pairs={{0,4},{4,0},{1,5},{5,1},{2,6},{6,2},{3,7},{7,3},{8,12},{12,8},{9,1... | collective-permute-start | bytes 294920 | tf_op jit(solution)/shard_map/ppermute | solution.py:61
  71.9 1.5 %collective-permute-done.21.refs_3_ = f32[2,56,128]{2,1,0:T(8,128)S(1)} collective-permute-done((f32[2,56,128]{2,1,0:T(8,128)S(1)}, f32[2,56,128]{2,1,0:T(8,128)S(1)}, u32[]{:S(2)}, u32[]{:S(2)}) %collective-permute-start.21) | collective-permute-done | bytes 57376 | tf_op jit(solution)/shard_map/ppermute | solution.py:634
  73.4 1.6 %collective-permute-start.22 = (bf16[128,1024]{1,0:T(8,128)(2,1)S(1)}, bf16[128,1024]{1,0:T(8,128)(2,1)S(1)}, u32[]{:S(2)}, u32[]{:S(2)}) collective-permute-start(bf16[128,1024]{1,0:T(8,128)(2,1)S(1)} %shard_map.176), channel_id=1, source_target_pairs={{0,2},{1,3},{2,0},{3,1},{4,6},{5,7},{6,4},{7,5},{8,10},{9,11},{10,... | collective-permute-start | bytes 786440 | tf_op jit(solution)/shard_map/ppermute | solution.py:638
  76.1 1.6 %collective-permute-start.25 = (bf16[48,1024]{1,0:T(8,128)(2,1)S(1)}, bf16[48,1024]{1,0:T(8,128)(2,1)S(1)}, u32[]{:S(2)}, u32[]{:S(2)}) collective-permute-start(bf16[48,1024]{1,0:T(8,128)(2,1)S(1)} %get-tuple-element.90), channel_id=1, source_target_pairs={{1,2},{2,1},{3,0},{0,3},{5,6},{6,5},{7,4},{4,7},{9,10},{10,9},{11,... | collective-permute-start | bytes 294920 | tf_op jit(solution)/shard_map/ppermute | solution.py:75
  77.7 3.0 %collective-permute-start.27 = (f32[2,56,128]{2,1,0:T(8,128)S(1)}, f32[2,56,128]{2,1,0:T(8,128)S(1)}, u32[]{:S(2)}, u32[]{:S(2)}) collective-permute-start(f32[2,56,128]{2,1,0:T(8,128)S(1)} %shard_map.185.refs_0_), channel_id=1, source_target_pairs={{0,4},{1,5},{2,6},{3,7},{4,0},{5,1},{6,2},{7,3},{8,12},{9,13},{10,... | collective-permute-start | bytes 172040 | tf_op jit(solution)/shard_map/ppermute | solution.py:638
  80.7 2.6 %shard_map.182.partial_ref = f32[8,128,128]{2,1,0:T(8,128)S(1)} custom-call(bf16[128,1024]{1,0:T(8,128)(2,1)S(1)} %get-tuple-element.86.refs_0_.field_ref, bf16[48,1024]{1,0:T(8,128)(2,1)S(1)} %collective-permute-done.23.refs_1_.refs_0_, f32[8,56,128]{2,1,0:T(8,128)S(1)} %shard_map.164.refs_2_.params_ref.refs_4_, bf16[128,1024]{1,0:T(8,128)(2,1)S(1)} %bitcast.20), custom_call_target="tpu_custom_call" | custom-call | bytes 8000000 | tf_op jit(solution)/shard_map/pallas_call | solution.py:26
  83.3 2.5 %collective-permute-start.28 = (f32[2,56,128]{2,1,0:T(8,128)S(1)}, f32[2,56,128]{2,1,0:T(8,128)S(1)}, u32[]{:S(2)}, u32[]{:S(2)}) collective-permute-start(f32[2,56,128]{2,1,0:T(8,128)S(1)} %shard_map.186.refs_0_), channel_id=1, source_target_pairs={{0,2},{1,3},{2,0},{3,1},{4,6},{5,7},{6,4},{7,5},{8,10},{9,11},{10,... | collective-permute-start | bytes 172040 | tf_op jit(solution)/shard_map/ppermute | solution.py:638
  85.9 1.7 %shard_map.184 = bf16[128,1024]{1,0:T(8,128)(2,1)} custom-call(f32[8,128,128]{2,1,0:T(8,128)S(1)} %shard_map.182.partial_ref, bf16[48,1024]{1,0:T(8,128)(2,1)S(1)} %collective-permute-done.24.first_ref, bf16[48,1024]{1,0:T(8,128)(2,1)S(1)} %collective-permute-done.25.second_ref, f32[8,56,128]{2,1,0:T(8,128)S(1)} %shard_map.164.refs_2_.params_ref.refs_4_), custom_call_target="tpu_custom_call" | custom-call | bytes 5000000 | tf_op jit(solution)/shard_map/pallas_call | solution.py:26
  (68 shorter events, 19.3 us)
Async XLA Ops:
  3.6 27.1 %collective-permute-start = (bf16[248,1024]{1,0:T(8,128)(2,1)}, bf16[248,1024]{1,0:T(8,128)(2,1)S(1)}, u32[]{:S(2)}, u32[]{:S(2)}) collective-permute-start(bf16[248,1024]{1,0:T(8,128)(2,1)} %get-tuple-element.53), channel_id=1, source_target_pairs={{0,4},{1,5},{2,6},{3,7},{4,0},{5,1},{6,2},{7,3},{8,12},{9,13},{10,... | collective-permute-start | bytes 1523720 | tf_op jit(solution)/shard_map/ppermute | solution.py:638
  7.7 16.8 %collective-permute-start.4 = (bf16[224,1024]{1,0:T(8,128)(2,1)}, bf16[224,1024]{1,0:T(8,128)(2,1)S(1)}, u32[]{:S(2)}, u32[]{:S(2)}) collective-permute-start(bf16[224,1024]{1,0:T(8,128)(2,1)} %get-tuple-element.54.refs_5_.refs_4_), channel_id=1, source_target_pairs={{0,24},{8,16},{16,8},{24,0},{1,25},{9,17},{17,9},{25,1},{2,26},{10... | collective-permute-start | bytes 1376264 | tf_op jit(solution)/shard_map/ppermute | solution.py:634
  10.1 20.5 %collective-permute-start.3 = (bf16[224,1024]{1,0:T(8,128)(2,1)}, bf16[224,1024]{1,0:T(8,128)(2,1)S(1)}, u32[]{:S(2)}, u32[]{:S(2)}) collective-permute-start(bf16[224,1024]{1,0:T(8,128)(2,1)} %get-tuple-element.54.refs_5_.refs_4_), channel_id=1, source_target_pairs={{0,16},{8,24},{16,0},{24,8},{1,17},{9,25},{17,1},{25,9},{2,18},{10... | collective-permute-start | bytes 1376264 | tf_op jit(solution)/shard_map/ppermute | solution.py:634
  10.6 20.1 %collective-permute-start.2 = (bf16[224,1024]{1,0:T(8,128)(2,1)}, bf16[224,1024]{1,0:T(8,128)(2,1)S(1)}, u32[]{:S(2)}, u32[]{:S(2)}) collective-permute-start(bf16[224,1024]{1,0:T(8,128)(2,1)} %get-tuple-element.54.refs_5_.refs_4_), channel_id=1, source_target_pairs={{0,8},{8,0},{16,24},{24,16},{1,9},{9,1},{17,25},{25,17},{2,10},{10... | collective-permute-start | bytes 1376264 | tf_op jit(solution)/shard_map/ppermute | solution.py:634
  11.2 13.3 %collective-permute-start.1 = (bf16[128,1024]{1,0:T(8,128)(2,1)}, bf16[128,1024]{1,0:T(8,128)(2,1)S(1)}, u32[]{:S(2)}, u32[]{:S(2)}) collective-permute-start(bf16[128,1024]{1,0:T(8,128)(2,1)} %bitcast.14), channel_id=1, source_target_pairs={{0,2},{1,3},{2,0},{3,1},{4,6},{5,7},{6,4},{7,5},{8,10},{9,11},{10,... | collective-permute-start | bytes 786440 | tf_op jit(solution)/shard_map/ppermute | solution.py:638
  30.7 11.4 %collective-permute-start.10 = (bf16[200,1024]{1,0:T(8,128)(2,1)S(1)}, bf16[200,1024]{1,0:T(8,128)(2,1)S(1)}, u32[]{:S(2)}, u32[]{:S(2)}) collective-permute-start(bf16[200,1024]{1,0:T(8,128)(2,1)S(1)} %shard_map.168.refs_9_.refs_8_), channel_id=1, source_target_pairs={{0,16},{8,24},{16,0},{24,8},{1,17},{9,25},{17,1},{25,9},{2,18},{10... | collective-permute-start | bytes 1228808 | tf_op jit(solution)/shard_map/ppermute | solution.py:634
  32.2 11.4 %collective-permute-start.9 = (bf16[200,1024]{1,0:T(8,128)(2,1)S(1)}, bf16[200,1024]{1,0:T(8,128)(2,1)S(1)}, u32[]{:S(2)}, u32[]{:S(2)}) collective-permute-start(bf16[200,1024]{1,0:T(8,128)(2,1)S(1)} %shard_map.168.refs_9_.refs_8_), channel_id=1, source_target_pairs={{0,8},{8,0},{16,24},{24,16},{1,9},{9,1},{17,25},{25,17},{2,10},{10... | collective-permute-start | bytes 1228808 | tf_op jit(solution)/shard_map/ppermute | solution.py:634
  35.0 9.3 %collective-permute-start.8 = (bf16[128,1024]{1,0:T(8,128)(2,1)S(1)}, bf16[128,1024]{1,0:T(8,128)(2,1)S(1)}, u32[]{:S(2)}, u32[]{:S(2)}) collective-permute-start(bf16[128,1024]{1,0:T(8,128)(2,1)S(1)} %bitcast.15), channel_id=1, source_target_pairs={{0,1},{1,0},{2,3},{3,2},{4,5},{5,4},{6,7},{7,6},{8,9},{9,8},{10,11... | collective-permute-start | bytes 786440 | tf_op jit(solution)/shard_map/ppermute | solution.py:638
  39.7 4.7 %collective-permute-start.7 = (bf16[128,1024]{1,0:T(8,128)(2,1)S(1)}, bf16[128,1024]{1,0:T(8,128)(2,1)S(1)}, u32[]{:S(2)}, u32[]{:S(2)}) collective-permute-start(bf16[128,1024]{1,0:T(8,128)(2,1)S(1)} %get-tuple-element.63.refs_0_), channel_id=1, source_target_pairs={{0,1},{1,0},{2,3},{3,2},{4,5},{5,4},{6,7},{7,6},{8,9},{9,8},{10,11... | collective-permute-start | bytes 786440 | tf_op jit(solution)/shard_map/ppermute | solution.py:638
  40.5 8.3 %collective-permute-start.13 = (bf16[128,1024]{1,0:T(8,128)(2,1)S(1)}, bf16[128,1024]{1,0:T(8,128)(2,1)S(1)}, u32[]{:S(2)}, u32[]{:S(2)}) collective-permute-start(bf16[128,1024]{1,0:T(8,128)(2,1)S(1)} %get-tuple-element.63.refs_0_), channel_id=1, source_target_pairs={{0,2},{1,3},{2,0},{3,1},{4,6},{5,7},{6,4},{7,5},{8,10},{9,11},{10,... | collective-permute-start | bytes 786440 | tf_op jit(solution)/shard_map/ppermute | solution.py:638
  42.1 7.3 %collective-permute-start.12 = (bf16[104,1024]{1,0:T(8,128)(2,1)S(1)}, bf16[104,1024]{1,0:T(8,128)(2,1)S(1)}, u32[]{:S(2)}, u32[]{:S(2)}) collective-permute-start(bf16[104,1024]{1,0:T(8,128)(2,1)S(1)} %shard_map.171), channel_id=1, source_target_pairs={{0,8},{8,0},{16,24},{24,16},{1,9},{9,1},{17,25},{25,17},{2,10},{10... | collective-permute-start | bytes 638984 | tf_op jit(solution)/shard_map/ppermute | solution.py:634
  43.7 5.7 %collective-permute-start.11 = (bf16[96,1024]{1,0:T(8,128)(2,1)S(1)}, bf16[96,1024]{1,0:T(8,128)(2,1)S(1)}, u32[]{:S(2)}, u32[]{:S(2)}) collective-permute-start(bf16[96,1024]{1,0:T(8,128)(2,1)S(1)} %shard_map.170), channel_id=1, source_target_pairs={{0,16},{8,24},{16,0},{24,8},{1,17},{9,25},{17,1},{25,9},{2,18},{10... | collective-permute-start | bytes 589832 | tf_op jit(solution)/shard_map/ppermute | solution.py:634
  44.3 6.2 %collective-permute-start.15 = (bf16[128,1024]{1,0:T(8,128)(2,1)S(1)}, bf16[128,1024]{1,0:T(8,128)(2,1)S(1)}, u32[]{:S(2)}, u32[]{:S(2)}) collective-permute-start(bf16[128,1024]{1,0:T(8,128)(2,1)S(1)} %collective-permute-done.1.refs_2_), channel_id=1, source_target_pairs={{0,1},{1,0},{2,3},{3,2},{4,5},{5,4},{6,7},{7,6},{8,9},{9,8},{10,11... | collective-permute-start | bytes 786440 | tf_op jit(solution)/shard_map/ppermute | solution.py:638
  54.5 17.4 %collective-permute-start.16 = (bf16[256,1024]{1,0:T(8,128)(2,1)S(1)}, bf16[256,1024]{1,0:T(8,128)(2,1)S(1)}, u32[]{:S(2)}, u32[]{:S(2)}) collective-permute-start(bf16[256,1024]{1,0:T(8,128)(2,1)S(1)} %get-tuple-element.73), channel_id=1, source_target_pairs={{0,1},{1,0},{2,3},{3,2},{4,5},{5,4},{6,7},{7,6},{8,9},{9,8},{10,11... | collective-permute-start | bytes 1572872 | tf_op jit(solution)/shard_map/ppermute | solution.py:638
  55.3 8.4 %collective-permute-start.18 = (bf16[128,1024]{1,0:T(8,128)(2,1)S(1)}, bf16[128,1024]{1,0:T(8,128)(2,1)S(1)}, u32[]{:S(2)}, u32[]{:S(2)}) collective-permute-start(bf16[128,1024]{1,0:T(8,128)(2,1)S(1)} %shard_map.177), channel_id=1, source_target_pairs={{0,2},{1,3},{2,0},{3,1},{4,6},{5,7},{6,4},{7,5},{8,10},{9,11},{10,... | collective-permute-start | bytes 786440 | tf_op jit(solution)/shard_map/ppermute | solution.py:638
  66.2 5.7 %collective-permute-start.19 = (f32[2,56,128]{2,1,0:T(8,128)S(1)}, f32[2,56,128]{2,1,0:T(8,128)S(1)}, u32[]{:S(2)}, u32[]{:S(2)}) collective-permute-start(f32[2,56,128]{2,1,0:T(8,128)S(1)} %get-tuple-element.82), channel_id=1, source_target_pairs={{0,8},{8,0},{16,24},{24,16},{1,9},{9,1},{17,25},{25,17},{2,10},{10... | collective-permute-start | bytes 172040 | tf_op jit(solution)/shard_map/ppermute | solution.py:634
  66.9 5.1 %collective-permute-start.20 = (f32[2,56,128]{2,1,0:T(8,128)S(1)}, f32[2,56,128]{2,1,0:T(8,128)S(1)}, u32[]{:S(2)}, u32[]{:S(2)}) collective-permute-start(f32[2,56,128]{2,1,0:T(8,128)S(1)} %get-tuple-element.83), channel_id=1, source_target_pairs={{0,16},{8,24},{16,0},{24,8},{1,17},{9,25},{17,1},{25,9},{2,18},{10... | collective-permute-start | bytes 172040 | tf_op jit(solution)/shard_map/ppermute | solution.py:634
  68.3 5.1 %collective-permute-start.21 = (f32[2,56,128]{2,1,0:T(8,128)S(1)}, f32[2,56,128]{2,1,0:T(8,128)S(1)}, u32[]{:S(2)}, u32[]{:S(2)}) collective-permute-start(f32[2,56,128]{2,1,0:T(8,128)S(1)} %get-tuple-element.84), channel_id=1, source_target_pairs={{0,24},{8,16},{16,8},{24,0},{1,25},{9,17},{17,9},{25,1},{2,26},{10... | collective-permute-start | bytes 172040 | tf_op jit(solution)/shard_map/ppermute | solution.py:634
  69.7 5.6 %collective-permute-start.23 = (bf16[48,1024]{1,0:T(8,128)(2,1)S(1)}, bf16[48,1024]{1,0:T(8,128)(2,1)S(1)}, u32[]{:S(2)}, u32[]{:S(2)}) collective-permute-start(bf16[48,1024]{1,0:T(8,128)(2,1)S(1)} %get-tuple-element.88), channel_id=1, source_target_pairs={{0,4},{4,0},{1,5},{5,1},{2,6},{6,2},{3,7},{7,3},{8,12},{12,8},{9,1... | collective-permute-start | bytes 294920 | tf_op jit(solution)/shard_map/ppermute | solution.py:61
  73.4 14.2 %collective-permute-start.22 = (bf16[128,1024]{1,0:T(8,128)(2,1)S(1)}, bf16[128,1024]{1,0:T(8,128)(2,1)S(1)}, u32[]{:S(2)}, u32[]{:S(2)}) collective-permute-start(bf16[128,1024]{1,0:T(8,128)(2,1)S(1)} %shard_map.176), channel_id=1, source_target_pairs={{0,2},{1,3},{2,0},{3,1},{4,6},{5,7},{6,4},{7,5},{8,10},{9,11},{10,... | collective-permute-start | bytes 786440 | tf_op jit(solution)/shard_map/ppermute | solution.py:638
  75.6 7.7 %collective-permute-start.24 = (bf16[48,1024]{1,0:T(8,128)(2,1)S(1)}, bf16[48,1024]{1,0:T(8,128)(2,1)S(1)}, u32[]{:S(2)}, u32[]{:S(2)}) collective-permute-start(bf16[48,1024]{1,0:T(8,128)(2,1)S(1)} %get-tuple-element.89), channel_id=1, source_target_pairs={{0,1},{1,0},{2,3},{3,2},{4,5},{5,4},{6,7},{7,6},{8,9},{9,8},{10,11... | collective-permute-start | bytes 294920 | tf_op jit(solution)/shard_map/ppermute | solution.py:75
  76.1 7.2 %collective-permute-start.25 = (bf16[48,1024]{1,0:T(8,128)(2,1)S(1)}, bf16[48,1024]{1,0:T(8,128)(2,1)S(1)}, u32[]{:S(2)}, u32[]{:S(2)}) collective-permute-start(bf16[48,1024]{1,0:T(8,128)(2,1)S(1)} %get-tuple-element.90), channel_id=1, source_target_pairs={{1,2},{2,1},{3,0},{0,3},{5,6},{6,5},{7,4},{4,7},{9,10},{10,9},{11,... | collective-permute-start | bytes 294920 | tf_op jit(solution)/shard_map/ppermute | solution.py:75
  77.7 5.6 %collective-permute-start.27 = (f32[2,56,128]{2,1,0:T(8,128)S(1)}, f32[2,56,128]{2,1,0:T(8,128)S(1)}, u32[]{:S(2)}, u32[]{:S(2)}) collective-permute-start(f32[2,56,128]{2,1,0:T(8,128)S(1)} %shard_map.185.refs_0_), channel_id=1, source_target_pairs={{0,4},{1,5},{2,6},{3,7},{4,0},{5,1},{6,2},{7,3},{8,12},{9,13},{10,... | collective-permute-start | bytes 172040 | tf_op jit(solution)/shard_map/ppermute | solution.py:638
  83.3 5.2 %collective-permute-start.28 = (f32[2,56,128]{2,1,0:T(8,128)S(1)}, f32[2,56,128]{2,1,0:T(8,128)S(1)}, u32[]{:S(2)}, u32[]{:S(2)}) collective-permute-start(f32[2,56,128]{2,1,0:T(8,128)S(1)} %shard_map.186.refs_0_), channel_id=1, source_target_pairs={{0,2},{1,3},{2,0},{3,1},{4,6},{5,7},{6,4},{7,5},{8,10},{9,11},{10,... | collective-permute-start | bytes 172040 | tf_op jit(solution)/shard_map/ppermute | solution.py:638
  (9 other events, 114.2 us)
